TPU v7x, 512 devices: a whole 4x4x16 slice. The times are simulated.
512 devices in a mesh: grp: 8 (over x, core), row: 4 (over z_hi), col: 16 (over z_lo, y).
Axes of the slice: x: 4, y: 4, z: 16 (z_hi: 4, z_lo: 4; z = z_hi * 4 + z_lo), core: 2. Of those that a mesh axis runs over, the one named last changes fastest.
Arguments:
- s_parent: float32 [15360, 15360], P(('row', 'col'), 'grp'), may hold values from -12 to 12
- child_factor: float32 [15360, 1024], P(('grp', 'row', 'col')), may hold values from -0.046875 to 0.046875
- panel_inverse: float32 [2, 512, 512], replicated, may hold values from -1 to 1, as said below
- pivot_kind: int32 [2, 512], replicated, may hold values from 0 to 2, as said below
- pivot_diag: float32 [2, 512], replicated, may hold values from -2 to 2, as said below
- pivot_couple: float32 [2, 512], replicated, may hold values from -4 to 4, as said below
- child_mask: int32 [2, 15360], replicated, may hold values 0 or 1
Outputs:
- off_inverse: float32 [15360, 1024], P(('row', 'col'), 'grp')
- diag_inverse: float32 [512, 1024], P(None, 'grp')
Inputs may be any that keep to these rules, and one draw needn't show every extreme that they name: `panel_inverse`: unit lower triangular. `pivot_kind`: 0 marks a 1x1 pivot, 1 and 2 the first and second column of a 2x2 pivot; 2x2 pivots occupy column pairs 2i, 2i + 1. `pivot_diag`: magnitudes from 0.5 to 2. `pivot_couple`: magnitudes from 3 to 4.
All inputs are finite; a program needn't handle non-finite values.
Results may differ from a plain program's by a relative error of at most 0.00011.
Values sent between devices are 32-bit elements; how exact they have to be, the bound alone decides.
No kernel may reach another device: no remote copies, remote signals or barrier semaphores. Data moves between devices by JAX's collectives and lax.ppermute only.
A program may use at most 64 MiB of HBM per device.

v0:
```python
import jax
import jax.numpy as jnp
from jax import lax
from jax.sharding import PartitionSpec as P

highest = lax.Precision.HIGHEST


def from_root(value, axis, source):
    kept = jnp.where(lax.axis_index(axis) == source, value, 0).astype(value.dtype)
    return lax.psum(kept, axis)


def pivot_solve(inverse, pivot_kind, pivot_diag, pivot_couple):
    diag_next = jnp.roll(pivot_diag, -1)
    diag_prev = jnp.roll(pivot_diag, 1)
    couple_prev = jnp.roll(pivot_couple, 1)
    det_here = pivot_diag * diag_next - pivot_couple * pivot_couple
    det_prev = diag_prev * pivot_diag - couple_prev * couple_prev
    self_coef = jnp.where(
        pivot_kind == 0,
        1.0 / pivot_diag,
        jnp.where(pivot_kind == 1, diag_next / det_here, diag_prev / det_prev),
    )
    next_coef = jnp.where(pivot_kind == 1, -pivot_couple / det_here, 0.0)
    prev_coef = jnp.where(pivot_kind == 2, -couple_prev / det_prev, 0.0)
    inv_next = jnp.roll(inverse, -1, axis=0)
    inv_prev = jnp.roll(inverse, 1, axis=0)
    return (
        self_coef[:, None] * inverse + next_coef[:, None] * inv_next + prev_coef[:, None] * inv_prev
    )


def inner_rows(left, right):
    return lax.dot_general(
        left, right, (((0,), (0,)), ((), ())), precision=highest, preferred_element_type=jnp.float32
    )


def per_device(
    s_parent, child_factor, panel_inverse, pivot_kind, pivot_diag, pivot_couple, child_mask
):
    group_total = lax.axis_size("grp")
    grid_total = lax.axis_size("row") * lax.axis_size("col")
    group_index = lax.axis_index("grp")
    grid_index = lax.axis_index("row") * lax.axis_size("col") + lax.axis_index("col")
    children = panel_inverse.shape[0]
    width = panel_inverse.shape[1]
    halves = group_total // children
    branch = group_index // halves
    share_cols = width // halves
    col_start = group_index % halves * share_cols
    own_count = child_factor.shape[0]
    own_start = (group_index * grid_total + grid_index) * own_count
    own_weight = lax.dynamic_slice_in_dim(child_mask, own_start, own_count, 1).astype(jnp.float32)
    pieces = []
    for child in range(children):
        factor = child_factor[:, child * width : (child + 1) * width]
        pieces.append(
            jnp.dot(
                own_weight[child][:, None] * factor,
                panel_inverse[child],
                precision=highest,
                preferred_element_type=jnp.float32,
            )
        )
    y_own = jnp.concatenate(pieces, axis=1)
    y_block = lax.all_gather(y_own, ("row", "col"), axis=0, tiled=True)
    tile_rows = s_parent.shape[0]
    block_rows = y_block.shape[0]
    tile_start = grid_index * tile_rows
    source = tile_start // block_rows
    local_rows = lax.dynamic_slice_in_dim(y_block, tile_start - source * block_rows, tile_rows, 0)
    y_tile = from_root(local_rows, "grp", source)
    tile_weight = lax.dynamic_slice(child_mask, (branch, tile_start), (1, tile_rows))[0].astype(
        jnp.float32
    )
    y_child = lax.dynamic_slice_in_dim(y_tile, branch * width, width, 1)
    inverse = lax.dynamic_index_in_dim(panel_inverse, branch, 0, keepdims=False)
    inverse_cols = lax.dynamic_slice_in_dim(inverse, col_start, share_cols, 1)
    kinds = lax.dynamic_index_in_dim(pivot_kind, branch, 0, keepdims=False)
    diags = lax.dynamic_index_in_dim(pivot_diag, branch, 0, keepdims=False)
    couples = lax.dynamic_index_in_dim(pivot_couple, branch, 0, keepdims=False)
    scaled = pivot_solve(inverse_cols, kinds, diags, couples)
    v_rows = lax.psum_scatter(
        lax.dot_general(
            y_block,
            s_parent,
            (((0,), (1,)), ((), ())),
            precision=highest,
            preferred_element_type=jnp.float32,
        ),
        "grp",
        scatter_dimension=0,
        tiled=True,
    )
    z_own = tile_weight[:, None] * v_rows.T
    local_term = inner_rows(y_child, z_own)
    summed = lax.psum(local_term, ("row", "col"))
    panel = summed + inner_rows(inverse, scaled)
    return (-z_own, panel)


def solution(mesh):
    placed = (P(("row", "col"), "grp"), P(("grp", "row", "col"), None), P(), P(), P(), P(), P())
    return jax.shard_map(
        per_device,
        mesh=mesh,
        in_specs=placed,
        out_specs=(P(("row", "col"), "grp"), P(None, "grp")),
        check_vma=False,
    )
```

profile of v0, /device:TPU:2, one launch (start us, length us, event | category | flops | bytes accessed | tf_op | source)
XLA Modules:
  0.0 575.7 jit_solution(10384009508145699371)
XLA Ops:
  7.2 0.0 copy-start
  7.2 0.0 all-gather.3.cloned.1.call-start
  7.2 0.9 fusion.34
  8.1 2.0 fusion.1
  10.1 2.0 fusion.3
  12.1 0.7 maximum_bitcast_fusion
  12.8 0.0 all-gather.3.cloned.1.call-update
  12.8 0.0 all-reduce.3.cloned.1.call-start
  12.9 161.5 %all-gather.3.cloned.1.call-done = f32[64,30,1024]{2,1,0:T(8,128)} async-done(((f32[1,30,1024]{2,1,0:T(8,128)}), f32[64,30,1024]{2,1,0:T(8,128)}) %all-gather.3.cloned.1.call-update) | async-done | bytes 7864336 | tf_op jit(solution)/shard_map/all_gather | solution.py:68
  174.4 8.3 %reshape.302 = f32[1920,1024]{1,0:T(8,128)} reshape(f32[64,30,1024]{2,1,0:T(8,128)} %all-gather.3.cloned.1.call-done) | data formatting | bytes 15728640
  182.7 2.3 dynamic-slice_select_fusion
  185.1 0.0 all-reduce.3.cloned.1.call-update
  185.1 0.0 copy-start.2
  185.1 0.0 copy-start.1
  185.1 0.0 copy-start.3
  185.1 0.0 reduce-scatter.2.cloned.1.call-start
  185.2 0.0 copy-done
  185.2 10.1 %fusion.40 = f32[1024,240]{0,1:T(8,128)} fusion(f32[1920,1024]{1,0:T(8,128)} %reshape.302, f32[240,1920]{1,0:T(8,128)S(1)} %copy-done), kind=kOutput, calls=%fused_computation.68 | convolution fusion | flops 5662310400 | bytes 10690560 | tf_op jit(solution)/shard_map/dot_general | solution.py:86
  195.3 0.0 reduce-scatter.2.cloned.1.call-update
  195.4 0.0 all-reduce.5.cloned.1.call-start
  195.4 0.0 copy-done.2
  195.5 0.6 dynamic-slice.6
  196.0 0.0 copy-done.1
  196.1 0.6 constant_dynamic-slice_fusion.3
  196.6 0.0 copy-done.3
  196.7 0.8 dynamic-slice_convert_fusion
  197.5 0.1 fusion.39
  197.5 1.5 constant_dynamic-slice_fusion.1
  199.0 2.0 divide_select_fusion
  201.0 54.4 %all-reduce.3.cloned.1.call-done = f32[240,1024]{1,0:T(8,128)} async-done(((f32[240,1024]{1,0:T(8,128)}), f32[240,1024]{1,0:T(8,128)}) %all-reduce.3.cloned.1.call-update) | async-done | bytes 983056 | tf_op jit(solution)/shard_map/psum | solution.py:11
  255.4 41.0 %reduce-scatter.2.cloned.1.call-done = f32[128,240]{0,1:T(8,128)} async-done(((f32[1024,240]{0,1:T(8,128)}), f32[128,240]{0,1:T(8,128)}) %reduce-scatter.2.cloned.1.call-update) | async-done | bytes 122896 | tf_op jit(solution)/shard_map/reduce_scatter | solution.py:85
  296.4 2.8 fusion.8
  299.2 0.0 all-reduce.5.cloned.1.call-update
  299.2 0.8 fusion.38
  300.0 1.6 negate_bitcast_fusion
  301.6 263.2 %all-reduce.5.cloned.1.call-done = f32[512,128]{1,0:T(8,128)} async-done(((f32[512,128]{1,0:T(8,128)}), f32[512,128]{1,0:T(8,128)}) %all-reduce.5.cloned.1.call-update) | async-done | bytes 262160 | tf_op jit(solution)/shard_map/psum | solution.py:99
  564.8 4.3 convolution_add_fusion
  (4 shorter events, 0.1 us)
Async XLA Ops:
  7.2 178.0 %copy-start = (f32[240,1920]{1,0:T(8,128)S(1)}, f32[240,1920]{1,0:T(8,128)}, u32[]{:S(2)}) copy-start(f32[240,1920]{1,0:T(8,128)} %param.7) | copy-start | bytes 5529604
  7.2 167.2 %all-gather.3.cloned.1.call-start = ((), (), s32[]{:S(2)}) async-start(), calls=%async_computation.4 | async-start | bytes 8519680 | tf_op jit(solution)/shard_map/all_gather | solution.py:68
  12.8 242.6 %all-reduce.3.cloned.1.call-start = ((), (), s32[]{:S(2)}) async-start(), calls=%async_computation.2 | async-start | bytes 1966080 | tf_op jit(solution)/shard_map/psum | solution.py:11
  185.1 10.4 %copy-start.2 = (f32[2,512]{1,0:T(2,128)S(1)}, f32[2,512]{1,0:T(2,128)}, u32[]{:S(2)}) copy-start(f32[2,512]{1,0:T(2,128)} %param.12) | copy-start | bytes 12292
  185.1 10.9 %copy-start.1 = (f32[2,512]{1,0:T(2,128)S(1)}, f32[2,512]{1,0:T(2,128)}, u32[]{:S(2)}) copy-start(f32[2,512]{1,0:T(2,128)} %param.11) | copy-start | bytes 12292
  185.1 11.5 %copy-start.3 = (s32[2,512]{1,0:T(2,128)S(1)}, s32[2,512]{1,0:T(2,128)}, u32[]{:S(2)}) copy-start(s32[2,512]{1,0:T(2,128)} %param.10) | copy-start | bytes 12292
  185.1 111.2 %reduce-scatter.2.cloned.1.call-start = ((), (), s32[]{:S(2)}) async-start(), calls=%async_computation.1 | async-start | bytes 1105920 | tf_op jit(solution)/shard_map/reduce_scatter | solution.py:85
  195.4 369.5 %all-reduce.5.cloned.1.call-start = ((), (), s32[]{:S(2)}) async-start(), calls=%async_computation.3 | async-start | bytes 524288 | tf_op jit(solution)/shard_map/psum | solution.py:99
Sparse Core Ops, SparseCore 0:
  12.9 161.4 all-gather.2
  185.2 70.1 all-reduce.2
  258.5 37.8 reduce-scatter.1
  300.2 264.5 all-reduce.4
where the time goes:
time: 576 us
  waiting for transfers between devices  520 us (90%)
  matrix products  21.3 us (4%)
  between operations  13.9 us (2%)
  local copies, waits for them, and re-layouts  11.9 us (2%)
  other arithmetic  8.29 us (1%)
    psum x1, waiting for transfers between devices, per_device(): summed = lax.psum(local_term, ('row', 'col'))  263 us
    all_gather x1, waiting for transfers between devices, per_device(): y_block = lax.all_gather(y_own, ('row', 'col'), axis=0, tiled=True)  162 us
    psum x1, waiting for transfers between devices, from_root(): return lax.psum(kept, axis)  54.4 us
    reduce_scatter x1, waiting for transfers between devices, per_device(): lax.psum_scatter(lax.dot_general(y_block, s_parent, (((0,), (1,)), ((), (...  41 us
  transfers between devices with their start and end apart: 4, of which 4 were waited for; matrix products, arithmetic and copies ran while one was open for 3% of the time, Pallas kernels for 0%

commit v1 on v0

v1 whole, which is shorter than its diff:
```python
import functools

import jax
import jax.numpy as jnp
import numpy as np
from jax import lax
from jax.experimental import pallas as pl
from jax.experimental.pallas import tpu as pltpu
from jax.sharding import Mesh
from jax.sharding import PartitionSpec as P

f32, bf16 = jnp.float32, jnp.bfloat16
highest = lax.Precision.HIGHEST

AXES = ("x", "c", "h", "l", "y")
Z = ("h", "l")
GRP = ("x", "c")
PLANE = ("x", "c", "y")
NZ, NY, NG = 16, 4, 8
SHARD = 30
SLOT = 32
ROWS = 240
PAD = 256
HALF = PAD // 2
COLS = 1920
WIDE = 1024
C = 512
OWN = 128
DEPTH = NZ * SLOT


def split2(a):
    hi = a.astype(bf16)
    return hi, (a - hi.astype(f32)).astype(bf16)


def dot3(ah, al, bh, bl):
    d = functools.partial(jnp.dot, preferred_element_type=f32)
    return d(ah, bh) + (d(ah, bl) + d(al, bh))


WINDOWS = [(480 * t // 128 * 128, -(-480 * (t + 1) // 128) * 128) for t in range(4)]


def sort_columns(s_any, out_any, s_ref, out_ref, in_sems, out_sems):
    loads = [
        pltpu.make_async_copy(
            s_any.at[:, pl.ds(begin, end - begin)], s_ref.at[t, :, pl.ds(0, end - begin)], in_sems.at[t]
        )
        for t, (begin, end) in enumerate(WINDOWS)
    ]
    stores = [
        pltpu.make_async_copy(
            out_ref.at[:, :, pl.ds(128 * t, 128)], out_any.at[:, :, pl.ds(128 * t, 128)], out_sems.at[t]
        )
        for t in range(4)
    ]
    for load in loads:
        load.start()
    for t, (begin, end) in enumerate(WINDOWS):
        row = lax.broadcasted_iota(jnp.int32, (end - begin, 512), 0)
        col = lax.broadcasted_iota(jnp.int32, (end - begin, 512), 1)
        part, place = col // 128, col % 128
        zz, i = place // SLOT, place % SLOT
        target = 480 * t - begin + 120 * zz + SHARD * part + i
        pick = jnp.where((row == target) & (i < SHARD), 1.0, 0.0).astype(bf16)
        loads[t].wait()
        hi, lo = split2(s_ref[t, :, :end - begin])
        got = jnp.dot(hi, pick, preferred_element_type=f32) + jnp.dot(
            lo, pick, preferred_element_type=f32
        )
        for q in range(NY):
            for k in range(8):
                out_ref[q, SLOT * k:SLOT * k + SHARD, 128 * t:128 * t + 128] = got[
                    SHARD * k:SHARD * (k + 1), 128 * q:128 * q + 128
                ]
                out_ref[q, SLOT * k + SHARD:SLOT * (k + 1), 128 * t:128 * t + 128] = jnp.zeros(
                    (SLOT - SHARD, 128), f32
                )
        stores[t].start()
    for store in stores:
        store.wait()


def spread_columns(s):
    anywhere = pl.BlockSpec(memory_space=pltpu.HBM)
    return pl.pallas_call(
        sort_columns,
        out_shape=jax.ShapeDtypeStruct((NY, PAD, DEPTH), f32),
        in_specs=[anywhere],
        out_specs=anywhere,
        scratch_shapes=[
            pltpu.VMEM((4, ROWS, 640), f32),
            pltpu.VMEM((NY, PAD, DEPTH), f32),
            pltpu.SemaphoreType.DMA((4,)),
            pltpu.SemaphoreType.DMA((4,)),
        ],
        compiler_params=pltpu.CompilerParams(vmem_limit_bytes=8 << 20),
        cost_estimate=pl.CostEstimate(
            flops=2 * 2 * ROWS * 640 * 512 * 4, bytes_accessed=4 * 2 * ROWS * 2048, transcendentals=0
        ),
    )(s)


PIECES = ((-4, 0, 4), (-5, -1, 3), (-3, 1, 5), (8,), (-6, -2), (2, 6), (7,), (9,))
N_PIECES = len(PIECES)


def panel_kernel(where_ref, *refs):
    pieces, (pinv_ref, yh_ref, yl_ref, first_ref, second_ref, fac_ref) = refs[:N_PIECES], refs[N_PIECES:]
    z = where_ref[0]
    for ref, offsets in zip(pieces, PIECES):
        for k, offset in enumerate(offsets):
            slot = lax.rem(z + (offset + NZ), NZ)
            fac_ref[pl.ds(pl.multiple_of(slot * SLOT, SLOT), SLOT), :] = ref[SLOT * k:SLOT * (k + 1), :]
    for child in range(2):
        fh, fl = split2(fac_ref[:, C * child:C * (child + 1)])
        for j in range(2):
            ph, plo = split2(pinv_ref[child, :, 256 * j:256 * (j + 1)])
            yh, yl = split2(dot3(fh, fl, ph, plo))
            begin = C * child + 256 * j
            yh_ref[:, begin:begin + 256] = yh
            yl_ref[:, begin:begin + 256] = yl
    for k, out_ref in enumerate((first_ref, second_ref)):
        half = pl.ds(pl.multiple_of(lax.rem(z, 2) * PAD + HALF * k, HALF), HALF)
        out_ref[...] = yh_ref[half, :].astype(f32) + yl_ref[half, :].astype(f32)


def panel_rows(where, pieces, pinv):
    vmem = pl.BlockSpec(memory_space=pltpu.VMEM)
    split = jax.ShapeDtypeStruct((DEPTH, WIDE), bf16)
    return pl.pallas_call(
        panel_kernel,
        out_shape=(split, split) + (jax.ShapeDtypeStruct((HALF, WIDE), f32),) * 2,
        in_specs=[pl.BlockSpec(memory_space=pltpu.SMEM)] + [vmem] * (N_PIECES + 1),
        out_specs=(vmem,) * 4,
        scratch_shapes=[pltpu.VMEM((DEPTH, WIDE), f32)],
        compiler_params=pltpu.CompilerParams(vmem_limit_bytes=12 << 20),
        cost_estimate=pl.CostEstimate(
            flops=6 * 6 * DEPTH * WIDE * C, bytes_accessed=7 << 20, transcendentals=0
        ),
    )(where, *pieces, pinv)


def image_kernel(side, where_ref, yh_ref, yl_ref, s_ref, *refs):
    (*added_refs, out_ref, sh_ref, sl_ref) = refs
    half = where_ref[1] if side == 0 else 1 - where_ref[1]
    rows = pl.ds(pl.multiple_of(HALF * half, HALF), HALF)
    sh, sl = split2(jnp.concatenate([s_ref[k, rows, :] for k in range(NY)], axis=0))
    sh_ref[...] = sh
    sl_ref[...] = sl

    @pl.loop(0, WIDE // 256)
    def _(j):
        cols = pl.ds(pl.multiple_of(256 * j, 256), 256)
        u = dot3(sh_ref[...], sl_ref[...], yh_ref[:, cols], yl_ref[:, cols])
        for source in range(NY):
            for k in range(NY):
                begin = HALF * source + SLOT * k
                for g in range(2):
                    part = u[begin:begin + SLOT, OWN * g:OWN * (g + 1)]
                    at = (2 * j + g, k, slice(SLOT * source, SLOT * (source + 1)))
                    for ref in added_refs:
                        part = part + ref[at]
                    out_ref[at] = part


def partial_image(side, where, yh, yl, s_parts, *added):
    vmem = pl.BlockSpec(memory_space=pltpu.VMEM)
    return pl.pallas_call(
        functools.partial(image_kernel, side),
        out_shape=jax.ShapeDtypeStruct((NG, NY, HALF, OWN), f32),
        in_specs=[pl.BlockSpec(memory_space=pltpu.SMEM)] + [vmem] * (3 + len(added)),
        out_specs=vmem,
        scratch_shapes=[pltpu.VMEM((NY * HALF, DEPTH), bf16), pltpu.VMEM((NY * HALF, DEPTH), bf16)],
        compiler_params=pltpu.CompilerParams(vmem_limit_bytes=12 << 20),
        cost_estimate=pl.CostEstimate(
            flops=6 * DEPTH * WIDE * NY * HALF, bytes_accessed=6 << 20, transcendentals=0
        ),
    )(where, yh, yl, s_parts, *added)


def finish_kernel(block_ref, got_ref, weight_ref, y_ref, pivot_ref, off_ref, term_ref):
    halves = []
    for core in range(2):
        total = got_ref[0, core, 0]
        for x in range(4):
            for y in range(NY):
                if x or y:
                    total = total + got_ref[x, core, y]
        halves.append(total)
    rows = [halves[core][SLOT * y:SLOT * (y + 1)] for y in range(NY) for core in range(2)]
    z_own = weight_ref[...] * jnp.concatenate(rows, axis=0)
    off_ref[...] = -z_own
    zh, zl = split2(z_own)
    yh, yl = split2(y_ref[...].T)
    term_ref[...] = dot3(yh, yl, zh, zl)
    mine = pl.ds(pl.multiple_of(32 * block_ref[0], 32), 32)
    term_ref[mine, :] += pivot_ref[...]


def finish(block, got, weight, y_rows, pivot):
    return pl.pallas_call(
        finish_kernel,
        out_shape=(
            jax.ShapeDtypeStruct((PAD, OWN), f32),
            jax.ShapeDtypeStruct((C, OWN), f32),
        ),
        in_specs=[pl.BlockSpec(memory_space=pltpu.SMEM)] + [pl.BlockSpec(memory_space=pltpu.VMEM)] * 4,
        compiler_params=pltpu.CompilerParams(vmem_limit_bytes=10 << 20),
        cost_estimate=pl.CostEstimate(
            flops=6 * C * PAD * OWN, bytes_accessed=4 << 20, transcendentals=0
        ),
    )(block, got, weight, y_rows, pivot)


def pivot_solve(inverse, pivot_kind, pivot_diag, pivot_couple):
    diag_next = jnp.roll(pivot_diag, -1)
    diag_prev = jnp.roll(pivot_diag, 1)
    couple_prev = jnp.roll(pivot_couple, 1)
    det_here = pivot_diag * diag_next - pivot_couple * pivot_couple
    det_prev = diag_prev * pivot_diag - couple_prev * couple_prev
    self_coef = jnp.where(
        pivot_kind == 0,
        1.0 / pivot_diag,
        jnp.where(pivot_kind == 1, diag_next / det_here, diag_prev / det_prev),
    )
    next_coef = jnp.where(pivot_kind == 1, -pivot_couple / det_here, 0.0)
    prev_coef = jnp.where(pivot_kind == 2, -couple_prev / det_prev, 0.0)
    inv_next = jnp.roll(inverse, -1, axis=0)
    inv_prev = jnp.roll(inverse, 1, axis=0)
    return (
        self_coef[:, None] * inverse + next_coef[:, None] * inv_next + prev_coef[:, None] * inv_prev
    )


def shift_z(a, step):
    return lax.ppermute(a, Z, [(i, (i + step) % NZ) for i in range(NZ)])


def swap_core(a):
    return lax.ppermute(a, "c", [(0, 1), (1, 0)])


def place(x, core, z, y):
    return ((x * 2 + core) * NZ + z) * NY + y


def from_root_core(a):
    pairs = [
        (place(z // 4, z // 2 % 2, z, y), place(z // 4, 1 - z // 2 % 2, z, y)) for z in range(NZ) for y in range(NY)
    ]
    return lax.ppermute(a, AXES, pairs)


def from_root(a, step):
    pairs = [
        (place(z // 4, core, z, y), place((z // 4 + step) % 4, core, z, y))
        for z in range(NZ)
        for y in range(NY)
        for core in range(2)
    ]
    return lax.ppermute(a, AXES, pairs)


def exchange(a, axes):
    return lax.all_to_all(a, axes, 0, 0, tiled=True)


def per_device(s_parent, child_factor, panel_inverse, pivot_kind, pivot_diag, pivot_couple, child_mask):
    group = lax.axis_index(GRP)
    z = lax.axis_index(Z)
    y = lax.axis_index("y")
    core = lax.axis_index("c")
    branch = group // 4
    grid = z * NY + y
    flat = group * (NZ * NY) + grid

    weight = lax.dynamic_slice_in_dim(child_mask, flat * SHARD, SHARD, 1).astype(f32)
    weight = jnp.repeat(weight.T, C, axis=1)
    own = jnp.pad(weight * child_factor, ((0, SLOT - SHARD), (0, 0)))

    below, above = shift_z(own, 4), shift_z(own, -4)

    s_sorted = spread_columns(s_parent)
    s_parts = exchange(s_sorted, "y")
    near = jnp.concatenate([below, own, above], axis=0)
    low, high = shift_z(near, 1), shift_z(near, -1)
    far = shift_z(below, 4)
    low2, high2 = shift_z(low[0:64], 1), shift_z(high[32:96], -1)
    low_far, high_far = shift_z(far, 1), shift_z(far, -1)
    pieces = (near, low, high, far, low2, high2, low_far, high_far)

    inverse = lax.dynamic_index_in_dim(panel_inverse, branch, 0, keepdims=False)

    inverse_cols = lax.dynamic_slice_in_dim(inverse, group % 4 * OWN, OWN, 1)
    kinds = lax.dynamic_index_in_dim(pivot_kind, branch, 0, keepdims=False)
    diags = lax.dynamic_index_in_dim(pivot_diag, branch, 0, keepdims=False)
    couples = lax.dynamic_index_in_dim(pivot_couple, branch, 0, keepdims=False)
    scaled = pivot_solve(inverse_cols, kinds, diags, couples)
    block = z % 4 * NY + y
    pivot_part = lax.dot_general(
        lax.dynamic_slice_in_dim(inverse, block * 32, 32, 1),
        scaled,
        (((0,), (0,)), ((), ())),
        precision=highest,
        preferred_element_type=f32,
    )
    pivot_part = jnp.where(lax.axis_index("h") == 0, pivot_part, 0.0)
    tile_weight = lax.dynamic_slice(child_mask, (branch, NY * ROWS * z), (1, NY * ROWS)).astype(f32)
    tile_weight = lax.dynamic_index_in_dim(tile_weight.reshape(NY, 2, NY, SHARD), y, 2, keepdims=False)
    tile_weight = jnp.pad(tile_weight, ((0, 0), (0, 0), (0, SLOT - SHARD))).reshape(PAD, 1)

    where = jnp.stack([z, core]).astype(jnp.int32)
    yh, yl, first, second = panel_rows(where, pieces, panel_inverse)
    at_core = core == z // 2 % 2
    half = jnp.where(at_core, first, from_root_core(second))
    send = partial_image(1, where, yh, yl, s_parts)
    received = swap_core(send)
    half, yh, yl = lax.optimization_barrier((half, yh, yl))
    x = lax.axis_index("x")
    parts = [
        from_root(lax.dynamic_slice_in_dim(half, (x + step) % 4 // 2 * C, C, 1), step) for step in (2, 1, 3)
    ]
    image = partial_image(0, where, yh, yl, s_parts, received)
    image, *parts = lax.optimization_barrier((image, *parts))
    got = exchange(image.reshape(32 * HALF, OWN), PLANE)
    kept = lax.dynamic_slice_in_dim(half, x // 2 * C, C, 1)
    mine = jnp.where(x == z // 4, kept, parts[0] + parts[1] + parts[2])
    other = swap_core(mine)
    y_rows = jnp.concatenate([jnp.where(at_core, mine, other), jnp.where(at_core, other, mine)], axis=0)

    off, term = finish(
        block.reshape(1).astype(jnp.int32), got.reshape(4, 2, NY, HALF, OWN), tile_weight, y_rows, pivot_part
    )

    rows = exchange(term, ("l", "y")).reshape(16, 32, OWN).sum(0)
    blocks = [
        lax.ppermute(
            lax.dynamic_slice_in_dim(off, (y + step) % NY * 2 * SLOT, 2 * SLOT, 0),
            "y", [(i, (i + step) % NY) for i in range(NY)],
        ) if step else lax.dynamic_slice_in_dim(off, y * 2 * SLOT, 2 * SLOT, 0)
        for step in range(NY)
    ]
    rows = exchange(jnp.tile(rows, (4, 1)), "h").reshape(4, 32, OWN).sum(0)
    panel = exchange(jnp.tile(rows, (16, 1)), ("l", "y"))
    blocks = jnp.stack([b.reshape(2, SLOT, OWN)[:, :SHARD] for b in blocks[::-1] + blocks[:0:-1]])
    off = lax.dynamic_slice_in_dim(blocks, 3 - y, NY, 0).transpose(1, 0, 2, 3).reshape(ROWS, OWN)
    return off, panel


def solution(mesh):
    grid = Mesh(mesh.devices.reshape(4, 2, 4, 4, 4), AXES)
    lines = ("h", "l", "y")
    placed = (P(lines, GRP), P(AXES, None), P(), P(), P(), P(), P())
    return jax.shard_map(
        per_device,
        mesh=grid,
        in_specs=placed,
        out_specs=(P(lines, GRP), P(None, GRP)),
        check_vma=False,
    )
```

time: 576 us -> 199 us (0.35)
  the two profiles are of different devices: /device:TPU:2 before, /device:TPU:8 now
where the time goes in v1:
time: 199 us; the launch traced here: 198 us
  starting transfers between devices  100 us (50%)
  waiting for transfers between devices  53.6 us (27%)
  local copies, waits for them, and re-layouts  17.3 us (9%)
  Pallas kernels  16.3 us (8%)
  other arithmetic  6.89 us (3%)
  matrix products  2.29 us (1%)
    ppermute x9, starting transfers between devices, shift_z(): return lax.ppermute(a, Z, [(i, (i + step) % NZ) for i in range(NZ)])  46.5 us
    all_to_all x5, waiting for transfers between devices, exchange(): return lax.all_to_all(a, axes, 0, 0, tiled=True)  36.3 us
    all_to_all x5, starting transfers between devices, exchange(): return lax.all_to_all(a, axes, 0, 0, tiled=True)  31.8 us
    ppermute x9, waiting for transfers between devices, shift_z(): return lax.ppermute(a, Z, [(i, (i + step) % NZ) for i in range(NZ)])  11.9 us
    unnamed x41, local copies, waits for them, and re-layouts  11.1 us
    ppermute x3, starting transfers between devices, per_device(): lax.ppermute(lax.dynamic_slice_in_dim(off, (y + step) % NY * 2 * SLOT, 2...  10.4 us
    pallas_call x2, Pallas kernels, partial_image(): pl.pallas_call(functools.partial(image_kernel, side), out_shape=jax.Shape...  8.41 us
    ppermute x3, starting transfers between devices, from_root(): return lax.ppermute(a, AXES, pairs)  4.29 us
  transfers between devices with their start and end apart: 23, of which 9 were waited for; matrix products, arithmetic and copies ran while one was open for 6% of the time, Pallas kernels for 5%

profile of v1, /device:TPU:8, one launch (start us, length us, event | category | flops | bytes accessed | tf_op | source)
XLA Modules:
  0.0 197.8 jit_solution(11974859197283812253)
XLA Ops:
  1.7 0.9 mul.143
  2.7 12.7 %collective-permute-start.1 = (f32[32,1024]{1,0:T(8,128)S(1)}, f32[32,1024]{1,0:T(8,128)S(1)}, u32[]{:S(2)}, u32[]{:S(2)}) collective-permute-start(f32[32,1024]{1,0:T(8,128)S(1)} %pad.8), channel_id=1, source_target_pairs={{0,48},{4,52},{8,56},{12,60},{16,0},{20,4},{24,8},{28,12},{32,16},... | collective-permute-start | bytes 393224 | tf_op jit(solution)/shard_map/ppermute | solution.py:238
  15.4 1.9 collective-permute-start
  17.3 1.5 copy-done.7
  18.8 3.2 %shard_map.87 = f32[4,256,512]{2,1,0:T(8,128)S(1)} custom-call(f32[240,1920]{1,0:T(8,128)S(1)} %copy-done.7), custom_call_target="tpu_custom_call" | custom-call | flops 1258291200 | bytes 3932160 | tf_op jit(solution)/shard_map/pallas_call | solution.py:87
  22.1 1.4 copy-done.4
  23.5 4.9 %all-to-all-start = ((f32[4,256,512]{2,1,0:T(8,128)}), f32[4,256,512]{2,1,0:T(8,128)S(1)}, u32[]{:S(2)}, u32[]{:S(2)}) async-start(f32[4,256,512]{2,1,0:T(8,128)} %copy-done.4), calls=%async_computation | async-start | bytes 4194304 | tf_op jit(solution)/shard_map/all_to_all | solution.py:267
  28.4 1.1 collective-permute-done
  29.5 4.6 %collective-permute-start.2 = (f32[96,1024]{1,0:T(8,128)S(1)}, f32[96,1024]{1,0:T(8,128)S(1)}, u32[]{:S(2)}, u32[]{:S(2)}) collective-permute-start(f32[96,1024]{1,0:T(8,128)S(1)} %pad_maximum_fusion.1.refs_0_), channel_id=1, source_target_pairs={{0,4},{4,8},{8,12},{12,16},{16,20},{20,24},{24,28},{28,32},{32,36}... | collective-permute-start | bytes 1179656 | tf_op jit(solution)/shard_map/ppermute | solution.py:238
  34.2 6.4 %collective-permute-start.3 = (f32[96,1024]{1,0:T(8,128)S(1)}, f32[96,1024]{1,0:T(8,128)S(1)}, u32[]{:S(2)}, u32[]{:S(2)}) collective-permute-start(f32[96,1024]{1,0:T(8,128)S(1)} %pad_maximum_fusion.1.refs_0_), channel_id=1, source_target_pairs={{0,60},{4,0},{8,4},{12,8},{16,12},{20,16},{24,20},{28,24},{32,28},... | collective-permute-start | bytes 1179656 | tf_op jit(solution)/shard_map/ppermute | solution.py:238
  40.6 4.4 %collective-permute-start.4 = (f32[32,1024]{1,0:T(8,128)S(1)}, f32[32,1024]{1,0:T(8,128)S(1)}, u32[]{:S(2)}, u32[]{:S(2)}) collective-permute-start(f32[32,1024]{1,0:T(8,128)S(1)} %collective-permute-done), channel_id=1, source_target_pairs={{0,16},{4,20},{8,24},{12,28},{16,32},{20,36},{24,40},{28,44},{32,4... | collective-permute-start | bytes 393224 | tf_op jit(solution)/shard_map/ppermute | solution.py:238
  45.0 8.4 %collective-permute-done.2.refs_1_ = f32[96,1024]{1,0:T(8,128)S(1)} collective-permute-done((f32[96,1024]{1,0:T(8,128)S(1)}, f32[96,1024]{1,0:T(8,128)S(1)}, u32[]{:S(2)}, u32[]{:S(2)}) %collective-permute-start.2) | collective-permute-done | bytes 393248 | tf_op jit(solution)/shard_map/ppermute | solution.py:238
  53.4 1.9 collective-permute-start.5
  55.4 7.4 %collective-permute-start.6 = (f32[64,1024]{1,0:T(8,128)S(1)}, f32[64,1024]{1,0:T(8,128)S(1)}, u32[]{:S(2)}, u32[]{:S(2)}) collective-permute-start(f32[64,1024]{1,0:T(8,128)S(1)} %slice.86), channel_id=1, source_target_pairs={{0,60},{4,0},{8,4},{12,8},{16,12},{20,16},{24,20},{28,24},{32,28},... | collective-permute-start | bytes 786440 | tf_op jit(solution)/shard_map/ppermute | solution.py:238
  62.8 1.9 collective-permute-start.7
  64.7 5.1 %collective-permute-start.8 = (f32[32,1024]{1,0:T(8,128)S(1)}, f32[32,1024]{1,0:T(8,128)S(1)}, u32[]{:S(2)}, u32[]{:S(2)}) collective-permute-start(f32[32,1024]{1,0:T(8,128)S(1)} %collective-permute-done.4.refs_3_), channel_id=1, source_target_pairs={{0,60},{4,0},{8,4},{12,8},{16,12},{20,16},{24,20},{28,24},{32,28},... | collective-permute-start | bytes 393224 | tf_op jit(solution)/shard_map/ppermute | solution.py:238
  70.9 1.5 collective-permute-done.8.refs_7_
  72.4 1.6 copy-done.5
  74.0 3.5 %shard_map.86 = (bf16[512,1024]{1,0:T(8,128)(2,1)S(1)}, bf16[512,1024]{1,0:T(8,128)(2,1)S(1)}, f32[128,1024]{1,0:T(8,128)S(1)}, f32[128,1024]{1,0:T(8,128)}) custom-call(s32[2]{0:T(128)S(1)} %pad_add_fusion.where_ref, f32[96,1024]{1,0:T(8,128)S(1)} %pad_maximum_fusion.1.refs_0_, f32[96,1024]{1,0:T(8,128)S(1)} %collective-permute-done.2.refs_1_, ...), custom_call_target="tpu_custom_call" | custom-call | flops 9663676416 | bytes 7340032 | tf_op jit(solution)/shard_map/pallas_call | solution.py:132
  77.4 1.0 copy-done.1
  79.3 1.2 copy-done.2
  80.5 4.3 %shard_map.88 = f32[8,4,128,128]{3,2,1,0:T(8,128)} custom-call(s32[2]{0:T(128)S(1)} %pad_add_fusion.where_ref, bf16[512,1024]{1,0:T(8,128)(2,1)S(1)} %get-tuple-element.19.yh_ref, bf16[512,1024]{1,0:T(8,128)(2,1)S(1)} %copy-done.2, f32[4,256,512]{2,1,0:T(8,128)S(1)} %all-to-all-done.s_ref), custom_call_target="tpu_custom_call" | custom-call | flops 1610612736 | bytes 6291456 | tf_op jit(solution)/shard_map/pallas_call | solution.py:170
  84.8 1.9 collective-permute-start.10
  86.8 3.2 %collective-permute-start.9 = (f32[128,1024]{1,0:T(8,128)}, f32[128,1024]{1,0:T(8,128)}, u32[]{:S(2)}, u32[]{:S(2)}) collective-permute-start(f32[128,1024]{1,0:T(8,128)} %get-tuple-element.16), channel_id=1, source_target_pairs={{0,64},{1,65},{2,66},{3,67},{4,68},{5,69},{6,70},{7,71},{72,8},{73... | collective-permute-start | bytes 1572872 | tf_op jit(solution)/shard_map/ppermute | solution.py:253
  90.0 1.6 collective-permute-done.9
  91.6 1.1 broadcast_select_fusion
  92.8 1.7 collective-permute-start.11
  94.5 1.3 collective-permute-start.12
  95.8 1.3 collective-permute-start.13
  97.2 4.1 %shard_map.89 = f32[8,4,128,128]{3,2,1,0:T(8,128)S(1)} custom-call(s32[2]{0:T(128)S(1)} %pad_add_fusion.where_ref, bf16[512,1024]{1,0:T(8,128)(2,1)S(1)} %get-tuple-element.19.yh_ref, bf16[512,1024]{1,0:T(8,128)(2,1)S(1)} %copy-done.3, f32[4,256,512]{2,1,0:T(8,128)S(1)} %all-to-all-done.s_ref, f32[8,4,128,128]{3,2,1,0:T(8,128)} %collective-permute-done.10.refs_0_), custom_call_target="tpu_custom_call" | custom-call | flops 1610612736 | bytes 6291456 | tf_op jit(solution)/shard_map/pallas_call | solution.py:170
  101.2 1.4 copy-done
  102.6 3.7 %collective-permute-done.12 = f32[128,512]{1,0:T(8,128)S(1)} collective-permute-done((f32[128,512]{1,0:T(8,128)S(1)}, f32[128,512]{1,0:T(8,128)S(1)}, u32[]{:S(2)}, u32[]{:S(2)}) %collective-permute-start.12) | collective-permute-done | bytes 262176 | tf_op jit(solution)/shard_map/ppermute | solution.py:263
  107.7 7.1 %all-to-all-start.1 = ((f32[32,128,128]{2,1,0:T(8,128)}), f32[32,128,128]{2,1,0:T(8,128)S(1)}, u32[]{:S(2)}, u32[]{:S(2)}) async-start(f32[32,128,128]{2,1,0:T(8,128)} %bitcast.57), calls=%async_computation.1 | async-start | bytes 4194304 | tf_op jit(solution)/shard_map/all_to_all | solution.py:267
  117.2 1.5 constant_dynamic-slice_fusion.1
  118.7 1.9 divide_select_fusion
  120.6 1.2 add_select_fusion
  121.8 2.0 collective-permute-start.14
  124.7 2.3 %convolution_select_fusion.pivot_ref = f32[32,128]{1,0:T(8,128)S(1)} fusion(f32[1,1,128]{2,1,0:T(1,128)S(1)} %get-tuple-element.32, f32[1,511,128]{2,1,0:T(8,128)S(1)} %get-tuple-element.34, f32[1,511,128]{2,1,0:T(8,128)S(1)} %get-tuple-element.33, f32[1,1,128]{2,1,0:T(1,128)S(1)} %get-tuple-element.31, f32[2,512,512]{2,1,0:T(8,128)} %refs_8_.1, ...), kind=kOutput, calls=%fused_computation | convolution fusion | flops 25628672 | bytes 1073664 | tf_op jit(solution)/shard_map/dot_general | solution.py:302
  127.1 14.6 %all-to-all-done.1 = f32[32,128,128]{2,1,0:T(8,128)S(1)} async-done(((f32[32,128,128]{2,1,0:T(8,128)}), f32[32,128,128]{2,1,0:T(8,128)S(1)}, u32[]{:S(2)}, u32[]{:S(2)}) %all-to-all-start.1) | async-done | bytes 2097184 | tf_op jit(solution)/shard_map/all_to_all | solution.py:267
  141.7 1.2 shard_map.90
  142.9 7.1 %all-to-all-start.2 = ((f32[16,32,128]{2,1,0:T(8,128)}), f32[16,32,128]{2,1,0:T(8,128)S(1)}, u32[]{:S(2)}, u32[]{:S(2)}) async-start(f32[16,32,128]{2,1,0:T(8,128)} %bitcast.27), calls=%async_computation.2 | async-start | bytes 524288 | tf_op jit(solution)/shard_map/all_to_all | solution.py:267
  150.0 2.1 %collective-permute-start.15 = (f32[64,128]{1,0:T(8,128)S(1)}, f32[64,128]{1,0:T(8,128)S(1)}, u32[]{:S(2)}, u32[]{:S(2)}) collective-permute-start(f32[64,128]{1,0:T(8,128)S(1)} %get-tuple-element.43), channel_id=1, source_target_pairs={{0,3},{1,0},{2,1},{3,2},{4,7},{5,4},{6,5},{7,6},{8,11},{9,8},{10,9... | collective-permute-start | bytes 98312 | tf_op jit(solution)/shard_map/ppermute | solution.py:339
  152.1 4.7 %collective-permute-start.16 = (f32[64,128]{1,0:T(8,128)S(1)}, f32[64,128]{1,0:T(8,128)S(1)}, u32[]{:S(2)}, u32[]{:S(2)}) collective-permute-start(f32[64,128]{1,0:T(8,128)S(1)} %get-tuple-element.42), channel_id=1, source_target_pairs={{0,2},{1,3},{2,0},{3,1},{4,6},{5,7},{6,4},{7,5},{8,10},{9,11},{10,... | collective-permute-start | bytes 98312 | tf_op jit(solution)/shard_map/ppermute | solution.py:339
  156.8 3.7 %collective-permute-start.17 = (f32[64,128]{1,0:T(8,128)S(1)}, f32[64,128]{1,0:T(8,128)S(1)}, u32[]{:S(2)}, u32[]{:S(2)}) collective-permute-start(f32[64,128]{1,0:T(8,128)S(1)} %get-tuple-element.41), channel_id=1, source_target_pairs={{0,1},{1,2},{2,3},{3,0},{4,5},{5,6},{6,7},{7,4},{8,9},{9,10},{10,1... | collective-permute-start | bytes 98312 | tf_op jit(solution)/shard_map/ppermute | solution.py:339
  161.2 6.8 %all-to-all-start.3 = ((f32[4,32,128]{2,1,0:T(8,128)}), f32[4,32,128]{2,1,0:T(8,128)S(1)}, u32[]{:S(2)}, u32[]{:S(2)}) async-start(f32[4,32,128]{2,1,0:T(8,128)} %tile.4), calls=%async_computation.3 | async-start | bytes 131072 | tf_op jit(solution)/shard_map/all_to_all | solution.py:267
  168.0 13.9 %all-to-all-done.3 = f32[4,32,128]{2,1,0:T(8,128)S(1)} async-done(((f32[4,32,128]{2,1,0:T(8,128)}), f32[4,32,128]{2,1,0:T(8,128)S(1)}, u32[]{:S(2)}, u32[]{:S(2)}) %all-to-all-start.3) | async-done | bytes 65568 | tf_op jit(solution)/shard_map/all_to_all | solution.py:267
  182.6 5.9 %all-to-all-start.4 = ((f32[16,32,128]{2,1,0:T(8,128)}), f32[16,32,128]{2,1,0:T(8,128)S(1)}, u32[]{:S(2)}, u32[]{:S(2)}) async-start(f32[16,32,128]{2,1,0:T(8,128)} %tile.5), calls=%async_computation.4 | async-start | bytes 524288 | tf_op jit(solution)/shard_map/all_to_all | solution.py:267
  189.2 7.9 %all-to-all-done.4 = f32[16,32,128]{2,1,0:T(8,128)S(1)} async-done(((f32[16,32,128]{2,1,0:T(8,128)}), f32[16,32,128]{2,1,0:T(8,128)S(1)}, u32[]{:S(2)}, u32[]{:S(2)}) %all-to-all-start.4) | async-done | bytes 262176 | tf_op jit(solution)/shard_map/all_to_all | solution.py:267
  (81 shorter events, 10.6 us)
Async XLA Ops:
  2.7 25.7 %collective-permute-start.1 = (f32[32,1024]{1,0:T(8,128)S(1)}, f32[32,1024]{1,0:T(8,128)S(1)}, u32[]{:S(2)}, u32[]{:S(2)}) collective-permute-start(f32[32,1024]{1,0:T(8,128)S(1)} %pad.8), channel_id=1, source_target_pairs={{0,48},{4,52},{8,56},{12,60},{16,0},{20,4},{24,8},{28,12},{32,16},... | collective-permute-start | bytes 393224 | tf_op jit(solution)/shard_map/ppermute | solution.py:238
  15.4 14.1 %collective-permute-start = (f32[32,1024]{1,0:T(8,128)S(1)}, f32[32,1024]{1,0:T(8,128)S(1)}, u32[]{:S(2)}, u32[]{:S(2)}) collective-permute-start(f32[32,1024]{1,0:T(8,128)S(1)} %pad.8), channel_id=1, source_target_pairs={{0,16},{4,20},{8,24},{12,28},{16,32},{20,36},{24,40},{28,44},{32,4... | collective-permute-start | bytes 393224 | tf_op jit(solution)/shard_map/ppermute | solution.py:238
  17.3 1.5 copy-start.7
  22.1 1.4 copy-start.4
  23.5 55.8 %all-to-all-start = ((f32[4,256,512]{2,1,0:T(8,128)}), f32[4,256,512]{2,1,0:T(8,128)S(1)}, u32[]{:S(2)}, u32[]{:S(2)}) async-start(f32[4,256,512]{2,1,0:T(8,128)} %copy-done.4), calls=%async_computation | async-start | bytes 4194304 | tf_op jit(solution)/shard_map/all_to_all | solution.py:267
  29.5 23.8 %collective-permute-start.2 = (f32[96,1024]{1,0:T(8,128)S(1)}, f32[96,1024]{1,0:T(8,128)S(1)}, u32[]{:S(2)}, u32[]{:S(2)}) collective-permute-start(f32[96,1024]{1,0:T(8,128)S(1)} %pad_maximum_fusion.1.refs_0_), channel_id=1, source_target_pairs={{0,4},{4,8},{8,12},{12,16},{16,20},{20,24},{24,28},{28,32},{32,36}... | collective-permute-start | bytes 1179656 | tf_op jit(solution)/shard_map/ppermute | solution.py:238
  34.2 21.1 %collective-permute-start.3 = (f32[96,1024]{1,0:T(8,128)S(1)}, f32[96,1024]{1,0:T(8,128)S(1)}, u32[]{:S(2)}, u32[]{:S(2)}) collective-permute-start(f32[96,1024]{1,0:T(8,128)S(1)} %pad_maximum_fusion.1.refs_0_), channel_id=1, source_target_pairs={{0,60},{4,0},{8,4},{12,8},{16,12},{20,16},{24,20},{28,24},{32,28},... | collective-permute-start | bytes 1179656 | tf_op jit(solution)/shard_map/ppermute | solution.py:238
  40.6 22.2 %collective-permute-start.4 = (f32[32,1024]{1,0:T(8,128)S(1)}, f32[32,1024]{1,0:T(8,128)S(1)}, u32[]{:S(2)}, u32[]{:S(2)}) collective-permute-start(f32[32,1024]{1,0:T(8,128)S(1)} %collective-permute-done), channel_id=1, source_target_pairs={{0,16},{4,20},{8,24},{12,28},{16,32},{20,36},{24,40},{28,44},{32,4... | collective-permute-start | bytes 393224 | tf_op jit(solution)/shard_map/ppermute | solution.py:238
  53.4 19.0 %collective-permute-start.5 = (f32[64,1024]{1,0:T(8,128)S(1)}, f32[64,1024]{1,0:T(8,128)S(1)}, u32[]{:S(2)}, u32[]{:S(2)}) collective-permute-start(f32[64,1024]{1,0:T(8,128)S(1)} %slice.85), channel_id=1, source_target_pairs={{0,4},{4,8},{8,12},{12,16},{16,20},{20,24},{24,28},{28,32},{32,36}... | collective-permute-start | bytes 786440 | tf_op jit(solution)/shard_map/ppermute | solution.py:238
  55.4 17.0 %collective-permute-start.6 = (f32[64,1024]{1,0:T(8,128)S(1)}, f32[64,1024]{1,0:T(8,128)S(1)}, u32[]{:S(2)}, u32[]{:S(2)}) collective-permute-start(f32[64,1024]{1,0:T(8,128)S(1)} %slice.86), channel_id=1, source_target_pairs={{0,60},{4,0},{8,4},{12,8},{16,12},{20,16},{24,20},{28,24},{32,28},... | collective-permute-start | bytes 786440 | tf_op jit(solution)/shard_map/ppermute | solution.py:238
  62.8 8.1 %collective-permute-start.7 = (f32[32,1024]{1,0:T(8,128)S(1)}, f32[32,1024]{1,0:T(8,128)S(1)}, u32[]{:S(2)}, u32[]{:S(2)}) collective-permute-start(f32[32,1024]{1,0:T(8,128)S(1)} %collective-permute-done.4.refs_3_), channel_id=1, source_target_pairs={{0,4},{4,8},{8,12},{12,16},{16,20},{20,24},{24,28},{28,32},{32,36}... | collective-permute-start | bytes 393224 | tf_op jit(solution)/shard_map/ppermute | solution.py:238
  64.7 7.6 %collective-permute-start.8 = (f32[32,1024]{1,0:T(8,128)S(1)}, f32[32,1024]{1,0:T(8,128)S(1)}, u32[]{:S(2)}, u32[]{:S(2)}) collective-permute-start(f32[32,1024]{1,0:T(8,128)S(1)} %collective-permute-done.4.refs_3_), channel_id=1, source_target_pairs={{0,60},{4,0},{8,4},{12,8},{16,12},{20,16},{24,20},{28,24},{32,28},... | collective-permute-start | bytes 393224 | tf_op jit(solution)/shard_map/ppermute | solution.py:238
  72.4 1.6 copy-start.5
  77.4 1.0 copy-start.1
  78.5 0.8 copy-start.6
  79.3 1.2 copy-start.2
  84.8 12.3 %collective-permute-start.10 = (f32[8,4,128,128]{3,2,1,0:T(8,128)}, f32[8,4,128,128]{3,2,1,0:T(8,128)}, u32[]{:S(2)}, u32[]{:S(2)}) collective-permute-start(f32[8,4,128,128]{3,2,1,0:T(8,128)} %shard_map.88), channel_id=1, source_target_pairs={{0,64},{64,0},{1,65},{65,1},{2,66},{66,2},{3,67},{67,3},{4,68},{68... | collective-permute-start | bytes 6291464 | tf_op jit(solution)/shard_map/ppermute | solution.py:242
  86.8 4.9 %collective-permute-start.9 = (f32[128,1024]{1,0:T(8,128)}, f32[128,1024]{1,0:T(8,128)}, u32[]{:S(2)}, u32[]{:S(2)}) collective-permute-start(f32[128,1024]{1,0:T(8,128)} %get-tuple-element.16), channel_id=1, source_target_pairs={{0,64},{1,65},{2,66},{3,67},{4,68},{5,69},{6,70},{7,71},{72,8},{73... | collective-permute-start | bytes 1572872 | tf_op jit(solution)/shard_map/ppermute | solution.py:253
  90.0 7.2 %copy-start.3 = (bf16[512,1024]{1,0:T(8,128)(2,1)S(1)}, bf16[512,1024]{1,0:T(8,128)(2,1)}, u32[]{:S(2)}) copy-start(bf16[512,1024]{1,0:T(8,128)(2,1)} %copy-done.1) | copy-start | bytes 3145732
  92.7 4.4 %copy-start.8 = (f32[128,1024]{1,0:T(8,128)}, f32[128,1024]{1,0:T(8,128)S(1)}, u32[]{:S(2)}) copy-start(f32[128,1024]{1,0:T(8,128)S(1)} %broadcast_select_fusion) | copy-start | bytes 1572868
  92.8 9.8 %collective-permute-start.11 = (f32[128,512]{1,0:T(8,128)S(1)}, f32[128,512]{1,0:T(8,128)S(1)}, u32[]{:S(2)}, u32[]{:S(2)}) collective-permute-start(f32[128,512]{1,0:T(8,128)S(1)} %get-tuple-element.39), channel_id=1, source_target_pairs={{0,256},{64,320},{1,257},{65,321},{2,258},{66,322},{3,259},{67,323... | collective-permute-start | bytes 786440 | tf_op jit(solution)/shard_map/ppermute | solution.py:263
  94.5 11.8 %collective-permute-start.12 = (f32[128,512]{1,0:T(8,128)S(1)}, f32[128,512]{1,0:T(8,128)S(1)}, u32[]{:S(2)}, u32[]{:S(2)}) collective-permute-start(f32[128,512]{1,0:T(8,128)S(1)} %get-tuple-element.38), channel_id=1, source_target_pairs={{0,128},{64,192},{1,129},{65,193},{2,130},{66,194},{3,131},{67,195... | collective-permute-start | bytes 786440 | tf_op jit(solution)/shard_map/ppermute | solution.py:263
  95.8 10.5 %collective-permute-start.13 = (f32[128,512]{1,0:T(8,128)S(1)}, f32[128,512]{1,0:T(8,128)S(1)}, u32[]{:S(2)}, u32[]{:S(2)}) collective-permute-start(f32[128,512]{1,0:T(8,128)S(1)} %get-tuple-element.37), channel_id=1, source_target_pairs={{0,384},{64,448},{1,385},{65,449},{2,386},{66,450},{3,387},{67,451... | collective-permute-start | bytes 786440 | tf_op jit(solution)/shard_map/ppermute | solution.py:263
  101.2 1.4 copy-start
  102.6 3.7 %copy-start.10 = (f32[128,512]{1,0:T(8,128)}, f32[128,512]{1,0:T(8,128)S(1)}, u32[]{:S(2)}) copy-start(f32[128,512]{1,0:T(8,128)S(1)} %collective-permute-done.11) | copy-start | bytes 786436
  106.3 0.7 copy-start.11
  107.0 0.7 copy-start.12
  107.7 8.1 %copy-start.14 = (f32[2,512]{1,0:T(2,128)S(1)}, f32[2,512]{1,0:T(2,128)}, u32[]{:S(2)}) copy-start(f32[2,512]{1,0:T(2,128)} %param.12) | copy-start | bytes 12292
  107.7 8.7 %copy-start.13 = (f32[2,512]{1,0:T(2,128)S(1)}, f32[2,512]{1,0:T(2,128)}, u32[]{:S(2)}) copy-start(f32[2,512]{1,0:T(2,128)} %param.11) | copy-start | bytes 12292
  107.7 9.3 %copy-start.15 = (s32[2,512]{1,0:T(2,128)S(1)}, s32[2,512]{1,0:T(2,128)}, u32[]{:S(2)}) copy-start(s32[2,512]{1,0:T(2,128)} %param.10) | copy-start | bytes 12292
  107.7 12.9 %copy-start.9 = (f32[128,1024]{1,0:T(8,128)S(1)}, f32[128,1024]{1,0:T(8,128)}, u32[]{:S(2)}) copy-start(f32[128,1024]{1,0:T(8,128)} %copy-done.8) | copy-start | bytes 1572868
  107.7 33.9 %all-to-all-start.1 = ((f32[32,128,128]{2,1,0:T(8,128)}), f32[32,128,128]{2,1,0:T(8,128)S(1)}, u32[]{:S(2)}, u32[]{:S(2)}) async-start(f32[32,128,128]{2,1,0:T(8,128)} %bitcast.57), calls=%async_computation.1 | async-start | bytes 4194304 | tf_op jit(solution)/shard_map/all_to_all | solution.py:267
  121.8 5.2 %collective-permute-start.14 = (f32[128,512]{1,0:T(8,128)S(1)}, f32[128,512]{1,0:T(8,128)S(1)}, u32[]{:S(2)}, u32[]{:S(2)}) collective-permute-start(f32[128,512]{1,0:T(8,128)S(1)} %add_select_fusion), channel_id=1, source_target_pairs={{0,64},{64,0},{1,65},{65,1},{2,66},{66,2},{3,67},{67,3},{4,68},{68... | collective-permute-start | bytes 786440 | tf_op jit(solution)/shard_map/ppermute | solution.py:242
  142.9 17.7 %all-to-all-start.2 = ((f32[16,32,128]{2,1,0:T(8,128)}), f32[16,32,128]{2,1,0:T(8,128)S(1)}, u32[]{:S(2)}, u32[]{:S(2)}) async-start(f32[16,32,128]{2,1,0:T(8,128)} %bitcast.27), calls=%async_computation.2 | async-start | bytes 524288 | tf_op jit(solution)/shard_map/all_to_all | solution.py:267
  150.0 10.5 %collective-permute-start.15 = (f32[64,128]{1,0:T(8,128)S(1)}, f32[64,128]{1,0:T(8,128)S(1)}, u32[]{:S(2)}, u32[]{:S(2)}) collective-permute-start(f32[64,128]{1,0:T(8,128)S(1)} %get-tuple-element.43), channel_id=1, source_target_pairs={{0,3},{1,0},{2,1},{3,2},{4,7},{5,4},{6,5},{7,6},{8,11},{9,8},{10,9... | collective-permute-start | bytes 98312 | tf_op jit(solution)/shard_map/ppermute | solution.py:339
  152.1 8.4 %collective-permute-start.16 = (f32[64,128]{1,0:T(8,128)S(1)}, f32[64,128]{1,0:T(8,128)S(1)}, u32[]{:S(2)}, u32[]{:S(2)}) collective-permute-start(f32[64,128]{1,0:T(8,128)S(1)} %get-tuple-element.42), channel_id=1, source_target_pairs={{0,2},{1,3},{2,0},{3,1},{4,6},{5,7},{6,4},{7,5},{8,10},{9,11},{10,... | collective-permute-start | bytes 98312 | tf_op jit(solution)/shard_map/ppermute | solution.py:339
  156.8 11.2 %collective-permute-start.17 = (f32[64,128]{1,0:T(8,128)S(1)}, f32[64,128]{1,0:T(8,128)S(1)}, u32[]{:S(2)}, u32[]{:S(2)}) collective-permute-start(f32[64,128]{1,0:T(8,128)S(1)} %get-tuple-element.41), channel_id=1, source_target_pairs={{0,1},{1,2},{2,3},{3,0},{4,5},{5,6},{6,7},{7,4},{8,9},{9,10},{10,1... | collective-permute-start | bytes 98312 | tf_op jit(solution)/shard_map/ppermute | solution.py:339
  161.2 20.7 %all-to-all-start.3 = ((f32[4,32,128]{2,1,0:T(8,128)}), f32[4,32,128]{2,1,0:T(8,128)S(1)}, u32[]{:S(2)}, u32[]{:S(2)}) async-start(f32[4,32,128]{2,1,0:T(8,128)} %tile.4), calls=%async_computation.3 | async-start | bytes 131072 | tf_op jit(solution)/shard_map/all_to_all | solution.py:267
  182.6 14.5 %all-to-all-start.4 = ((f32[16,32,128]{2,1,0:T(8,128)}), f32[16,32,128]{2,1,0:T(8,128)S(1)}, u32[]{:S(2)}, u32[]{:S(2)}) async-start(f32[16,32,128]{2,1,0:T(8,128)} %tile.5), calls=%async_computation.4 | async-start | bytes 524288 | tf_op jit(solution)/shard_map/all_to_all | solution.py:267

commit v2 on v1

--- a/solution.py
+++ b/solution.py
@@ -106,45 +106,7 @@
 N_PIECES = len(PIECES)
 
 
-def panel_kernel(where_ref, *refs):
-    pieces, (pinv_ref, yh_ref, yl_ref, first_ref, second_ref, fac_ref) = refs[:N_PIECES], refs[N_PIECES:]
-    z = where_ref[0]
-    for ref, offsets in zip(pieces, PIECES):
-        for k, offset in enumerate(offsets):
-            slot = lax.rem(z + (offset + NZ), NZ)
-            fac_ref[pl.ds(pl.multiple_of(slot * SLOT, SLOT), SLOT), :] = ref[SLOT * k:SLOT * (k + 1), :]
-    for child in range(2):
-        fh, fl = split2(fac_ref[:, C * child:C * (child + 1)])
-        for j in range(2):
-            ph, plo = split2(pinv_ref[child, :, 256 * j:256 * (j + 1)])
-            yh, yl = split2(dot3(fh, fl, ph, plo))
-            begin = C * child + 256 * j
-            yh_ref[:, begin:begin + 256] = yh
-            yl_ref[:, begin:begin + 256] = yl
-    for k, out_ref in enumerate((first_ref, second_ref)):
-        half = pl.ds(pl.multiple_of(lax.rem(z, 2) * PAD + HALF * k, HALF), HALF)
-        out_ref[...] = yh_ref[half, :].astype(f32) + yl_ref[half, :].astype(f32)
-
-
-def panel_rows(where, pieces, pinv):
-    vmem = pl.BlockSpec(memory_space=pltpu.VMEM)
-    split = jax.ShapeDtypeStruct((DEPTH, WIDE), bf16)
-    return pl.pallas_call(
-        panel_kernel,
-        out_shape=(split, split) + (jax.ShapeDtypeStruct((HALF, WIDE), f32),) * 2,
-        in_specs=[pl.BlockSpec(memory_space=pltpu.SMEM)] + [vmem] * (N_PIECES + 1),
-        out_specs=(vmem,) * 4,
-        scratch_shapes=[pltpu.VMEM((DEPTH, WIDE), f32)],
-        compiler_params=pltpu.CompilerParams(vmem_limit_bytes=12 << 20),
-        cost_estimate=pl.CostEstimate(
-            flops=6 * 6 * DEPTH * WIDE * C, bytes_accessed=7 << 20, transcendentals=0
-        ),
-    )(where, *pieces, pinv)
-
-
-def image_kernel(side, where_ref, yh_ref, yl_ref, s_ref, *refs):
-    (*added_refs, out_ref, sh_ref, sl_ref) = refs
-    half = where_ref[1] if side == 0 else 1 - where_ref[1]
+def image_rows(half, yh_ref, yl_ref, s_ref, out_ref, sh_ref, sl_ref, added_ref=None):
     rows = pl.ds(pl.multiple_of(HALF * half, HALF), HALF)
     sh, sl = split2(jnp.concatenate([s_ref[k, rows, :] for k in range(NY)], axis=0))
     sh_ref[...] = sh
@@ -160,24 +122,88 @@
                 for g in range(2):
                     part = u[begin:begin + SLOT, OWN * g:OWN * (g + 1)]
                     at = (2 * j + g, k, slice(SLOT * source, SLOT * (source + 1)))
-                    for ref in added_refs:
-                        part = part + ref[at]
-                    out_ref[at] = part
-
-
-def partial_image(side, where, yh, yl, s_parts, *added):
+                    out_ref[at] = part if added_ref is None else part + added_ref[at]
+
+
+def panel_kernel(where_ref, *refs):
+    pieces, (pinv_ref, yh_ref, yl_ref, fac_ref) = refs[:N_PIECES], refs[N_PIECES:]
+    z = where_ref[0]
+    for ref, offsets in zip(pieces, PIECES):
+        for k, offset in enumerate(offsets):
+            slot = lax.rem(z + (1 - 2 * where_ref[1]) * offset + NZ, NZ)
+            fac_ref[pl.ds(pl.multiple_of(slot * SLOT, SLOT), SLOT), :] = ref[SLOT * k:SLOT * (k + 1), :]
+    for child in range(2):
+        fh, fl = split2(fac_ref[:, C * child:C * (child + 1)])
+        for j in range(2):
+            ph, plo = split2(pinv_ref[child, :, 256 * j:256 * (j + 1)])
+            yh, yl = split2(dot3(fh, fl, ph, plo))
+            begin = C * child + 256 * j
+            yh_ref[:, begin:begin + 256] = yh
+            yl_ref[:, begin:begin + 256] = yl
+
+
+def panel_rows(where, pieces, pinv):
     vmem = pl.BlockSpec(memory_space=pltpu.VMEM)
-    return pl.pallas_call(
-        functools.partial(image_kernel, side),
+    split = jax.ShapeDtypeStruct((DEPTH, WIDE), bf16)
+    return pl.pallas_call(
+        panel_kernel,
+        out_shape=(split, split),
+        in_specs=[pl.BlockSpec(memory_space=pltpu.SMEM)] + [vmem] * (N_PIECES + 1),
+        out_specs=(vmem, vmem),
+        scratch_shapes=[pltpu.VMEM((DEPTH, WIDE), f32)],
+        compiler_params=pltpu.CompilerParams(vmem_limit_bytes=12 << 20),
+        cost_estimate=pl.CostEstimate(
+            flops=6 * 6 * DEPTH * WIDE * C, bytes_accessed=7 << 20, transcendentals=0
+        ),
+    )(where, *pieces, pinv)
+
+
+STEPS = (0, 2, 1, 3)
+
+
+def other_kernel(where_ref, yh_ref, yl_ref, s_ref, send_ref, *refs):
+    *own_refs, sh_ref, sl_ref = refs
+    rows = pl.ds(pl.multiple_of(lax.rem(where_ref[0], 2) * PAD, PAD), PAD)
+    for step, out_ref in zip(STEPS, own_refs):
+        child = lax.rem(where_ref[2] + step, 4) // 2
+        cols = pl.ds(pl.multiple_of(child * C, C), C)
+        out_ref[...] = yh_ref[rows, cols].astype(f32) + yl_ref[rows, cols].astype(f32)
+    image_rows(1 - where_ref[1], yh_ref, yl_ref, s_ref, send_ref, sh_ref, sl_ref)
+
+
+def other_image(where, yh, yl, s_parts):
+    vmem = pl.BlockSpec(memory_space=pltpu.VMEM)
+    own = jax.ShapeDtypeStruct((PAD, C), f32)
+    return pl.pallas_call(
+        other_kernel,
+        out_shape=(jax.ShapeDtypeStruct((NG, NY, HALF, OWN), f32),) + (own,) * 4,
+        in_specs=[pl.BlockSpec(memory_space=pltpu.SMEM)] + [vmem] * 3,
+        out_specs=(vmem,) * 5,
+        scratch_shapes=[pltpu.VMEM((NY * HALF, DEPTH), bf16), pltpu.VMEM((NY * HALF, DEPTH), bf16)],
+        compiler_params=pltpu.CompilerParams(vmem_limit_bytes=14 << 20),
+        cost_estimate=pl.CostEstimate(
+            flops=6 * DEPTH * WIDE * NY * HALF, bytes_accessed=8 << 20, transcendentals=0
+        ),
+    )(where, yh, yl, s_parts)
+
+
+def image_kernel(where_ref, yh_ref, yl_ref, s_ref, added_ref, out_ref, sh_ref, sl_ref):
+    image_rows(where_ref[1], yh_ref, yl_ref, s_ref, out_ref, sh_ref, sl_ref, added_ref)
+
+
+def own_image(where, yh, yl, s_parts, added):
+    vmem = pl.BlockSpec(memory_space=pltpu.VMEM)
+    return pl.pallas_call(
+        image_kernel,
         out_shape=jax.ShapeDtypeStruct((NG, NY, HALF, OWN), f32),
-        in_specs=[pl.BlockSpec(memory_space=pltpu.SMEM)] + [vmem] * (3 + len(added)),
+        in_specs=[pl.BlockSpec(memory_space=pltpu.SMEM)] + [vmem] * 4,
         out_specs=vmem,
         scratch_shapes=[pltpu.VMEM((NY * HALF, DEPTH), bf16), pltpu.VMEM((NY * HALF, DEPTH), bf16)],
-        compiler_params=pltpu.CompilerParams(vmem_limit_bytes=12 << 20),
+        compiler_params=pltpu.CompilerParams(vmem_limit_bytes=14 << 20),
         cost_estimate=pl.CostEstimate(
             flops=6 * DEPTH * WIDE * NY * HALF, bytes_accessed=6 << 20, transcendentals=0
         ),
-    )(where, yh, yl, s_parts, *added)
+    )(where, yh, yl, s_parts, added)
 
 
 def finish_kernel(block_ref, got_ref, weight_ref, y_ref, pivot_ref, off_ref, term_ref):
@@ -235,7 +261,10 @@
 
 
 def shift_z(a, step):
-    return lax.ppermute(a, Z, [(i, (i + step) % NZ) for i in range(NZ)])
+    pairs = [
+        (core * NZ + z, core * NZ + (z + (1 - 2 * core) * step) % NZ) for core in range(2) for z in range(NZ)
+    ]
+    return lax.ppermute(a, ("c",) + Z, pairs)
 
 
 def swap_core(a):
@@ -246,21 +275,54 @@
     return ((x * 2 + core) * NZ + z) * NY + y
 
 
-def from_root_core(a):
+def to_other_core(a):
     pairs = [
-        (place(z // 4, z // 2 % 2, z, y), place(z // 4, 1 - z // 2 % 2, z, y)) for z in range(NZ) for y in range(NY)
+        (place(x, z // 2 % 2, z, y), place(x, 1 - z // 2 % 2, z, y))
+        for x in range(4)
+        for z in range(NZ)
+        for y in range(NY)
     ]
     return lax.ppermute(a, AXES, pairs)
 
 
 def from_root(a, step):
     pairs = [
-        (place(z // 4, core, z, y), place((z // 4 + step) % 4, core, z, y))
+        (place(z // 4, z // 2 % 2, z, y), place((z // 4 + step) % 4, z // 2 % 2, z, y))
         for z in range(NZ)
         for y in range(NY)
-        for core in range(2)
     ]
     return lax.ppermute(a, AXES, pairs)
+
+
+def block_for(off, y):
+    return lax.dynamic_slice_in_dim(off, y * 2 * SLOT, 2 * SLOT, 0)
+
+
+def swap_y(a, bit):
+    return lax.ppermute(a, "y", [(i, i ^ bit) for i in range(NY)])
+
+
+def order_kernel(y_ref, off_ref, first_ref, second_ref, out_ref):
+    y = y_ref[0]
+    block = 2 * SLOT
+    own = off_ref[pl.ds(pl.multiple_of(block * y, block), block), :]
+    got = own, first_ref[:block], second_ref[:block], second_ref[block:]
+    for source in range(NY):
+        at = source ^ y
+        rows = jnp.where(at == 0, got[0], jnp.where(at == 1, got[1], jnp.where(at == 2, got[2], got[3])))
+        for k in range(2):
+            begin = 120 * k + SHARD * source
+            out_ref[begin:begin + SHARD, :] = rows[SLOT * k:SLOT * k + SHARD]
+
+
+def in_order(y, off, first, second):
+    vmem = pl.BlockSpec(memory_space=pltpu.VMEM)
+    return pl.pallas_call(
+        order_kernel,
+        out_shape=jax.ShapeDtypeStruct((ROWS, OWN), f32),
+        in_specs=[pl.BlockSpec(memory_space=pltpu.SMEM)] + [vmem] * 3,
+        out_specs=vmem,
+    )(y, off, first, second)
 
 
 def exchange(a, axes):
@@ -311,41 +373,29 @@
     tile_weight = lax.dynamic_index_in_dim(tile_weight.reshape(NY, 2, NY, SHARD), y, 2, keepdims=False)
     tile_weight = jnp.pad(tile_weight, ((0, 0), (0, 0), (0, SLOT - SHARD))).reshape(PAD, 1)
 
-    where = jnp.stack([z, core]).astype(jnp.int32)
-    yh, yl, first, second = panel_rows(where, pieces, panel_inverse)
-    at_core = core == z // 2 % 2
-    half = jnp.where(at_core, first, from_root_core(second))
-    send = partial_image(1, where, yh, yl, s_parts)
-    received = swap_core(send)
-    half, yh, yl = lax.optimization_barrier((half, yh, yl))
     x = lax.axis_index("x")
-    parts = [
-        from_root(lax.dynamic_slice_in_dim(half, (x + step) % 4 // 2 * C, C, 1), step) for step in (2, 1, 3)
-    ]
-    image = partial_image(0, where, yh, yl, s_parts, received)
+    where = jnp.stack([z, core, x]).astype(jnp.int32)
+    yh, yl = panel_rows(where, pieces, panel_inverse)
+    send, kept, *leaving = other_image(where, yh, yl, s_parts)
+
+    parts = [from_root(a, step) for a, step in zip(leaving, STEPS[1:])]
+    image = own_image(where, yh, yl, s_parts, swap_core(send))
     image, *parts = lax.optimization_barrier((image, *parts))
     got = exchange(image.reshape(32 * HALF, OWN), PLANE)
-    kept = lax.dynamic_slice_in_dim(half, x // 2 * C, C, 1)
     mine = jnp.where(x == z // 4, kept, parts[0] + parts[1] + parts[2])
-    other = swap_core(mine)
-    y_rows = jnp.concatenate([jnp.where(at_core, mine, other), jnp.where(at_core, other, mine)], axis=0)
+    y_rows = jnp.where(core == z // 2 % 2, mine, to_other_core(mine))
 
     off, term = finish(
         block.reshape(1).astype(jnp.int32), got.reshape(4, 2, NY, HALF, OWN), tile_weight, y_rows, pivot_part
     )
 
     rows = exchange(term, ("l", "y")).reshape(16, 32, OWN).sum(0)
-    blocks = [
-        lax.ppermute(
-            lax.dynamic_slice_in_dim(off, (y + step) % NY * 2 * SLOT, 2 * SLOT, 0),
-            "y", [(i, (i + step) % NY) for i in range(NY)],
-        ) if step else lax.dynamic_slice_in_dim(off, y * 2 * SLOT, 2 * SLOT, 0)
-        for step in range(NY)
-    ]
+    first = swap_y(jnp.concatenate([block_for(off, y ^ 1), block_for(off, y ^ 3)], axis=0), 1)
+    rows, first = lax.optimization_barrier((rows, first))
+    second = swap_y(jnp.concatenate([block_for(off, y ^ 2), first[2 * SLOT:]], axis=0), 2)
     rows = exchange(jnp.tile(rows, (4, 1)), "h").reshape(4, 32, OWN).sum(0)
     panel = exchange(jnp.tile(rows, (16, 1)), ("l", "y"))
-    blocks = jnp.stack([b.reshape(2, SLOT, OWN)[:, :SHARD] for b in blocks[::-1] + blocks[:0:-1]])
-    off = lax.dynamic_slice_in_dim(blocks, 3 - y, NY, 0).transpose(1, 0, 2, 3).reshape(ROWS, OWN)
+    off = in_order(y.reshape(1).astype(jnp.int32), off, first, second)
     return off, panel
 
 

time: 199 us -> 184 us (0.925)
  blocking collectives: 0 us -> 20.4 us
  starting transfers between devices: 100 us -> 83.5 us
  waiting for transfers between devices: 53.6 us -> 38.1 us
    all_to_all x0 -> x1, blocking collectives: none -> 20.4 us  [exchange(): return lax.all_to_all(a, axes, 0, 0, tiled=True)]
    all_to_all x5 -> x4, waiting for transfers between devices: 36.3 us -> 21.2 us  [exchange(): return lax.all_to_all(a, axes, 0, 0, tiled=True)]
    ppermute x13 -> x12, starting transfers between devices: 60.1 us -> 47.9 us  [the longest x9 39.9 us: shift_z(): return lax.ppermute(a, ('c',) + Z, pairs)]
    all_to_all x5 -> x4, starting transfers between devices: 31.8 us -> 25.3 us  [exchange(): return lax.all_to_all(a, axes, 0, 0, tiled=True)]
    ppermute x3, starting transfers between devices: 4.29 us -> 8.35 us  [from_root(): return lax.ppermute(a, AXES, pairs)]
    pallas_call x3 -> x4, Pallas kernels: 11.9 us -> 10.4 us  [the longest x1 3.22 us: other_image(): pl.pallas_call(other_kernel, out_shape=(jax.ShapeDtypeStruct((NG, NY, HAL...]
    ppermute x13 -> x12, waiting for transfers between devices: 13.6 us -> 12.5 us  [the longest x9 8.59 us: shift_z(): return lax.ppermute(a, ('c',) + Z, pairs)]
    unnamed x41 -> x39, local copies, waits for them, and re-layouts: 11.1 us -> 11 us
  transfers between devices with their start and end apart: 23 -> 20, of which waited for: 9 -> 9; matrix products, arithmetic and copies ran while one was open for 6% -> 6% of each run, Pallas kernels for 5% -> 6%
where the time goes in v2:
time: 184 us; the launch traced here: 182 us
  starting transfers between devices  83.5 us (45%)
  waiting for transfers between devices  38.1 us (21%)
  blocking collectives  20.4 us (11%)
  local copies, waits for them, and re-layouts  15.8 us (9%)
  Pallas kernels  14.8 us (8%)
  other arithmetic  6.16 us (3%)
  matrix products  2.27 us (1%)
    ppermute x9, starting transfers between devices, shift_z(): return lax.ppermute(a, ('c',) + Z, pairs)  39.9 us
    all_to_all x4, starting transfers between devices, exchange(): return lax.all_to_all(a, axes, 0, 0, tiled=True)  25.3 us
    all_to_all x4, waiting for transfers between devices, exchange(): return lax.all_to_all(a, axes, 0, 0, tiled=True)  21.2 us
    all_to_all x1, blocking collectives, exchange(): return lax.all_to_all(a, axes, 0, 0, tiled=True)  20.4 us
    unnamed x39, local copies, waits for them, and re-layouts  11 us
    ppermute x9, waiting for transfers between devices, shift_z(): return lax.ppermute(a, ('c',) + Z, pairs)  8.59 us
    ppermute x3, starting transfers between devices, from_root(): return lax.ppermute(a, AXES, pairs)  8.35 us
    ppermute x2, starting transfers between devices, swap_y(): return lax.ppermute(a, 'y', [(i, i ^ bit) for i in range(NY)])  6.02 us
  transfers between devices with their start and end apart: 20, of which 9 were waited for; matrix products, arithmetic and copies ran while one was open for 6% of the time, Pallas kernels for 6%

profile of v2, /device:TPU:8, one launch (start us, length us, event | category | flops | bytes accessed | tf_op | source)
XLA Modules:
  0.0 182.4 jit_solution(16642471269346019008)
XLA Ops:
  1.7 0.9 mul.127
  2.7 12.7 %collective-permute-start.1 = (f32[32,1024]{1,0:T(8,128)S(1)}, f32[32,1024]{1,0:T(8,128)S(1)}, u32[]{:S(2)}, u32[]{:S(2)}) collective-permute-start(f32[32,1024]{1,0:T(8,128)S(1)} %pad.8), channel_id=1, source_target_pairs={{0,48},{4,52},{8,56},{12,60},{16,0},{20,4},{24,8},{28,12},{32,16},... | collective-permute-start | bytes 393224 | tf_op jit(solution)/shard_map/ppermute | solution.py:267
  15.4 1.9 %collective-permute-start = (f32[32,1024]{1,0:T(8,128)S(1)}, f32[32,1024]{1,0:T(8,128)S(1)}, u32[]{:S(2)}, u32[]{:S(2)}) collective-permute-start(f32[32,1024]{1,0:T(8,128)S(1)} %pad.8), channel_id=1, source_target_pairs={{0,16},{4,20},{8,24},{12,28},{16,32},{20,36},{24,40},{28,44},{32,4... | collective-permute-start | bytes 393224 | tf_op jit(solution)/shard_map/ppermute | solution.py:267
  17.3 1.5 copy-done.9
  18.8 3.2 %shard_map.87 = f32[4,256,512]{2,1,0:T(8,128)S(1)} custom-call(f32[240,1920]{1,0:T(8,128)S(1)} %copy-done.9), custom_call_target="tpu_custom_call" | custom-call | flops 1258291200 | bytes 3932160 | tf_op jit(solution)/shard_map/pallas_call | solution.py:87
  22.1 1.3 copy-done.1
  23.4 4.9 %all-to-all-start = ((f32[4,256,512]{2,1,0:T(8,128)}), f32[4,256,512]{2,1,0:T(8,128)S(1)}, u32[]{:S(2)}, u32[]{:S(2)}) async-start(f32[4,256,512]{2,1,0:T(8,128)} %copy-done.1), calls=%async_computation | async-start | bytes 4194304 | tf_op jit(solution)/shard_map/all_to_all | solution.py:329
  28.3 1.4 collective-permute-done
  29.8 4.3 %collective-permute-start.2 = (f32[96,1024]{1,0:T(8,128)S(1)}, f32[96,1024]{1,0:T(8,128)S(1)}, u32[]{:S(2)}, u32[]{:S(2)}) collective-permute-start(f32[96,1024]{1,0:T(8,128)S(1)} %pad_maximum_fusion.refs_0_), channel_id=1, source_target_pairs={{0,4},{4,8},{8,12},{12,16},{16,20},{20,24},{24,28},{28,32},{32,36}... | collective-permute-start | bytes 1179656 | tf_op jit(solution)/shard_map/ppermute | solution.py:267
  34.1 2.8 %collective-permute-start.3 = (f32[96,1024]{1,0:T(8,128)S(1)}, f32[96,1024]{1,0:T(8,128)S(1)}, u32[]{:S(2)}, u32[]{:S(2)}) collective-permute-start(f32[96,1024]{1,0:T(8,128)S(1)} %pad_maximum_fusion.refs_0_), channel_id=1, source_target_pairs={{0,60},{4,0},{8,4},{12,8},{16,12},{20,16},{24,20},{28,24},{32,28},... | collective-permute-start | bytes 1179656 | tf_op jit(solution)/shard_map/ppermute | solution.py:267
  36.9 4.0 %collective-permute-start.4 = (f32[32,1024]{1,0:T(8,128)S(1)}, f32[32,1024]{1,0:T(8,128)S(1)}, u32[]{:S(2)}, u32[]{:S(2)}) collective-permute-start(f32[32,1024]{1,0:T(8,128)S(1)} %collective-permute-done), channel_id=1, source_target_pairs={{0,16},{4,20},{8,24},{12,28},{16,32},{20,36},{24,40},{28,44},{32,4... | collective-permute-start | bytes 393224 | tf_op jit(solution)/shard_map/ppermute | solution.py:267
  40.9 3.4 %collective-permute-done.2.refs_1_ = f32[96,1024]{1,0:T(8,128)S(1)} collective-permute-done((f32[96,1024]{1,0:T(8,128)S(1)}, f32[96,1024]{1,0:T(8,128)S(1)}, u32[]{:S(2)}, u32[]{:S(2)}) %collective-permute-start.2) | collective-permute-done | bytes 393248 | tf_op jit(solution)/shard_map/ppermute | solution.py:267
  44.3 4.7 %collective-permute-start.5 = (f32[64,1024]{1,0:T(8,128)S(1)}, f32[64,1024]{1,0:T(8,128)S(1)}, u32[]{:S(2)}, u32[]{:S(2)}) collective-permute-start(f32[64,1024]{1,0:T(8,128)S(1)} %slice.70), channel_id=1, source_target_pairs={{0,4},{4,8},{8,12},{12,16},{16,20},{20,24},{24,28},{28,32},{32,36}... | collective-permute-start | bytes 786440 | tf_op jit(solution)/shard_map/ppermute | solution.py:267
  49.7 2.5 %collective-permute-start.6 = (f32[64,1024]{1,0:T(8,128)S(1)}, f32[64,1024]{1,0:T(8,128)S(1)}, u32[]{:S(2)}, u32[]{:S(2)}) collective-permute-start(f32[64,1024]{1,0:T(8,128)S(1)} %slice.71), channel_id=1, source_target_pairs={{0,60},{4,0},{8,4},{12,8},{16,12},{20,16},{24,20},{28,24},{32,28},... | collective-permute-start | bytes 786440 | tf_op jit(solution)/shard_map/ppermute | solution.py:267
  52.1 3.4 %collective-permute-start.7 = (f32[32,1024]{1,0:T(8,128)S(1)}, f32[32,1024]{1,0:T(8,128)S(1)}, u32[]{:S(2)}, u32[]{:S(2)}) collective-permute-start(f32[32,1024]{1,0:T(8,128)S(1)} %collective-permute-done.4.refs_3_), channel_id=1, source_target_pairs={{0,4},{4,8},{8,12},{12,16},{16,20},{20,24},{24,28},{28,32},{32,36}... | collective-permute-start | bytes 393224 | tf_op jit(solution)/shard_map/ppermute | solution.py:267
  55.5 3.7 %collective-permute-start.8 = (f32[32,1024]{1,0:T(8,128)S(1)}, f32[32,1024]{1,0:T(8,128)S(1)}, u32[]{:S(2)}, u32[]{:S(2)}) collective-permute-start(f32[32,1024]{1,0:T(8,128)S(1)} %collective-permute-done.4.refs_3_), channel_id=1, source_target_pairs={{0,60},{4,0},{8,4},{12,8},{16,12},{20,16},{24,20},{28,24},{32,28},... | collective-permute-start | bytes 393224 | tf_op jit(solution)/shard_map/ppermute | solution.py:267
  59.3 1.0 collective-permute-done.7.refs_6_
  60.3 2.1 %collective-permute-done.8.refs_7_ = f32[32,1024]{1,0:T(8,128)S(1)} collective-permute-done((f32[32,1024]{1,0:T(8,128)S(1)}, f32[32,1024]{1,0:T(8,128)S(1)}, u32[]{:S(2)}, u32[]{:S(2)}) %collective-permute-start.8) | collective-permute-done | bytes 131104 | tf_op jit(solution)/shard_map/ppermute | solution.py:267
  62.4 1.6 copy-done.5
  64.0 2.5 %shard_map.86 = (bf16[512,1024]{1,0:T(8,128)(2,1)S(1)}, bf16[512,1024]{1,0:T(8,128)(2,1)S(1)}) custom-call(s32[3]{0:T(128)S(1)} %pad_add_fusion.where_ref, f32[96,1024]{1,0:T(8,128)S(1)} %pad_maximum_fusion.refs_0_, f32[96,1024]{1,0:T(8,128)S(1)} %collective-permute-done.2.refs_1_, f32[96,1024]{1,0:T(8,128)S(1)} %collective-permute-done.3.refs_2_, ...), custom_call_target="tpu_custom_call" | custom-call | flops 9663676416 | bytes 7340032 | tf_op jit(solution)/shard_map/pallas_call | solution.py:148
  66.5 1.0 copy-done.2
  67.5 1.2 copy-done.3
  68.7 3.2 %shard_map.88 = (f32[8,4,128,128]{3,2,1,0:T(8,128)S(1)}, f32[256,512]{1,0:T(8,128)S(1)}, f32[256,512]{1,0:T(8,128)S(1)}, f32[256,512]{1,0:T(8,128)S(1)}, f32[256,512]{1,0:T(8,128)S(1)}) custom-call(s32[3]{0:T(128)S(1)} %pad_add_fusion.where_ref, bf16[512,1024]{1,0:T(8,128)(2,1)S(1)} %get-tuple-element.17.yh_ref, bf16[512,1024]{1,0:T(8,128)(2,1)S(1)} %copy-done.3, ...), custom_call_target="tpu_custom_call" | custom-call | flops 1610612736 | bytes 8388608 | tf_op jit(solution)/shard_map/pallas_call | solution.py:177
  72.8 1.9 %collective-permute-start.9 = (f32[8,4,128,128]{3,2,1,0:T(8,128)S(1)}, f32[8,4,128,128]{3,2,1,0:T(8,128)S(1)}, u32[]{:S(2)}, u32[]{:S(2)}) collective-permute-start(f32[8,4,128,128]{3,2,1,0:T(8,128)S(1)} %get-tuple-element.19), channel_id=1, source_target_pairs={{0,64},{64,0},{1,65},{65,1},{2,66},{66,2},{3,67},{67,3},{4,68},{68... | collective-permute-start | bytes 6291464 | tf_op jit(solution)/shard_map/ppermute | solution.py:271
  74.7 5.0 %collective-permute-start.10 = (f32[256,512]{1,0:T(8,128)S(1)}, f32[256,512]{1,0:T(8,128)S(1)}, u32[]{:S(2)}, u32[]{:S(2)}) collective-permute-start(f32[256,512]{1,0:T(8,128)S(1)} %get-tuple-element.20), channel_id=1, source_target_pairs={{0,256},{1,257},{2,258},{3,259},{4,260},{5,261},{6,262},{7,263},{7... | collective-permute-start | bytes 1572872 | tf_op jit(solution)/shard_map/ppermute | solution.py:294
  79.7 2.1 %collective-permute-start.11 = (f32[256,512]{1,0:T(8,128)S(1)}, f32[256,512]{1,0:T(8,128)}, u32[]{:S(2)}, u32[]{:S(2)}) collective-permute-start(f32[256,512]{1,0:T(8,128)S(1)} %get-tuple-element.21), channel_id=1, source_target_pairs={{0,128},{1,129},{2,130},{3,131},{4,132},{5,133},{6,134},{7,135},{7... | collective-permute-start | bytes 1572872 | tf_op jit(solution)/shard_map/ppermute | solution.py:294
  81.7 1.3 collective-permute-start.12
  83.1 3.0 %shard_map.89 = f32[8,4,128,128]{3,2,1,0:T(8,128)S(1)} custom-call(s32[3]{0:T(128)S(1)} %pad_add_fusion.where_ref, bf16[512,1024]{1,0:T(8,128)(2,1)S(1)} %get-tuple-element.17.yh_ref, bf16[512,1024]{1,0:T(8,128)(2,1)S(1)} %copy-done.4, f32[4,256,512]{2,1,0:T(8,128)S(1)} %all-to-all-done.s_ref, f32[8,4,128,128]{3,2,1,0:T(8,128)S(1)} %collective-permute-done.9.added_ref), custom_call_target="tpu_custom_call" | custom-call | flops 1610612736 | bytes 6291456 | tf_op jit(solution)/shard_map/pallas_call | solution.py:196
  86.1 1.3 copy-done
  87.5 4.5 %collective-permute-done.11 = f32[256,512]{1,0:T(8,128)} collective-permute-done((f32[256,512]{1,0:T(8,128)S(1)}, f32[256,512]{1,0:T(8,128)}, u32[]{:S(2)}, u32[]{:S(2)}) %collective-permute-start.11) | collective-permute-done | bytes 524320 | tf_op jit(solution)/shard_map/ppermute | solution.py:294
  91.9 0.8 copy-done.12
  92.8 7.2 %all-to-all-start.1 = ((f32[32,128,128]{2,1,0:T(8,128)}), f32[32,128,128]{2,1,0:T(8,128)S(1)}, u32[]{:S(2)}, u32[]{:S(2)}) async-start(f32[32,128,128]{2,1,0:T(8,128)} %bitcast.31), calls=%async_computation.1 | async-start | bytes 4194304 | tf_op jit(solution)/shard_map/all_to_all | solution.py:329
  102.6 1.5 constant_dynamic-slice_fusion.1
  104.1 1.4 add_select_fusion
  105.5 2.0 %collective-permute-start.13 = (f32[256,512]{1,0:T(8,128)S(1)}, f32[256,512]{1,0:T(8,128)S(1)}, u32[]{:S(2)}, u32[]{:S(2)}) collective-permute-start(f32[256,512]{1,0:T(8,128)S(1)} %add_select_fusion), channel_id=1, source_target_pairs={{0,64},{1,65},{2,66},{3,67},{4,68},{5,69},{6,70},{7,71},{72,8},{73... | collective-permute-start | bytes 1572872 | tf_op jit(solution)/shard_map/ppermute | solution.py:285
  107.5 0.8 fusion.22
  108.3 2.0 %divide_select_fusion = (f32[512]{0:T(512)S(1)}, f32[512]{0:T(512)S(1)}, f32[512]{0:T(512)S(1)}) fusion(pred[512]{0:T(512)(128)(4,1)S(1)} %get-tuple-element.32, f32[512]{0:T(512)S(1)} %bitcast.41, pred[512]{0:T(512)(128)(4,1)S(1)} %get-tuple-element.33, f32[512]{0:T(512)S(1)} %bitcast.39, f32[511]{0:T(512)S(1)} %bitcast.36, f32[1]{0:T(128)} %bitcast.16, ...), kind=kLoop, calls=%fused_computation.40 | loop fusion | flops 9216 | bytes 19968 | tf_op jit(solution)/shard_map/jit(_where)/select_n | solution.py:249
  110.3 2.3 %convolution_select_fusion.pivot_ref = f32[32,128]{1,0:T(8,128)S(1)} fusion(f32[1,1,128]{2,1,0:T(1,128)S(1)} %get-tuple-element.36, f32[1,511,128]{2,1,0:T(8,128)S(1)} %get-tuple-element.38, f32[1,511,128]{2,1,0:T(8,128)S(1)} %get-tuple-element.37, f32[1,1,128]{2,1,0:T(1,128)S(1)} %get-tuple-element.35, f32[2,512,512]{2,1,0:T(8,128)} %refs_8_.1, ...), kind=kOutput, calls=%fused_computation | convolution fusion | flops 25628672 | bytes 1073664 | tf_op jit(solution)/shard_map/dot_general | solution.py:364
  112.7 14.1 %all-to-all-done.1 = f32[32,128,128]{2,1,0:T(8,128)S(1)} async-done(((f32[32,128,128]{2,1,0:T(8,128)}), f32[32,128,128]{2,1,0:T(8,128)S(1)}, u32[]{:S(2)}, u32[]{:S(2)}) %all-to-all-start.1) | async-done | bytes 2097184 | tf_op jit(solution)/shard_map/all_to_all | solution.py:329
  126.8 1.2 shard_map.90
  128.0 8.0 %all-to-all-start.2 = ((f32[16,32,128]{2,1,0:T(8,128)}), f32[16,32,128]{2,1,0:T(8,128)S(1)}, u32[]{:S(2)}, u32[]{:S(2)}) async-start(f32[16,32,128]{2,1,0:T(8,128)} %bitcast.20), calls=%async_computation.2 | async-start | bytes 524288 | tf_op jit(solution)/shard_map/all_to_all | solution.py:329
  136.0 2.0 %collective-permute-start.14 = (f32[128,128]{1,0:T(8,128)S(1)}, f32[128,128]{1,0:T(8,128)S(1)}, u32[]{:S(2)}, u32[]{:S(2)}) collective-permute-start(f32[128,128]{1,0:T(8,128)S(1)} %pad_maximum_fusion.1), channel_id=1, source_target_pairs={{0,1},{1,0},{2,3},{3,2},{4,5},{5,4},{6,7},{7,6},{8,9},{9,8},{10,11... | collective-permute-start | bytes 196616 | tf_op jit(solution)/shard_map/ppermute | solution.py:302
  138.0 7.0 %all-to-all-done.2 = f32[16,32,128]{2,1,0:T(8,128)S(1)} async-done(((f32[16,32,128]{2,1,0:T(8,128)}), f32[16,32,128]{2,1,0:T(8,128)S(1)}, u32[]{:S(2)}, u32[]{:S(2)}) %all-to-all-start.2) | async-done | bytes 262176 | tf_op jit(solution)/shard_map/all_to_all | solution.py:329
  145.2 20.4 %all_to_all.38 = f32[4,32,128]{2,1,0:T(8,128)S(1)} all-to-all(f32[4,32,128]{2,1,0:T(8,128)S(1)} %tile.4), channel_id=1, replica_groups=mesh['x'=4,'c'=2,'h'=4,'l'=4,'y'=4] {'h'}, dimensions={0} | all-to-all | bytes 131072 | tf_op jit(solution)/shard_map/all_to_all | solution.py:329
  166.3 5.2 %all-to-all-start.4 = ((f32[16,32,128]{2,1,0:T(8,128)}), f32[16,32,128]{2,1,0:T(8,128)S(1)}, u32[]{:S(2)}, u32[]{:S(2)}) async-start(f32[16,32,128]{2,1,0:T(8,128)} %tile.5), calls=%async_computation.4 | async-start | bytes 524288 | tf_op jit(solution)/shard_map/all_to_all | solution.py:329
  171.6 4.0 %collective-permute-start.15 = (f32[128,128]{1,0:T(8,128)S(1)}, f32[128,128]{1,0:T(8,128)S(1)}, u32[]{:S(2)}, u32[]{:S(2)}) collective-permute-start(f32[128,128]{1,0:T(8,128)S(1)} %pad_maximum_fusion.2), channel_id=1, source_target_pairs={{0,2},{1,3},{2,0},{3,1},{4,6},{5,7},{6,4},{7,5},{8,10},{9,11},{10,... | collective-permute-start | bytes 196616 | tf_op jit(solution)/shard_map/ppermute | solution.py:302
  175.5 3.9 %collective-permute-done.15.second_ref = f32[128,128]{1,0:T(8,128)S(1)} collective-permute-done((f32[128,128]{1,0:T(8,128)S(1)}, f32[128,128]{1,0:T(8,128)S(1)}, u32[]{:S(2)}, u32[]{:S(2)}) %collective-permute-start.15) | collective-permute-done | bytes 65568 | tf_op jit(solution)/shard_map/ppermute | solution.py:302
  180.1 1.6 shard_map.91
  (72 shorter events, 7.3 us)
Async XLA Ops:
  2.7 25.7 %collective-permute-start.1 = (f32[32,1024]{1,0:T(8,128)S(1)}, f32[32,1024]{1,0:T(8,128)S(1)}, u32[]{:S(2)}, u32[]{:S(2)}) collective-permute-start(f32[32,1024]{1,0:T(8,128)S(1)} %pad.8), channel_id=1, source_target_pairs={{0,48},{4,52},{8,56},{12,60},{16,0},{20,4},{24,8},{28,12},{32,16},... | collective-permute-start | bytes 393224 | tf_op jit(solution)/shard_map/ppermute | solution.py:267
  15.4 14.4 %collective-permute-start = (f32[32,1024]{1,0:T(8,128)S(1)}, f32[32,1024]{1,0:T(8,128)S(1)}, u32[]{:S(2)}, u32[]{:S(2)}) collective-permute-start(f32[32,1024]{1,0:T(8,128)S(1)} %pad.8), channel_id=1, source_target_pairs={{0,16},{4,20},{8,24},{12,28},{16,32},{20,36},{24,40},{28,44},{32,4... | collective-permute-start | bytes 393224 | tf_op jit(solution)/shard_map/ppermute | solution.py:267
  17.3 1.5 copy-start.9
  22.1 1.3 copy-start.1
  23.4 44.1 %all-to-all-start = ((f32[4,256,512]{2,1,0:T(8,128)}), f32[4,256,512]{2,1,0:T(8,128)S(1)}, u32[]{:S(2)}, u32[]{:S(2)}) async-start(f32[4,256,512]{2,1,0:T(8,128)} %copy-done.1), calls=%async_computation | async-start | bytes 4194304 | tf_op jit(solution)/shard_map/all_to_all | solution.py:329
  29.8 14.5 %collective-permute-start.2 = (f32[96,1024]{1,0:T(8,128)S(1)}, f32[96,1024]{1,0:T(8,128)S(1)}, u32[]{:S(2)}, u32[]{:S(2)}) collective-permute-start(f32[96,1024]{1,0:T(8,128)S(1)} %pad_maximum_fusion.refs_0_), channel_id=1, source_target_pairs={{0,4},{4,8},{8,12},{12,16},{16,20},{20,24},{24,28},{28,32},{32,36}... | collective-permute-start | bytes 1179656 | tf_op jit(solution)/shard_map/ppermute | solution.py:267
  34.1 15.5 %collective-permute-start.3 = (f32[96,1024]{1,0:T(8,128)S(1)}, f32[96,1024]{1,0:T(8,128)S(1)}, u32[]{:S(2)}, u32[]{:S(2)}) collective-permute-start(f32[96,1024]{1,0:T(8,128)S(1)} %pad_maximum_fusion.refs_0_), channel_id=1, source_target_pairs={{0,60},{4,0},{8,4},{12,8},{16,12},{20,16},{24,20},{28,24},{32,28},... | collective-permute-start | bytes 1179656 | tf_op jit(solution)/shard_map/ppermute | solution.py:267
  36.9 15.2 %collective-permute-start.4 = (f32[32,1024]{1,0:T(8,128)S(1)}, f32[32,1024]{1,0:T(8,128)S(1)}, u32[]{:S(2)}, u32[]{:S(2)}) collective-permute-start(f32[32,1024]{1,0:T(8,128)S(1)} %collective-permute-done), channel_id=1, source_target_pairs={{0,16},{4,20},{8,24},{12,28},{16,32},{20,36},{24,40},{28,44},{32,4... | collective-permute-start | bytes 393224 | tf_op jit(solution)/shard_map/ppermute | solution.py:267
  44.3 18.1 %collective-permute-start.5 = (f32[64,1024]{1,0:T(8,128)S(1)}, f32[64,1024]{1,0:T(8,128)S(1)}, u32[]{:S(2)}, u32[]{:S(2)}) collective-permute-start(f32[64,1024]{1,0:T(8,128)S(1)} %slice.70), channel_id=1, source_target_pairs={{0,4},{4,8},{8,12},{12,16},{16,20},{20,24},{24,28},{28,32},{32,36}... | collective-permute-start | bytes 786440 | tf_op jit(solution)/shard_map/ppermute | solution.py:267
  49.7 12.7 %collective-permute-start.6 = (f32[64,1024]{1,0:T(8,128)S(1)}, f32[64,1024]{1,0:T(8,128)S(1)}, u32[]{:S(2)}, u32[]{:S(2)}) collective-permute-start(f32[64,1024]{1,0:T(8,128)S(1)} %slice.71), channel_id=1, source_target_pairs={{0,60},{4,0},{8,4},{12,8},{16,12},{20,16},{24,20},{28,24},{32,28},... | collective-permute-start | bytes 786440 | tf_op jit(solution)/shard_map/ppermute | solution.py:267
  52.1 8.1 %collective-permute-start.7 = (f32[32,1024]{1,0:T(8,128)S(1)}, f32[32,1024]{1,0:T(8,128)S(1)}, u32[]{:S(2)}, u32[]{:S(2)}) collective-permute-start(f32[32,1024]{1,0:T(8,128)S(1)} %collective-permute-done.4.refs_3_), channel_id=1, source_target_pairs={{0,4},{4,8},{8,12},{12,16},{16,20},{20,24},{24,28},{28,32},{32,36}... | collective-permute-start | bytes 393224 | tf_op jit(solution)/shard_map/ppermute | solution.py:267
  55.5 6.9 %collective-permute-start.8 = (f32[32,1024]{1,0:T(8,128)S(1)}, f32[32,1024]{1,0:T(8,128)S(1)}, u32[]{:S(2)}, u32[]{:S(2)}) collective-permute-start(f32[32,1024]{1,0:T(8,128)S(1)} %collective-permute-done.4.refs_3_), channel_id=1, source_target_pairs={{0,60},{4,0},{8,4},{12,8},{16,12},{20,16},{24,20},{28,24},{32,28},... | collective-permute-start | bytes 393224 | tf_op jit(solution)/shard_map/ppermute | solution.py:267
  62.4 1.6 copy-start.5
  66.5 1.0 copy-start.2
  67.5 1.2 copy-start.3
  68.7 14.3 %copy-start.4 = (bf16[512,1024]{1,0:T(8,128)(2,1)S(1)}, bf16[512,1024]{1,0:T(8,128)(2,1)}, u32[]{:S(2)}) copy-start(bf16[512,1024]{1,0:T(8,128)(2,1)} %copy-done.2) | copy-start | bytes 3145732
  72.0 0.8 copy-start.6
  72.8 10.3 %collective-permute-start.9 = (f32[8,4,128,128]{3,2,1,0:T(8,128)S(1)}, f32[8,4,128,128]{3,2,1,0:T(8,128)S(1)}, u32[]{:S(2)}, u32[]{:S(2)}) collective-permute-start(f32[8,4,128,128]{3,2,1,0:T(8,128)S(1)} %get-tuple-element.19), channel_id=1, source_target_pairs={{0,64},{64,0},{1,65},{65,1},{2,66},{66,2},{3,67},{67,3},{4,68},{68... | collective-permute-start | bytes 6291464 | tf_op jit(solution)/shard_map/ppermute | solution.py:271
  74.7 12.8 %collective-permute-start.10 = (f32[256,512]{1,0:T(8,128)S(1)}, f32[256,512]{1,0:T(8,128)S(1)}, u32[]{:S(2)}, u32[]{:S(2)}) collective-permute-start(f32[256,512]{1,0:T(8,128)S(1)} %get-tuple-element.20), channel_id=1, source_target_pairs={{0,256},{1,257},{2,258},{3,259},{4,260},{5,261},{6,262},{7,263},{7... | collective-permute-start | bytes 1572872 | tf_op jit(solution)/shard_map/ppermute | solution.py:294
  79.7 12.3 %collective-permute-start.11 = (f32[256,512]{1,0:T(8,128)S(1)}, f32[256,512]{1,0:T(8,128)}, u32[]{:S(2)}, u32[]{:S(2)}) collective-permute-start(f32[256,512]{1,0:T(8,128)S(1)} %get-tuple-element.21), channel_id=1, source_target_pairs={{0,128},{1,129},{2,130},{3,131},{4,132},{5,133},{6,134},{7,135},{7... | collective-permute-start | bytes 1572872 | tf_op jit(solution)/shard_map/ppermute | solution.py:294
  81.7 10.2 %collective-permute-start.12 = (f32[256,512]{1,0:T(8,128)S(1)}, f32[256,512]{1,0:T(8,128)S(1)}, u32[]{:S(2)}, u32[]{:S(2)}) collective-permute-start(f32[256,512]{1,0:T(8,128)S(1)} %get-tuple-element.22), channel_id=1, source_target_pairs={{0,384},{1,385},{2,386},{3,387},{4,388},{5,389},{6,390},{7,391},{7... | collective-permute-start | bytes 1572872 | tf_op jit(solution)/shard_map/ppermute | solution.py:294
  86.1 1.3 copy-start
  87.5 4.5 %copy-start.10 = (f32[256,512]{1,0:T(8,128)}, f32[256,512]{1,0:T(8,128)S(1)}, u32[]{:S(2)}) copy-start(f32[256,512]{1,0:T(8,128)S(1)} %collective-permute-done.10) | copy-start | bytes 1572868
  91.9 0.8 copy-start.12
  92.7 8.5 %copy-start.16 = (f32[2,512]{1,0:T(2,128)S(1)}, f32[2,512]{1,0:T(2,128)}, u32[]{:S(2)}) copy-start(f32[2,512]{1,0:T(2,128)} %param.12) | copy-start | bytes 12292
  92.7 9.1 %copy-start.15 = (f32[2,512]{1,0:T(2,128)S(1)}, f32[2,512]{1,0:T(2,128)}, u32[]{:S(2)}) copy-start(f32[2,512]{1,0:T(2,128)} %param.11) | copy-start | bytes 12292
  92.7 9.7 %copy-start.17 = (s32[2,512]{1,0:T(2,128)S(1)}, s32[2,512]{1,0:T(2,128)}, u32[]{:S(2)}) copy-start(s32[2,512]{1,0:T(2,128)} %param.10) | copy-start | bytes 12292
  92.7 11.3 %copy-start.7 = (f32[256,512]{1,0:T(8,128)S(1)}, f32[256,512]{1,0:T(8,128)}, u32[]{:S(2)}) copy-start(f32[256,512]{1,0:T(8,128)} %copy-done.6) | copy-start | bytes 1572868
  92.8 11.3 %copy-start.11 = (f32[256,512]{1,0:T(8,128)S(1)}, f32[256,512]{1,0:T(8,128)}, u32[]{:S(2)}) copy-start(f32[256,512]{1,0:T(8,128)} %copy-done.10) | copy-start | bytes 1572868
  92.8 34.1 %all-to-all-start.1 = ((f32[32,128,128]{2,1,0:T(8,128)}), f32[32,128,128]{2,1,0:T(8,128)S(1)}, u32[]{:S(2)}, u32[]{:S(2)}) async-start(f32[32,128,128]{2,1,0:T(8,128)} %bitcast.31), calls=%async_computation.1 | async-start | bytes 4194304 | tf_op jit(solution)/shard_map/all_to_all | solution.py:329
  105.5 7.1 %collective-permute-start.13 = (f32[256,512]{1,0:T(8,128)S(1)}, f32[256,512]{1,0:T(8,128)S(1)}, u32[]{:S(2)}, u32[]{:S(2)}) collective-permute-start(f32[256,512]{1,0:T(8,128)S(1)} %add_select_fusion), channel_id=1, source_target_pairs={{0,64},{1,65},{2,66},{3,67},{4,68},{5,69},{6,70},{7,71},{72,8},{73... | collective-permute-start | bytes 1572872 | tf_op jit(solution)/shard_map/ppermute | solution.py:285
  128.0 51.4 %copy-start.8 = (f32[256,128]{1,0:T(8,128)}, f32[256,128]{1,0:T(8,128)S(1)}, u32[]{:S(2)}) copy-start(f32[256,128]{1,0:T(8,128)S(1)} %get-tuple-element.28.off_ref) | copy-start | bytes 393220
  128.0 17.1 %all-to-all-start.2 = ((f32[16,32,128]{2,1,0:T(8,128)}), f32[16,32,128]{2,1,0:T(8,128)S(1)}, u32[]{:S(2)}, u32[]{:S(2)}) async-start(f32[16,32,128]{2,1,0:T(8,128)} %bitcast.20), calls=%async_computation.2 | async-start | bytes 524288 | tf_op jit(solution)/shard_map/all_to_all | solution.py:329
  136.0 9.1 %collective-permute-start.14 = (f32[128,128]{1,0:T(8,128)S(1)}, f32[128,128]{1,0:T(8,128)S(1)}, u32[]{:S(2)}, u32[]{:S(2)}) collective-permute-start(f32[128,128]{1,0:T(8,128)S(1)} %pad_maximum_fusion.1), channel_id=1, source_target_pairs={{0,1},{1,0},{2,3},{3,2},{4,5},{5,4},{6,7},{7,6},{8,9},{9,8},{10,11... | collective-permute-start | bytes 196616 | tf_op jit(solution)/shard_map/ppermute | solution.py:302
  145.1 34.3 %copy-start.13 = (f32[128,128]{1,0:T(8,128)}, f32[128,128]{1,0:T(8,128)S(1)}, u32[]{:S(2)}) copy-start(f32[128,128]{1,0:T(8,128)S(1)} %collective-permute-done.14.first_ref) | copy-start | bytes 196612
  166.3 15.3 %all-to-all-start.4 = ((f32[16,32,128]{2,1,0:T(8,128)}), f32[16,32,128]{2,1,0:T(8,128)S(1)}, u32[]{:S(2)}, u32[]{:S(2)}) async-start(f32[16,32,128]{2,1,0:T(8,128)} %tile.5), calls=%async_computation.4 | async-start | bytes 524288 | tf_op jit(solution)/shard_map/all_to_all | solution.py:329
  171.6 7.9 %collective-permute-start.15 = (f32[128,128]{1,0:T(8,128)S(1)}, f32[128,128]{1,0:T(8,128)S(1)}, u32[]{:S(2)}, u32[]{:S(2)}) collective-permute-start(f32[128,128]{1,0:T(8,128)S(1)} %pad_maximum_fusion.2), channel_id=1, source_target_pairs={{0,2},{1,3},{2,0},{3,1},{4,6},{5,7},{6,4},{7,5},{8,10},{9,11},{10,... | collective-permute-start | bytes 196616 | tf_op jit(solution)/shard_map/ppermute | solution.py:302
  179.4 0.6 copy-start.14

commit v3 on v2

--- a/solution.py
+++ b/solution.py
@@ -71,12 +71,11 @@
         )
         for q in range(NY):
             for k in range(8):
-                out_ref[q, SLOT * k:SLOT * k + SHARD, 128 * t:128 * t + 128] = got[
+                part, begin, cols = k // 4 * NY + q, SLOT * (k % 4), slice(128 * t, 128 * t + 128)
+                out_ref[part, begin:begin + SHARD, cols] = got[
                     SHARD * k:SHARD * (k + 1), 128 * q:128 * q + 128
                 ]
-                out_ref[q, SLOT * k + SHARD:SLOT * (k + 1), 128 * t:128 * t + 128] = jnp.zeros(
-                    (SLOT - SHARD, 128), f32
-                )
+                out_ref[part, begin + SHARD:begin + SLOT, cols] = jnp.zeros((SLOT - SHARD, 128), f32)
         stores[t].start()
     for store in stores:
         store.wait()
@@ -86,12 +85,12 @@
     anywhere = pl.BlockSpec(memory_space=pltpu.HBM)
     return pl.pallas_call(
         sort_columns,
-        out_shape=jax.ShapeDtypeStruct((NY, PAD, DEPTH), f32),
+        out_shape=jax.ShapeDtypeStruct((2 * NY, HALF, DEPTH), f32),
         in_specs=[anywhere],
         out_specs=anywhere,
         scratch_shapes=[
             pltpu.VMEM((4, ROWS, 640), f32),
-            pltpu.VMEM((NY, PAD, DEPTH), f32),
+            pltpu.VMEM((2 * NY, HALF, DEPTH), f32),
             pltpu.SemaphoreType.DMA((4,)),
             pltpu.SemaphoreType.DMA((4,)),
         ],
@@ -102,108 +101,83 @@
     )(s)
 
 
-PIECES = ((-4, 0, 4), (-5, -1, 3), (-3, 1, 5), (8,), (-6, -2), (2, 6), (7,), (9,))
+PIECES = ((-4, 0, 4), (-5, -1, 3), (-3, 1, 5), (8,), (-6, -2, 7), (2, 6, 9))
 N_PIECES = len(PIECES)
 
 
-def image_rows(half, yh_ref, yl_ref, s_ref, out_ref, sh_ref, sl_ref, added_ref=None):
-    rows = pl.ds(pl.multiple_of(HALF * half, HALF), HALF)
-    sh, sl = split2(jnp.concatenate([s_ref[k, rows, :] for k in range(NY)], axis=0))
-    sh_ref[...] = sh
-    sl_ref[...] = sl
-
-    @pl.loop(0, WIDE // 256)
-    def _(j):
-        cols = pl.ds(pl.multiple_of(256 * j, 256), 256)
-        u = dot3(sh_ref[...], sl_ref[...], yh_ref[:, cols], yl_ref[:, cols])
-        for source in range(NY):
-            for k in range(NY):
-                begin = HALF * source + SLOT * k
-                for g in range(2):
-                    part = u[begin:begin + SLOT, OWN * g:OWN * (g + 1)]
-                    at = (2 * j + g, k, slice(SLOT * source, SLOT * (source + 1)))
-                    out_ref[at] = part if added_ref is None else part + added_ref[at]
+STEPS = (0, 2, 1, 3)
 
 
 def panel_kernel(where_ref, *refs):
-    pieces, (pinv_ref, yh_ref, yl_ref, fac_ref) = refs[:N_PIECES], refs[N_PIECES:]
-    z = where_ref[0]
+    pieces, (pinv_ref, y_ref, *own_refs, fac_ref) = refs[:N_PIECES], refs[N_PIECES:]
+    z, core, x = where_ref[0], where_ref[1], where_ref[2]
     for ref, offsets in zip(pieces, PIECES):
         for k, offset in enumerate(offsets):
-            slot = lax.rem(z + (1 - 2 * where_ref[1]) * offset + NZ, NZ)
+            slot = lax.rem(z + (1 - 2 * core) * offset + NZ, NZ)
             fac_ref[pl.ds(pl.multiple_of(slot * SLOT, SLOT), SLOT), :] = ref[SLOT * k:SLOT * (k + 1), :]
     for child in range(2):
         fh, fl = split2(fac_ref[:, C * child:C * (child + 1)])
         for j in range(2):
             ph, plo = split2(pinv_ref[child, :, 256 * j:256 * (j + 1)])
-            yh, yl = split2(dot3(fh, fl, ph, plo))
             begin = C * child + 256 * j
-            yh_ref[:, begin:begin + 256] = yh
-            yl_ref[:, begin:begin + 256] = yl
+            y_ref[:, begin:begin + 256] = dot3(fh, fl, ph, plo)
+    rows = pl.ds(pl.multiple_of(lax.rem(z, 2) * PAD, PAD), PAD)
+    for step, out_ref in zip(STEPS, own_refs):
+        child = lax.rem(x + step, 4) // 2
+        out_ref[...] = y_ref[rows, pl.ds(pl.multiple_of(child * C, C), C)]
 
 
 def panel_rows(where, pieces, pinv):
     vmem = pl.BlockSpec(memory_space=pltpu.VMEM)
-    split = jax.ShapeDtypeStruct((DEPTH, WIDE), bf16)
+    own = jax.ShapeDtypeStruct((PAD, C), f32)
     return pl.pallas_call(
         panel_kernel,
-        out_shape=(split, split),
+        out_shape=(jax.ShapeDtypeStruct((DEPTH, WIDE), f32),) + (own,) * 4,
         in_specs=[pl.BlockSpec(memory_space=pltpu.SMEM)] + [vmem] * (N_PIECES + 1),
-        out_specs=(vmem, vmem),
+        out_specs=(vmem,) * 5,
         scratch_shapes=[pltpu.VMEM((DEPTH, WIDE), f32)],
-        compiler_params=pltpu.CompilerParams(vmem_limit_bytes=12 << 20),
-        cost_estimate=pl.CostEstimate(
-            flops=6 * 6 * DEPTH * WIDE * C, bytes_accessed=7 << 20, transcendentals=0
-        ),
-    )(where, *pieces, pinv)
-
-
-STEPS = (0, 2, 1, 3)
-
-
-def other_kernel(where_ref, yh_ref, yl_ref, s_ref, send_ref, *refs):
-    *own_refs, sh_ref, sl_ref = refs
-    rows = pl.ds(pl.multiple_of(lax.rem(where_ref[0], 2) * PAD, PAD), PAD)
-    for step, out_ref in zip(STEPS, own_refs):
-        child = lax.rem(where_ref[2] + step, 4) // 2
-        cols = pl.ds(pl.multiple_of(child * C, C), C)
-        out_ref[...] = yh_ref[rows, cols].astype(f32) + yl_ref[rows, cols].astype(f32)
-    image_rows(1 - where_ref[1], yh_ref, yl_ref, s_ref, send_ref, sh_ref, sl_ref)
-
-
-def other_image(where, yh, yl, s_parts):
-    vmem = pl.BlockSpec(memory_space=pltpu.VMEM)
-    own = jax.ShapeDtypeStruct((PAD, C), f32)
-    return pl.pallas_call(
-        other_kernel,
-        out_shape=(jax.ShapeDtypeStruct((NG, NY, HALF, OWN), f32),) + (own,) * 4,
-        in_specs=[pl.BlockSpec(memory_space=pltpu.SMEM)] + [vmem] * 3,
-        out_specs=(vmem,) * 5,
-        scratch_shapes=[pltpu.VMEM((NY * HALF, DEPTH), bf16), pltpu.VMEM((NY * HALF, DEPTH), bf16)],
         compiler_params=pltpu.CompilerParams(vmem_limit_bytes=14 << 20),
         cost_estimate=pl.CostEstimate(
-            flops=6 * DEPTH * WIDE * NY * HALF, bytes_accessed=8 << 20, transcendentals=0
-        ),
-    )(where, yh, yl, s_parts)
-
-
-def image_kernel(where_ref, yh_ref, yl_ref, s_ref, added_ref, out_ref, sh_ref, sl_ref):
-    image_rows(where_ref[1], yh_ref, yl_ref, s_ref, out_ref, sh_ref, sl_ref, added_ref)
-
-
-def own_image(where, yh, yl, s_parts, added):
+            flops=5 * 6 * DEPTH * WIDE * C, bytes_accessed=9 << 20, transcendentals=0
+        ),
+    )(where, *pieces, pinv)
+
+
+def image_kernel(where_ref, y_ref, other_ref, s_ref, out_ref, sh_ref, sl_ref):
+    core = where_ref[1]
+    for side in range(2):
+        first = NY * (core if side == 0 else 1 - core)
+        sh, sl = split2(jnp.concatenate([s_ref[first + k] for k in range(NY)], axis=0))
+        sh_ref[side] = sh
+        sl_ref[side] = sl
+
+    @pl.loop(0, WIDE // 256)
+    def _(j):
+        cols = pl.ds(pl.multiple_of(256 * j, 256), 256)
+        u = dot3(sh_ref[0], sl_ref[0], *split2(y_ref[:, cols]))
+        u = u + dot3(sh_ref[1], sl_ref[1], *split2(other_ref[:, cols]))
+        for source in range(NY):
+            for k in range(NY):
+                begin = HALF * source + SLOT * k
+                for g in range(2):
+                    out_ref[2 * j + g, k, SLOT * source:SLOT * (source + 1), :] = u[
+                        begin:begin + SLOT, OWN * g:OWN * (g + 1)
+                    ]
+
+
+def chip_image(where, y_rows, other, s_parts):
     vmem = pl.BlockSpec(memory_space=pltpu.VMEM)
     return pl.pallas_call(
         image_kernel,
         out_shape=jax.ShapeDtypeStruct((NG, NY, HALF, OWN), f32),
-        in_specs=[pl.BlockSpec(memory_space=pltpu.SMEM)] + [vmem] * 4,
+        in_specs=[pl.BlockSpec(memory_space=pltpu.SMEM)] + [vmem] * 3,
         out_specs=vmem,
-        scratch_shapes=[pltpu.VMEM((NY * HALF, DEPTH), bf16), pltpu.VMEM((NY * HALF, DEPTH), bf16)],
-        compiler_params=pltpu.CompilerParams(vmem_limit_bytes=14 << 20),
+        scratch_shapes=[pltpu.VMEM((2, NY * HALF, DEPTH), bf16), pltpu.VMEM((2, NY * HALF, DEPTH), bf16)],
+        compiler_params=pltpu.CompilerParams(vmem_limit_bytes=16 << 20),
         cost_estimate=pl.CostEstimate(
-            flops=6 * DEPTH * WIDE * NY * HALF, bytes_accessed=6 << 20, transcendentals=0
-        ),
-    )(where, yh, yl, s_parts, added)
+            flops=12 * DEPTH * WIDE * NY * HALF, bytes_accessed=8 << 20, transcendentals=0
+        ),
+    )(where, y_rows, other, s_parts)
 
 
 def finish_kernel(block_ref, got_ref, weight_ref, y_ref, pivot_ref, off_ref, term_ref):
@@ -306,7 +280,7 @@
     y = y_ref[0]
     block = 2 * SLOT
     own = off_ref[pl.ds(pl.multiple_of(block * y, block), block), :]
-    got = own, first_ref[:block], second_ref[:block], second_ref[block:]
+    got = own, second_ref[:block], first_ref[:block], second_ref[block:]
     for source in range(NY):
         at = source ^ y
         rows = jnp.where(at == 0, got[0], jnp.where(at == 1, got[1], jnp.where(at == 2, got[2], got[3])))
@@ -345,13 +319,13 @@
     below, above = shift_z(own, 4), shift_z(own, -4)
 
     s_sorted = spread_columns(s_parent)
-    s_parts = exchange(s_sorted, "y")
+    s_parts = exchange(s_sorted, ("c", "y"))
     near = jnp.concatenate([below, own, above], axis=0)
     low, high = shift_z(near, 1), shift_z(near, -1)
     far = shift_z(below, 4)
-    low2, high2 = shift_z(low[0:64], 1), shift_z(high[32:96], -1)
-    low_far, high_far = shift_z(far, 1), shift_z(far, -1)
-    pieces = (near, low, high, far, low2, high2, low_far, high_far)
+    low2 = shift_z(jnp.concatenate([low[0:64], far], axis=0), 1)
+    high2 = shift_z(jnp.concatenate([high[32:96], far], axis=0), -1)
+    pieces = (near, low, high, far, low2, high2)
 
     inverse = lax.dynamic_index_in_dim(panel_inverse, branch, 0, keepdims=False)
 
@@ -375,11 +349,11 @@
 
     x = lax.axis_index("x")
     where = jnp.stack([z, core, x]).astype(jnp.int32)
-    yh, yl = panel_rows(where, pieces, panel_inverse)
-    send, kept, *leaving = other_image(where, yh, yl, s_parts)
+    y_all, kept, *leaving = panel_rows(where, pieces, panel_inverse)
+    y_all, s_parts = lax.optimization_barrier((y_all, s_parts))
 
     parts = [from_root(a, step) for a, step in zip(leaving, STEPS[1:])]
-    image = own_image(where, yh, yl, s_parts, swap_core(send))
+    image = chip_image(where, y_all, swap_core(y_all), s_parts)
     image, *parts = lax.optimization_barrier((image, *parts))
     got = exchange(image.reshape(32 * HALF, OWN), PLANE)
     mine = jnp.where(x == z // 4, kept, parts[0] + parts[1] + parts[2])
@@ -390,9 +364,9 @@
     )
 
     rows = exchange(term, ("l", "y")).reshape(16, 32, OWN).sum(0)
-    first = swap_y(jnp.concatenate([block_for(off, y ^ 1), block_for(off, y ^ 3)], axis=0), 1)
+    first = swap_y(jnp.concatenate([block_for(off, y ^ 2), block_for(off, y ^ 3)], axis=0), 2)
     rows, first = lax.optimization_barrier((rows, first))
-    second = swap_y(jnp.concatenate([block_for(off, y ^ 2), first[2 * SLOT:]], axis=0), 2)
+    second = swap_y(jnp.concatenate([block_for(off, y ^ 1), first[2 * SLOT:]], axis=0), 1)
     rows = exchange(jnp.tile(rows, (4, 1)), "h").reshape(4, 32, OWN).sum(0)
     panel = exchange(jnp.tile(rows, (16, 1)), ("l", "y"))
     off = in_order(y.reshape(1).astype(jnp.int32), off, first, second)

time: 184 us -> 179 us (0.973)
  starting transfers between devices: 83.5 us -> 74.9 us
  waiting for transfers between devices: 38.1 us -> 44 us
    ppermute x9 -> x7, waiting for transfers between devices: 8.59 us -> 18.4 us  [shift_z(): return lax.ppermute(a, ('c',) + Z, pairs)]
    ppermute x9 -> x7, starting transfers between devices: 39.9 us -> 33.4 us  [shift_z(): return lax.ppermute(a, ('c',) + Z, pairs)]
    all_to_all x4, starting transfers between devices: 25.3 us -> 23 us  [exchange(): return lax.all_to_all(a, axes, 0, 0, tiled=True)]
    ppermute x3, waiting for transfers between devices: 4.47 us -> 2.14 us  [from_root(): return lax.ppermute(a, AXES, pairs)]
    all_to_all x4, waiting for transfers between devices: 21.2 us -> 19.1 us  [exchange(): return lax.all_to_all(a, axes, 0, 0, tiled=True)]
    pallas_call x4 -> x3, Pallas kernels: 12 us -> 10.7 us  [the longest x1 4.81 us: chip_image(): pl.pallas_call(image_kernel, out_shape=jax.ShapeDtypeStruct((NG, NY, HALF...]
  transfers between devices with their start and end apart: 20 -> 18, of which waited for: 9 -> 8; matrix products, arithmetic and copies ran while one was open for 6% -> 6% of each run, Pallas kernels for 6% -> 7%
where the time goes in v3:
time: 179 us; the launch traced here: 178 us
  starting transfers between devices  74.9 us (42%)
  waiting for transfers between devices  44 us (25%)
  blocking collectives  19 us (11%)
  local copies, waits for them, and re-layouts  16.5 us (9%)
  Pallas kernels  13.5 us (8%)
  other arithmetic  6.23 us (3%)
  matrix products  2.27 us (1%)
    ppermute x7, starting transfers between devices, shift_z(): return lax.ppermute(a, ('c',) + Z, pairs)  33.4 us
    all_to_all x4, starting transfers between devices, exchange(): return lax.all_to_all(a, axes, 0, 0, tiled=True)  23 us
    all_to_all x4, waiting for transfers between devices, exchange(): return lax.all_to_all(a, axes, 0, 0, tiled=True)  19.1 us
    all_to_all x1, blocking collectives, exchange(): return lax.all_to_all(a, axes, 0, 0, tiled=True)  19 us
    ppermute x7, waiting for transfers between devices, shift_z(): return lax.ppermute(a, ('c',) + Z, pairs)  18.4 us
    unnamed x39, local copies, waits for them, and re-layouts  11.7 us
    ppermute x3, starting transfers between devices, from_root(): return lax.ppermute(a, AXES, pairs)  7.6 us
    ppermute x2, starting transfers between devices, swap_y(): return lax.ppermute(a, 'y', [(i, i ^ bit) for i in range(NY)])  6 us
  transfers between devices with their start and end apart: 18, of which 8 were waited for; matrix products, arithmetic and copies ran while one was open for 6% of the time, Pallas kernels for 7%

profile of v3, /device:TPU:8, one launch (start us, length us, event | category | flops | bytes accessed | tf_op | source)
XLA Modules:
  0.0 177.7 jit_solution(13532633546049137123)
XLA Ops:
  1.7 0.9 mul.127
  2.7 12.7 %collective-permute-start.1 = (f32[32,1024]{1,0:T(8,128)S(1)}, f32[32,1024]{1,0:T(8,128)S(1)}, u32[]{:S(2)}, u32[]{:S(2)}) collective-permute-start(f32[32,1024]{1,0:T(8,128)S(1)} %pad.8), channel_id=1, source_target_pairs={{0,48},{4,52},{8,56},{12,60},{16,0},{20,4},{24,8},{28,12},{32,16},... | collective-permute-start | bytes 393224 | tf_op jit(solution)/shard_map/ppermute | solution.py:241
  15.4 1.9 %collective-permute-start = (f32[32,1024]{1,0:T(8,128)S(1)}, f32[32,1024]{1,0:T(8,128)S(1)}, u32[]{:S(2)}, u32[]{:S(2)}) collective-permute-start(f32[32,1024]{1,0:T(8,128)S(1)} %pad.8), channel_id=1, source_target_pairs={{0,16},{4,20},{8,24},{12,28},{16,32},{20,36},{24,40},{28,44},{32,4... | collective-permute-start | bytes 393224 | tf_op jit(solution)/shard_map/ppermute | solution.py:241
  17.3 1.5 copy-done.6
  18.8 3.2 %shard_map.87 = f32[8,128,512]{2,1,0:T(8,128)S(1)} custom-call(f32[240,1920]{1,0:T(8,128)S(1)} %copy-done.6), custom_call_target="tpu_custom_call" | custom-call | flops 1258291200 | bytes 3932160 | tf_op jit(solution)/shard_map/pallas_call | solution.py:86
  22.1 1.3 copy-done.1
  23.4 4.9 %all-to-all-start = ((f32[8,128,512]{2,1,0:T(8,128)}), f32[8,128,512]{2,1,0:T(8,128)S(1)}, u32[]{:S(2)}, u32[]{:S(2)}) async-start(f32[8,128,512]{2,1,0:T(8,128)} %copy-done.1), calls=%async_computation | async-start | bytes 4194304 | tf_op jit(solution)/shard_map/all_to_all | solution.py:303
  28.3 1.5 collective-permute-done
  29.8 5.2 %collective-permute-start.3 = (f32[96,1024]{1,0:T(8,128)S(1)}, f32[96,1024]{1,0:T(8,128)S(1)}, u32[]{:S(2)}, u32[]{:S(2)}) collective-permute-start(f32[96,1024]{1,0:T(8,128)S(1)} %pad_maximum_fusion.2.refs_0_), channel_id=1, source_target_pairs={{0,60},{4,0},{8,4},{12,8},{16,12},{20,16},{24,20},{28,24},{32,28},... | collective-permute-start | bytes 1179656 | tf_op jit(solution)/shard_map/ppermute | solution.py:241
  35.0 1.9 %collective-permute-start.2 = (f32[96,1024]{1,0:T(8,128)S(1)}, f32[96,1024]{1,0:T(8,128)S(1)}, u32[]{:S(2)}, u32[]{:S(2)}) collective-permute-start(f32[96,1024]{1,0:T(8,128)S(1)} %pad_maximum_fusion.2.refs_0_), channel_id=1, source_target_pairs={{0,4},{4,8},{8,12},{12,16},{16,20},{20,24},{24,28},{28,32},{32,36}... | collective-permute-start | bytes 1179656 | tf_op jit(solution)/shard_map/ppermute | solution.py:241
  36.9 2.9 %collective-permute-start.4 = (f32[32,1024]{1,0:T(8,128)S(1)}, f32[32,1024]{1,0:T(8,128)S(1)}, u32[]{:S(2)}, u32[]{:S(2)}) collective-permute-start(f32[32,1024]{1,0:T(8,128)S(1)} %collective-permute-done), channel_id=1, source_target_pairs={{0,16},{4,20},{8,24},{12,28},{16,32},{20,36},{24,40},{28,44},{32,4... | collective-permute-start | bytes 393224 | tf_op jit(solution)/shard_map/ppermute | solution.py:241
  39.8 4.0 %collective-permute-done.3.refs_2_ = f32[96,1024]{1,0:T(8,128)S(1)} collective-permute-done((f32[96,1024]{1,0:T(8,128)S(1)}, f32[96,1024]{1,0:T(8,128)S(1)}, u32[]{:S(2)}, u32[]{:S(2)}) %collective-permute-start.3) | collective-permute-done | bytes 393248 | tf_op jit(solution)/shard_map/ppermute | solution.py:241
  43.9 6.2 %collective-permute-done.2.refs_1_ = f32[96,1024]{1,0:T(8,128)S(1)} collective-permute-done((f32[96,1024]{1,0:T(8,128)S(1)}, f32[96,1024]{1,0:T(8,128)S(1)}, u32[]{:S(2)}, u32[]{:S(2)}) %collective-permute-start.2) | collective-permute-done | bytes 393248 | tf_op jit(solution)/shard_map/ppermute | solution.py:241
  50.2 2.8 %collective-permute-start.5 = (f32[96,1024]{1,0:T(8,128)S(1)}, f32[96,1024]{1,0:T(8,128)S(1)}, u32[]{:S(2)}, u32[]{:S(2)}) collective-permute-start(f32[96,1024]{1,0:T(8,128)S(1)} %get-tuple-element.43), channel_id=1, source_target_pairs={{0,4},{4,8},{8,12},{12,16},{16,20},{20,24},{24,28},{28,32},{32,36}... | collective-permute-start | bytes 1179656 | tf_op jit(solution)/shard_map/ppermute | solution.py:241
  53.0 6.0 %collective-permute-start.6 = (f32[96,1024]{1,0:T(8,128)S(1)}, f32[96,1024]{1,0:T(8,128)S(1)}, u32[]{:S(2)}, u32[]{:S(2)}) collective-permute-start(f32[96,1024]{1,0:T(8,128)S(1)} %get-tuple-element.42), channel_id=1, source_target_pairs={{0,60},{4,0},{8,4},{12,8},{16,12},{20,16},{24,20},{28,24},{32,28},... | collective-permute-start | bytes 1179656 | tf_op jit(solution)/shard_map/ppermute | solution.py:241
  59.1 6.7 %collective-permute-done.5.refs_4_ = f32[96,1024]{1,0:T(8,128)S(1)} collective-permute-done((f32[96,1024]{1,0:T(8,128)S(1)}, f32[96,1024]{1,0:T(8,128)S(1)}, u32[]{:S(2)}, u32[]{:S(2)}) %collective-permute-start.5) | collective-permute-done | bytes 393248 | tf_op jit(solution)/shard_map/ppermute | solution.py:241
  65.8 2.6 %shard_map.86 = (f32[512,1024]{1,0:T(8,128)S(1)}, f32[256,512]{1,0:T(8,128)S(1)}, f32[256,512]{1,0:T(8,128)S(1)}, f32[256,512]{1,0:T(8,128)S(1)}, f32[256,512]{1,0:T(8,128)S(1)}) custom-call(s32[3]{0:T(128)S(1)} %pad_add_fusion.where_ref, f32[96,1024]{1,0:T(8,128)S(1)} %pad_maximum_fusion.2.refs_0_, f32[96,1024]{1,0:T(8,128)S(1)} %collective-permute-done.2.refs_1_, ...), custom_call_target="tpu_custom_call" | custom-call | flops 8053063680 | bytes 9437184 | tf_op jit(solution)/shard_map/pallas_call | solution.py:133
  68.4 1.3 copy-done.4
  69.7 0.8 copy-done.7
  70.6 0.8 copy-done.8
  71.4 3.0 %collective-permute-start.7 = (f32[512,1024]{1,0:T(8,128)}, f32[512,1024]{1,0:T(8,128)S(1)}, u32[]{:S(2)}, u32[]{:S(2)}) collective-permute-start(f32[512,1024]{1,0:T(8,128)} %copy-done.4), channel_id=1, source_target_pairs={{0,64},{64,0},{1,65},{65,1},{2,66},{66,2},{3,67},{67,3},{4,68},{68... | collective-permute-start | bytes 6291464 | tf_op jit(solution)/shard_map/ppermute | solution.py:245
  74.3 5.0 %collective-permute-start.8 = (f32[256,512]{1,0:T(8,128)}, f32[256,512]{1,0:T(8,128)S(1)}, u32[]{:S(2)}, u32[]{:S(2)}) collective-permute-start(f32[256,512]{1,0:T(8,128)} %copy-done.8), channel_id=1, source_target_pairs={{0,256},{1,257},{2,258},{3,259},{4,260},{5,261},{6,262},{7,263},{7... | collective-permute-start | bytes 1572872 | tf_op jit(solution)/shard_map/ppermute | solution.py:268
  79.3 1.3 collective-permute-start.9
  80.6 1.3 collective-permute-start.10
  82.0 1.6 copy-done.5
  83.6 4.8 %shard_map.88 = f32[8,4,128,128]{3,2,1,0:T(8,128)S(1)} custom-call(s32[3]{0:T(128)S(1)} %pad_add_fusion.where_ref, f32[512,1024]{1,0:T(8,128)S(1)} %copy-done.5, f32[512,1024]{1,0:T(8,128)S(1)} %collective-permute-done.7.other_ref, f32[8,128,512]{2,1,0:T(8,128)S(1)} %all-to-all-done.s_ref), custom_call_target="tpu_custom_call" | custom-call | flops 3221225472 | bytes 8388608 | tf_op jit(solution)/shard_map/pallas_call | solution.py:170
  88.4 1.3 copy-done
  89.8 2.1 %collective-permute-done.9 = f32[256,512]{1,0:T(8,128)S(1)} collective-permute-done((f32[256,512]{1,0:T(8,128)}, f32[256,512]{1,0:T(8,128)S(1)}, u32[]{:S(2)}, u32[]{:S(2)}) %collective-permute-start.9) | collective-permute-done | bytes 524320 | tf_op jit(solution)/shard_map/ppermute | solution.py:268
  91.9 0.8 copy-done.11
  92.7 0.8 copy-done.12
  93.5 6.9 %all-to-all-start.1 = ((f32[32,128,128]{2,1,0:T(8,128)}), f32[32,128,128]{2,1,0:T(8,128)S(1)}, u32[]{:S(2)}, u32[]{:S(2)}) async-start(f32[32,128,128]{2,1,0:T(8,128)} %bitcast.31), calls=%async_computation.1 | async-start | bytes 4194304 | tf_op jit(solution)/shard_map/all_to_all | solution.py:303
  100.5 0.8 convert_reduce_fusion
  103.0 1.5 constant_dynamic-slice_fusion.1
  104.5 1.4 add_select_fusion
  105.9 2.0 %collective-permute-start.11 = (f32[256,512]{1,0:T(8,128)S(1)}, f32[256,512]{1,0:T(8,128)S(1)}, u32[]{:S(2)}, u32[]{:S(2)}) collective-permute-start(f32[256,512]{1,0:T(8,128)S(1)} %add_select_fusion), channel_id=1, source_target_pairs={{0,64},{1,65},{2,66},{3,67},{4,68},{5,69},{6,70},{7,71},{72,8},{73... | collective-permute-start | bytes 1572872 | tf_op jit(solution)/shard_map/ppermute | solution.py:259
  107.9 0.8 fusion.22
  108.7 2.0 %divide_select_fusion = (f32[512]{0:T(512)S(1)}, f32[512]{0:T(512)S(1)}, f32[512]{0:T(512)S(1)}) fusion(pred[512]{0:T(512)(128)(4,1)S(1)} %get-tuple-element.32, f32[512]{0:T(512)S(1)} %bitcast.41, pred[512]{0:T(512)(128)(4,1)S(1)} %get-tuple-element.33, f32[512]{0:T(512)S(1)} %bitcast.39, f32[511]{0:T(512)S(1)} %bitcast.36, f32[1]{0:T(128)} %bitcast.16, ...), kind=kLoop, calls=%fused_computation.42 | loop fusion | flops 9216 | bytes 19968 | tf_op jit(solution)/shard_map/jit(_where)/select_n | solution.py:223
  110.7 2.3 %convolution_select_fusion.pivot_ref = f32[32,128]{1,0:T(8,128)S(1)} fusion(f32[1,1,128]{2,1,0:T(1,128)S(1)} %get-tuple-element.36, f32[1,511,128]{2,1,0:T(8,128)S(1)} %get-tuple-element.38, f32[1,511,128]{2,1,0:T(8,128)S(1)} %get-tuple-element.37, f32[1,1,128]{2,1,0:T(1,128)S(1)} %get-tuple-element.35, f32[2,512,512]{2,1,0:T(8,128)} %refs_6_.1, ...), kind=kOutput, calls=%fused_computation | convolution fusion | flops 25628672 | bytes 1073664 | tf_op jit(solution)/shard_map/dot_general | solution.py:338
  113.1 14.1 %all-to-all-done.1 = f32[32,128,128]{2,1,0:T(8,128)S(1)} async-done(((f32[32,128,128]{2,1,0:T(8,128)}), f32[32,128,128]{2,1,0:T(8,128)S(1)}, u32[]{:S(2)}, u32[]{:S(2)}) %all-to-all-start.1) | async-done | bytes 2097184 | tf_op jit(solution)/shard_map/all_to_all | solution.py:303
  127.2 1.2 shard_map.89
  128.4 5.1 %all-to-all-start.2 = ((f32[16,32,128]{2,1,0:T(8,128)}), f32[16,32,128]{2,1,0:T(8,128)S(1)}, u32[]{:S(2)}, u32[]{:S(2)}) async-start(f32[16,32,128]{2,1,0:T(8,128)} %bitcast.20), calls=%async_computation.2 | async-start | bytes 524288 | tf_op jit(solution)/shard_map/all_to_all | solution.py:303
  133.5 4.0 %collective-permute-start.12 = (f32[128,128]{1,0:T(8,128)S(1)}, f32[128,128]{1,0:T(8,128)S(1)}, u32[]{:S(2)}, u32[]{:S(2)}) collective-permute-start(f32[128,128]{1,0:T(8,128)S(1)} %pad_maximum_fusion.3), channel_id=1, source_target_pairs={{0,2},{1,3},{2,0},{3,1},{4,6},{5,7},{6,4},{7,5},{8,10},{9,11},{10,... | collective-permute-start | bytes 196616 | tf_op jit(solution)/shard_map/ppermute | solution.py:276
  137.5 5.0 %all-to-all-done.2 = f32[16,32,128]{2,1,0:T(8,128)S(1)} async-done(((f32[16,32,128]{2,1,0:T(8,128)}), f32[16,32,128]{2,1,0:T(8,128)S(1)}, u32[]{:S(2)}, u32[]{:S(2)}) %all-to-all-start.2) | async-done | bytes 262176 | tf_op jit(solution)/shard_map/all_to_all | solution.py:303
  142.5 19.0 %all_to_all.38 = f32[4,32,128]{2,1,0:T(8,128)S(1)} all-to-all(f32[4,32,128]{2,1,0:T(8,128)S(1)} %tile.4), channel_id=1, replica_groups=mesh['x'=4,'c'=2,'h'=4,'l'=4,'y'=4] {'h'}, dimensions={0} | all-to-all | bytes 131072 | tf_op jit(solution)/shard_map/all_to_all | solution.py:303
  162.3 6.0 %all-to-all-start.4 = ((f32[16,32,128]{2,1,0:T(8,128)}), f32[16,32,128]{2,1,0:T(8,128)S(1)}, u32[]{:S(2)}, u32[]{:S(2)}) async-start(f32[16,32,128]{2,1,0:T(8,128)} %tile.5), calls=%async_computation.4 | async-start | bytes 524288 | tf_op jit(solution)/shard_map/all_to_all | solution.py:303
  168.4 2.0 %collective-permute-start.13 = (f32[128,128]{1,0:T(8,128)S(1)}, f32[128,128]{1,0:T(8,128)S(1)}, u32[]{:S(2)}, u32[]{:S(2)}) collective-permute-start(f32[128,128]{1,0:T(8,128)S(1)} %pad_maximum_fusion.4), channel_id=1, source_target_pairs={{0,1},{1,0},{2,3},{3,2},{4,5},{5,4},{6,7},{7,6},{8,9},{9,8},{10,11... | collective-permute-start | bytes 196616 | tf_op jit(solution)/shard_map/ppermute | solution.py:276
  170.4 4.3 %collective-permute-done.13.second_ref = f32[128,128]{1,0:T(8,128)S(1)} collective-permute-done((f32[128,128]{1,0:T(8,128)S(1)}, f32[128,128]{1,0:T(8,128)S(1)}, u32[]{:S(2)}, u32[]{:S(2)}) %collective-permute-start.13) | collective-permute-done | bytes 65568 | tf_op jit(solution)/shard_map/ppermute | solution.py:276
  175.3 1.6 shard_map.90
  (68 shorter events, 5.1 us)
Async XLA Ops:
  2.7 25.7 %collective-permute-start.1 = (f32[32,1024]{1,0:T(8,128)S(1)}, f32[32,1024]{1,0:T(8,128)S(1)}, u32[]{:S(2)}, u32[]{:S(2)}) collective-permute-start(f32[32,1024]{1,0:T(8,128)S(1)} %pad.8), channel_id=1, source_target_pairs={{0,48},{4,52},{8,56},{12,60},{16,0},{20,4},{24,8},{28,12},{32,16},... | collective-permute-start | bytes 393224 | tf_op jit(solution)/shard_map/ppermute | solution.py:241
  15.4 14.4 %collective-permute-start = (f32[32,1024]{1,0:T(8,128)S(1)}, f32[32,1024]{1,0:T(8,128)S(1)}, u32[]{:S(2)}, u32[]{:S(2)}) collective-permute-start(f32[32,1024]{1,0:T(8,128)S(1)} %pad.8), channel_id=1, source_target_pairs={{0,16},{4,20},{8,24},{12,28},{16,32},{20,36},{24,40},{28,44},{32,4... | collective-permute-start | bytes 393224 | tf_op jit(solution)/shard_map/ppermute | solution.py:241
  17.3 1.5 copy-start.6
  22.1 1.3 copy-start.1
  23.4 48.0 %all-to-all-start = ((f32[8,128,512]{2,1,0:T(8,128)}), f32[8,128,512]{2,1,0:T(8,128)S(1)}, u32[]{:S(2)}, u32[]{:S(2)}) async-start(f32[8,128,512]{2,1,0:T(8,128)} %copy-done.1), calls=%async_computation | async-start | bytes 4194304 | tf_op jit(solution)/shard_map/all_to_all | solution.py:303
  28.3 37.4 %copy-start.2 = (f32[2,512,512]{2,1,0:T(8,128)S(1)}, f32[2,512,512]{2,1,0:T(8,128)}, u32[]{:S(2)}) copy-start(f32[2,512,512]{2,1,0:T(8,128)} %refs_6_.1) | copy-start | bytes 6291460
  29.8 14.0 %collective-permute-start.3 = (f32[96,1024]{1,0:T(8,128)S(1)}, f32[96,1024]{1,0:T(8,128)S(1)}, u32[]{:S(2)}, u32[]{:S(2)}) collective-permute-start(f32[96,1024]{1,0:T(8,128)S(1)} %pad_maximum_fusion.2.refs_0_), channel_id=1, source_target_pairs={{0,60},{4,0},{8,4},{12,8},{16,12},{20,16},{24,20},{28,24},{32,28},... | collective-permute-start | bytes 1179656 | tf_op jit(solution)/shard_map/ppermute | solution.py:241
  35.0 15.1 %collective-permute-start.2 = (f32[96,1024]{1,0:T(8,128)S(1)}, f32[96,1024]{1,0:T(8,128)S(1)}, u32[]{:S(2)}, u32[]{:S(2)}) collective-permute-start(f32[96,1024]{1,0:T(8,128)S(1)} %pad_maximum_fusion.2.refs_0_), channel_id=1, source_target_pairs={{0,4},{4,8},{8,12},{12,16},{16,20},{20,24},{24,28},{28,32},{32,36}... | collective-permute-start | bytes 1179656 | tf_op jit(solution)/shard_map/ppermute | solution.py:241
  36.9 13.2 %collective-permute-start.4 = (f32[32,1024]{1,0:T(8,128)S(1)}, f32[32,1024]{1,0:T(8,128)S(1)}, u32[]{:S(2)}, u32[]{:S(2)}) collective-permute-start(f32[32,1024]{1,0:T(8,128)S(1)} %collective-permute-done), channel_id=1, source_target_pairs={{0,16},{4,20},{8,24},{12,28},{16,32},{20,36},{24,40},{28,44},{32,4... | collective-permute-start | bytes 393224 | tf_op jit(solution)/shard_map/ppermute | solution.py:241
  50.2 15.5 %collective-permute-start.5 = (f32[96,1024]{1,0:T(8,128)S(1)}, f32[96,1024]{1,0:T(8,128)S(1)}, u32[]{:S(2)}, u32[]{:S(2)}) collective-permute-start(f32[96,1024]{1,0:T(8,128)S(1)} %get-tuple-element.43), channel_id=1, source_target_pairs={{0,4},{4,8},{8,12},{12,16},{16,20},{20,24},{24,28},{28,32},{32,36}... | collective-permute-start | bytes 1179656 | tf_op jit(solution)/shard_map/ppermute | solution.py:241
  53.0 12.8 %collective-permute-start.6 = (f32[96,1024]{1,0:T(8,128)S(1)}, f32[96,1024]{1,0:T(8,128)S(1)}, u32[]{:S(2)}, u32[]{:S(2)}) collective-permute-start(f32[96,1024]{1,0:T(8,128)S(1)} %get-tuple-element.42), channel_id=1, source_target_pairs={{0,60},{4,0},{8,4},{12,8},{16,12},{20,16},{24,20},{28,24},{32,28},... | collective-permute-start | bytes 1179656 | tf_op jit(solution)/shard_map/ppermute | solution.py:241
  68.4 1.4 copy-start.4
  69.7 0.8 copy-start.7
  70.5 0.8 copy-start.8
  71.4 10.6 %collective-permute-start.7 = (f32[512,1024]{1,0:T(8,128)}, f32[512,1024]{1,0:T(8,128)S(1)}, u32[]{:S(2)}, u32[]{:S(2)}) collective-permute-start(f32[512,1024]{1,0:T(8,128)} %copy-done.4), channel_id=1, source_target_pairs={{0,64},{64,0},{1,65},{65,1},{2,66},{66,2},{3,67},{67,3},{4,68},{68... | collective-permute-start | bytes 6291464 | tf_op jit(solution)/shard_map/ppermute | solution.py:245
  74.3 15.4 %collective-permute-start.8 = (f32[256,512]{1,0:T(8,128)}, f32[256,512]{1,0:T(8,128)S(1)}, u32[]{:S(2)}, u32[]{:S(2)}) collective-permute-start(f32[256,512]{1,0:T(8,128)} %copy-done.8), channel_id=1, source_target_pairs={{0,256},{1,257},{2,258},{3,259},{4,260},{5,261},{6,262},{7,263},{7... | collective-permute-start | bytes 1572872 | tf_op jit(solution)/shard_map/ppermute | solution.py:268
  79.3 12.6 %collective-permute-start.9 = (f32[256,512]{1,0:T(8,128)}, f32[256,512]{1,0:T(8,128)S(1)}, u32[]{:S(2)}, u32[]{:S(2)}) collective-permute-start(f32[256,512]{1,0:T(8,128)} %copy-done.7), channel_id=1, source_target_pairs={{0,128},{1,129},{2,130},{3,131},{4,132},{5,133},{6,134},{7,135},{7... | collective-permute-start | bytes 1572872 | tf_op jit(solution)/shard_map/ppermute | solution.py:268
  80.6 11.3 %collective-permute-start.10 = (f32[256,512]{1,0:T(8,128)S(1)}, f32[256,512]{1,0:T(8,128)S(1)}, u32[]{:S(2)}, u32[]{:S(2)}) collective-permute-start(f32[256,512]{1,0:T(8,128)S(1)} %get-tuple-element.22), channel_id=1, source_target_pairs={{0,384},{1,385},{2,386},{3,387},{4,388},{5,389},{6,390},{7,391},{7... | collective-permute-start | bytes 1572872 | tf_op jit(solution)/shard_map/ppermute | solution.py:268
  82.0 1.6 copy-start.5
  88.4 1.4 copy-start
  89.7 2.1 %copy-start.9 = (f32[256,512]{1,0:T(8,128)}, f32[256,512]{1,0:T(8,128)S(1)}, u32[]{:S(2)}) copy-start(f32[256,512]{1,0:T(8,128)S(1)} %collective-permute-done.8) | copy-start | bytes 1572868
  91.9 0.8 copy-start.11
  92.7 0.8 copy-start.12
  93.5 8.2 %copy-start.16 = (f32[2,512]{1,0:T(2,128)S(1)}, f32[2,512]{1,0:T(2,128)}, u32[]{:S(2)}) copy-start(f32[2,512]{1,0:T(2,128)} %param.12) | copy-start | bytes 12292
  93.5 8.8 %copy-start.15 = (f32[2,512]{1,0:T(2,128)S(1)}, f32[2,512]{1,0:T(2,128)}, u32[]{:S(2)}) copy-start(f32[2,512]{1,0:T(2,128)} %param.11) | copy-start | bytes 12292
  93.5 9.4 %copy-start.17 = (s32[2,512]{1,0:T(2,128)S(1)}, s32[2,512]{1,0:T(2,128)}, u32[]{:S(2)}) copy-start(s32[2,512]{1,0:T(2,128)} %param.10) | copy-start | bytes 12292
  93.5 11.0 %copy-start.10 = (f32[256,512]{1,0:T(8,128)S(1)}, f32[256,512]{1,0:T(8,128)}, u32[]{:S(2)}) copy-start(f32[256,512]{1,0:T(8,128)} %copy-done.9) | copy-start | bytes 1572868
  93.5 33.7 %all-to-all-start.1 = ((f32[32,128,128]{2,1,0:T(8,128)}), f32[32,128,128]{2,1,0:T(8,128)S(1)}, u32[]{:S(2)}, u32[]{:S(2)}) async-start(f32[32,128,128]{2,1,0:T(8,128)} %bitcast.31), calls=%async_computation.1 | async-start | bytes 4194304 | tf_op jit(solution)/shard_map/all_to_all | solution.py:303
  105.9 7.1 %collective-permute-start.11 = (f32[256,512]{1,0:T(8,128)S(1)}, f32[256,512]{1,0:T(8,128)S(1)}, u32[]{:S(2)}, u32[]{:S(2)}) collective-permute-start(f32[256,512]{1,0:T(8,128)S(1)} %add_select_fusion), channel_id=1, source_target_pairs={{0,64},{1,65},{2,66},{3,67},{4,68},{5,69},{6,70},{7,71},{72,8},{73... | collective-permute-start | bytes 1572872 | tf_op jit(solution)/shard_map/ppermute | solution.py:259
  128.4 46.3 %copy-start.3 = (f32[256,128]{1,0:T(8,128)}, f32[256,128]{1,0:T(8,128)S(1)}, u32[]{:S(2)}) copy-start(f32[256,128]{1,0:T(8,128)S(1)} %get-tuple-element.28.off_ref) | copy-start | bytes 393220
  128.4 14.1 %all-to-all-start.2 = ((f32[16,32,128]{2,1,0:T(8,128)}), f32[16,32,128]{2,1,0:T(8,128)S(1)}, u32[]{:S(2)}, u32[]{:S(2)}) async-start(f32[16,32,128]{2,1,0:T(8,128)} %bitcast.20), calls=%async_computation.2 | async-start | bytes 524288 | tf_op jit(solution)/shard_map/all_to_all | solution.py:303
  133.5 9.0 %collective-permute-start.12 = (f32[128,128]{1,0:T(8,128)S(1)}, f32[128,128]{1,0:T(8,128)S(1)}, u32[]{:S(2)}, u32[]{:S(2)}) collective-permute-start(f32[128,128]{1,0:T(8,128)S(1)} %pad_maximum_fusion.3), channel_id=1, source_target_pairs={{0,2},{1,3},{2,0},{3,1},{4,6},{5,7},{6,4},{7,5},{8,10},{9,11},{10,... | collective-permute-start | bytes 196616 | tf_op jit(solution)/shard_map/ppermute | solution.py:276
  142.5 32.2 %copy-start.13 = (f32[128,128]{1,0:T(8,128)}, f32[128,128]{1,0:T(8,128)S(1)}, u32[]{:S(2)}) copy-start(f32[128,128]{1,0:T(8,128)S(1)} %collective-permute-done.12.first_ref) | copy-start | bytes 196612
  162.3 14.7 %all-to-all-start.4 = ((f32[16,32,128]{2,1,0:T(8,128)}), f32[16,32,128]{2,1,0:T(8,128)S(1)}, u32[]{:S(2)}, u32[]{:S(2)}) async-start(f32[16,32,128]{2,1,0:T(8,128)} %tile.5), calls=%async_computation.4 | async-start | bytes 524288 | tf_op jit(solution)/shard_map/all_to_all | solution.py:303
  168.4 6.3 %collective-permute-start.13 = (f32[128,128]{1,0:T(8,128)S(1)}, f32[128,128]{1,0:T(8,128)S(1)}, u32[]{:S(2)}, u32[]{:S(2)}) collective-permute-start(f32[128,128]{1,0:T(8,128)S(1)} %pad_maximum_fusion.4), channel_id=1, source_target_pairs={{0,1},{1,0},{2,3},{3,2},{4,5},{5,4},{6,7},{7,6},{8,9},{9,8},{10,11... | collective-permute-start | bytes 196616 | tf_op jit(solution)/shard_map/ppermute | solution.py:276
  174.7 0.6 copy-start.14

commit v4 on v3

--- a/solution.py
+++ b/solution.py
@@ -296,6 +296,7 @@
         out_shape=jax.ShapeDtypeStruct((ROWS, OWN), f32),
         in_specs=[pl.BlockSpec(memory_space=pltpu.SMEM)] + [vmem] * 3,
         out_specs=vmem,
+        compiler_params=pltpu.CompilerParams(vmem_limit_bytes=2 << 20),
     )(y, off, first, second)
 
 

time: 179 us -> 179 us (level)
    unnamed x39 -> x33, local copies, waits for them, and re-layouts: 11.7 us -> 11.1 us
  transfers between devices with their start and end apart: 18 -> 18, of which waited for: 8 -> 9; matrix products, arithmetic and copies ran while one was open for 6% -> 6% of each run, Pallas kernels for 7% -> 6%
where the time goes in v4:
time: 179 us; the launch traced here: 178 us
  starting transfers between devices  74.9 us (42%)
  waiting for transfers between devices  45.7 us (26%)
  blocking collectives  19 us (11%)
  local copies, waits for them, and re-layouts  15.9 us (9%)
  Pallas kernels  12.5 us (7%)
  other arithmetic  6.15 us (3%)
  matrix products  2.27 us (1%)
    ppermute x7, starting transfers between devices, shift_z(): return lax.ppermute(a, ('c',) + Z, pairs)  33.4 us
    all_to_all x4, starting transfers between devices, exchange(): return lax.all_to_all(a, axes, 0, 0, tiled=True)  22.9 us
    all_to_all x4, waiting for transfers between devices, exchange(): return lax.all_to_all(a, axes, 0, 0, tiled=True)  20.8 us
    all_to_all x1, blocking collectives, exchange(): return lax.all_to_all(a, axes, 0, 0, tiled=True)  19 us
    ppermute x7, waiting for transfers between devices, shift_z(): return lax.ppermute(a, ('c',) + Z, pairs)  18.4 us
    unnamed x33, local copies, waits for them, and re-layouts  11.1 us
    ppermute x3, starting transfers between devices, from_root(): return lax.ppermute(a, AXES, pairs)  7.61 us
    ppermute x2, starting transfers between devices, swap_y(): return lax.ppermute(a, 'y', [(i, i ^ bit) for i in range(NY)])  6 us
  transfers between devices with their start and end apart: 18, of which 9 were waited for; matrix products, arithmetic and copies ran while one was open for 6% of the time, Pallas kernels for 6%

profile of v4, /device:TPU:8, one launch (start us, length us, event | category | flops | bytes accessed | tf_op | source)
XLA Modules:
  0.0 177.7 jit_solution(13226033400218692134)
XLA Ops:
  1.7 0.9 mul.127
  2.7 12.7 %collective-permute-start.1 = (f32[32,1024]{1,0:T(8,128)S(1)}, f32[32,1024]{1,0:T(8,128)S(1)}, u32[]{:S(2)}, u32[]{:S(2)}) collective-permute-start(f32[32,1024]{1,0:T(8,128)S(1)} %pad.8), channel_id=1, source_target_pairs={{0,48},{4,52},{8,56},{12,60},{16,0},{20,4},{24,8},{28,12},{32,16},... | collective-permute-start | bytes 393224 | tf_op jit(solution)/shard_map/ppermute | solution.py:241
  15.4 1.9 %collective-permute-start = (f32[32,1024]{1,0:T(8,128)S(1)}, f32[32,1024]{1,0:T(8,128)S(1)}, u32[]{:S(2)}, u32[]{:S(2)}) collective-permute-start(f32[32,1024]{1,0:T(8,128)S(1)} %pad.8), channel_id=1, source_target_pairs={{0,16},{4,20},{8,24},{12,28},{16,32},{20,36},{24,40},{28,44},{32,4... | collective-permute-start | bytes 393224 | tf_op jit(solution)/shard_map/ppermute | solution.py:241
  17.3 1.5 copy-done.5
  18.8 3.2 %shard_map.87 = f32[8,128,512]{2,1,0:T(8,128)S(1)} custom-call(f32[240,1920]{1,0:T(8,128)S(1)} %copy-done.5), custom_call_target="tpu_custom_call" | custom-call | flops 1258291200 | bytes 3932160 | tf_op jit(solution)/shard_map/pallas_call | solution.py:86
  22.1 1.3 copy-done.1
  23.4 4.9 %all-to-all-start = ((f32[8,128,512]{2,1,0:T(8,128)}), f32[8,128,512]{2,1,0:T(8,128)S(1)}, u32[]{:S(2)}, u32[]{:S(2)}) async-start(f32[8,128,512]{2,1,0:T(8,128)} %copy-done.1), calls=%async_computation | async-start | bytes 4194304 | tf_op jit(solution)/shard_map/all_to_all | solution.py:304
  28.3 1.5 collective-permute-done
  29.8 5.2 %collective-permute-start.3 = (f32[96,1024]{1,0:T(8,128)S(1)}, f32[96,1024]{1,0:T(8,128)S(1)}, u32[]{:S(2)}, u32[]{:S(2)}) collective-permute-start(f32[96,1024]{1,0:T(8,128)S(1)} %pad_maximum_fusion.2.refs_0_), channel_id=1, source_target_pairs={{0,60},{4,0},{8,4},{12,8},{16,12},{20,16},{24,20},{28,24},{32,28},... | collective-permute-start | bytes 1179656 | tf_op jit(solution)/shard_map/ppermute | solution.py:241
  35.0 1.9 %collective-permute-start.2 = (f32[96,1024]{1,0:T(8,128)S(1)}, f32[96,1024]{1,0:T(8,128)S(1)}, u32[]{:S(2)}, u32[]{:S(2)}) collective-permute-start(f32[96,1024]{1,0:T(8,128)S(1)} %pad_maximum_fusion.2.refs_0_), channel_id=1, source_target_pairs={{0,4},{4,8},{8,12},{12,16},{16,20},{20,24},{24,28},{28,32},{32,36}... | collective-permute-start | bytes 1179656 | tf_op jit(solution)/shard_map/ppermute | solution.py:241
  36.9 2.9 %collective-permute-start.4 = (f32[32,1024]{1,0:T(8,128)S(1)}, f32[32,1024]{1,0:T(8,128)S(1)}, u32[]{:S(2)}, u32[]{:S(2)}) collective-permute-start(f32[32,1024]{1,0:T(8,128)S(1)} %collective-permute-done), channel_id=1, source_target_pairs={{0,16},{4,20},{8,24},{12,28},{16,32},{20,36},{24,40},{28,44},{32,4... | collective-permute-start | bytes 393224 | tf_op jit(solution)/shard_map/ppermute | solution.py:241
  39.8 4.1 %collective-permute-done.3.refs_2_ = f32[96,1024]{1,0:T(8,128)S(1)} collective-permute-done((f32[96,1024]{1,0:T(8,128)S(1)}, f32[96,1024]{1,0:T(8,128)S(1)}, u32[]{:S(2)}, u32[]{:S(2)}) %collective-permute-start.3) | collective-permute-done | bytes 393248 | tf_op jit(solution)/shard_map/ppermute | solution.py:241
  43.9 6.1 %collective-permute-done.2.refs_1_ = f32[96,1024]{1,0:T(8,128)S(1)} collective-permute-done((f32[96,1024]{1,0:T(8,128)S(1)}, f32[96,1024]{1,0:T(8,128)S(1)}, u32[]{:S(2)}, u32[]{:S(2)}) %collective-permute-start.2) | collective-permute-done | bytes 393248 | tf_op jit(solution)/shard_map/ppermute | solution.py:241
  50.2 2.8 %collective-permute-start.5 = (f32[96,1024]{1,0:T(8,128)S(1)}, f32[96,1024]{1,0:T(8,128)S(1)}, u32[]{:S(2)}, u32[]{:S(2)}) collective-permute-start(f32[96,1024]{1,0:T(8,128)S(1)} %get-tuple-element.43), channel_id=1, source_target_pairs={{0,4},{4,8},{8,12},{12,16},{16,20},{20,24},{24,28},{28,32},{32,36}... | collective-permute-start | bytes 1179656 | tf_op jit(solution)/shard_map/ppermute | solution.py:241
  53.0 6.0 %collective-permute-start.6 = (f32[96,1024]{1,0:T(8,128)S(1)}, f32[96,1024]{1,0:T(8,128)S(1)}, u32[]{:S(2)}, u32[]{:S(2)}) collective-permute-start(f32[96,1024]{1,0:T(8,128)S(1)} %get-tuple-element.42), channel_id=1, source_target_pairs={{0,60},{4,0},{8,4},{12,8},{16,12},{20,16},{24,20},{28,24},{32,28},... | collective-permute-start | bytes 1179656 | tf_op jit(solution)/shard_map/ppermute | solution.py:241
  59.0 6.7 %collective-permute-done.5.refs_4_ = f32[96,1024]{1,0:T(8,128)S(1)} collective-permute-done((f32[96,1024]{1,0:T(8,128)S(1)}, f32[96,1024]{1,0:T(8,128)S(1)}, u32[]{:S(2)}, u32[]{:S(2)}) %collective-permute-start.5) | collective-permute-done | bytes 393248 | tf_op jit(solution)/shard_map/ppermute | solution.py:241
  65.7 2.6 %shard_map.86 = (f32[512,1024]{1,0:T(8,128)S(1)}, f32[256,512]{1,0:T(8,128)S(1)}, f32[256,512]{1,0:T(8,128)S(1)}, f32[256,512]{1,0:T(8,128)S(1)}, f32[256,512]{1,0:T(8,128)S(1)}) custom-call(s32[3]{0:T(128)S(1)} %pad_add_fusion.where_ref, f32[96,1024]{1,0:T(8,128)S(1)} %pad_maximum_fusion.2.refs_0_, f32[96,1024]{1,0:T(8,128)S(1)} %collective-permute-done.2.refs_1_, ...), custom_call_target="tpu_custom_call" | custom-call | flops 8053063680 | bytes 9437184 | tf_op jit(solution)/shard_map/pallas_call | solution.py:133
  68.4 1.3 copy-done.3
  69.7 0.8 copy-done.6
  70.5 0.8 copy-done.7
  71.4 3.0 %collective-permute-start.7 = (f32[512,1024]{1,0:T(8,128)}, f32[512,1024]{1,0:T(8,128)S(1)}, u32[]{:S(2)}, u32[]{:S(2)}) collective-permute-start(f32[512,1024]{1,0:T(8,128)} %copy-done.3), channel_id=1, source_target_pairs={{0,64},{64,0},{1,65},{65,1},{2,66},{66,2},{3,67},{67,3},{4,68},{68... | collective-permute-start | bytes 6291464 | tf_op jit(solution)/shard_map/ppermute | solution.py:245
  74.3 5.0 %collective-permute-start.8 = (f32[256,512]{1,0:T(8,128)}, f32[256,512]{1,0:T(8,128)S(1)}, u32[]{:S(2)}, u32[]{:S(2)}) collective-permute-start(f32[256,512]{1,0:T(8,128)} %copy-done.7), channel_id=1, source_target_pairs={{0,256},{1,257},{2,258},{3,259},{4,260},{5,261},{6,262},{7,263},{7... | collective-permute-start | bytes 1572872 | tf_op jit(solution)/shard_map/ppermute | solution.py:268
  79.3 1.3 collective-permute-start.9
  80.6 1.3 collective-permute-start.10
  82.0 1.6 copy-done.4
  83.6 4.8 %shard_map.88 = f32[8,4,128,128]{3,2,1,0:T(8,128)S(1)} custom-call(s32[3]{0:T(128)S(1)} %pad_add_fusion.where_ref, f32[512,1024]{1,0:T(8,128)S(1)} %copy-done.4, f32[512,1024]{1,0:T(8,128)S(1)} %collective-permute-done.7.other_ref, f32[8,128,512]{2,1,0:T(8,128)S(1)} %all-to-all-done.s_ref), custom_call_target="tpu_custom_call" | custom-call | flops 3221225472 | bytes 8388608 | tf_op jit(solution)/shard_map/pallas_call | solution.py:170
  88.4 1.3 copy-done
  89.8 2.1 %collective-permute-done.9 = f32[256,512]{1,0:T(8,128)S(1)} collective-permute-done((f32[256,512]{1,0:T(8,128)}, f32[256,512]{1,0:T(8,128)S(1)}, u32[]{:S(2)}, u32[]{:S(2)}) %collective-permute-start.9) | collective-permute-done | bytes 524320 | tf_op jit(solution)/shard_map/ppermute | solution.py:268
  91.9 0.8 copy-done.10
  92.7 0.8 copy-done.11
  93.5 6.9 %all-to-all-start.1 = ((f32[32,128,128]{2,1,0:T(8,128)}), f32[32,128,128]{2,1,0:T(8,128)S(1)}, u32[]{:S(2)}, u32[]{:S(2)}) async-start(f32[32,128,128]{2,1,0:T(8,128)} %bitcast.31), calls=%async_computation.1 | async-start | bytes 4194304 | tf_op jit(solution)/shard_map/all_to_all | solution.py:304
  100.5 0.8 convert_reduce_fusion
  103.0 1.5 constant_dynamic-slice_fusion.1
  104.5 1.4 add_select_fusion
  105.9 2.0 %collective-permute-start.11 = (f32[256,512]{1,0:T(8,128)S(1)}, f32[256,512]{1,0:T(8,128)S(1)}, u32[]{:S(2)}, u32[]{:S(2)}) collective-permute-start(f32[256,512]{1,0:T(8,128)S(1)} %add_select_fusion), channel_id=1, source_target_pairs={{0,64},{1,65},{2,66},{3,67},{4,68},{5,69},{6,70},{7,71},{72,8},{73... | collective-permute-start | bytes 1572872 | tf_op jit(solution)/shard_map/ppermute | solution.py:259
  107.9 0.8 fusion.22
  108.7 1.9 %divide_select_fusion = (f32[512]{0:T(512)S(1)}, f32[512]{0:T(512)S(1)}, f32[512]{0:T(512)S(1)}) fusion(pred[512]{0:T(512)(128)(4,1)S(1)} %get-tuple-element.32, f32[512]{0:T(512)S(1)} %bitcast.41, pred[512]{0:T(512)(128)(4,1)S(1)} %get-tuple-element.33, f32[512]{0:T(512)S(1)} %bitcast.39, f32[511]{0:T(512)S(1)} %bitcast.36, f32[1]{0:T(128)} %bitcast.16, ...), kind=kLoop, calls=%fused_computation.42 | loop fusion | flops 9216 | bytes 19968 | tf_op jit(solution)/shard_map/jit(_where)/select_n | solution.py:223
  110.6 2.3 %convolution_select_fusion.pivot_ref = f32[32,128]{1,0:T(8,128)S(1)} fusion(f32[1,1,128]{2,1,0:T(1,128)S(1)} %get-tuple-element.36, f32[1,511,128]{2,1,0:T(8,128)S(1)} %get-tuple-element.38, f32[1,511,128]{2,1,0:T(8,128)S(1)} %get-tuple-element.37, f32[1,1,128]{2,1,0:T(1,128)S(1)} %get-tuple-element.35, f32[2,512,512]{2,1,0:T(8,128)} %refs_6_.1, ...), kind=kOutput, calls=%fused_computation | convolution fusion | flops 25628672 | bytes 1073664 | tf_op jit(solution)/shard_map/dot_general | solution.py:339
  113.0 14.2 %all-to-all-done.1 = f32[32,128,128]{2,1,0:T(8,128)S(1)} async-done(((f32[32,128,128]{2,1,0:T(8,128)}), f32[32,128,128]{2,1,0:T(8,128)S(1)}, u32[]{:S(2)}, u32[]{:S(2)}) %all-to-all-start.1) | async-done | bytes 2097184 | tf_op jit(solution)/shard_map/all_to_all | solution.py:304
  127.2 1.2 shard_map.89
  128.4 5.1 %all-to-all-start.2 = ((f32[16,32,128]{2,1,0:T(8,128)}), f32[16,32,128]{2,1,0:T(8,128)S(1)}, u32[]{:S(2)}, u32[]{:S(2)}) async-start(f32[16,32,128]{2,1,0:T(8,128)} %bitcast.20), calls=%async_computation.2 | async-start | bytes 524288 | tf_op jit(solution)/shard_map/all_to_all | solution.py:304
  133.5 4.0 %collective-permute-start.12 = (f32[128,128]{1,0:T(8,128)S(1)}, f32[128,128]{1,0:T(8,128)S(1)}, u32[]{:S(2)}, u32[]{:S(2)}) collective-permute-start(f32[128,128]{1,0:T(8,128)S(1)} %pad_maximum_fusion.3), channel_id=1, source_target_pairs={{0,2},{1,3},{2,0},{3,1},{4,6},{5,7},{6,4},{7,5},{8,10},{9,11},{10,... | collective-permute-start | bytes 196616 | tf_op jit(solution)/shard_map/ppermute | solution.py:276
  137.5 5.0 %all-to-all-done.2 = f32[16,32,128]{2,1,0:T(8,128)S(1)} async-done(((f32[16,32,128]{2,1,0:T(8,128)}), f32[16,32,128]{2,1,0:T(8,128)S(1)}, u32[]{:S(2)}, u32[]{:S(2)}) %all-to-all-start.2) | async-done | bytes 262176 | tf_op jit(solution)/shard_map/all_to_all | solution.py:304
  142.5 19.0 %all_to_all.38 = f32[4,32,128]{2,1,0:T(8,128)S(1)} all-to-all(f32[4,32,128]{2,1,0:T(8,128)S(1)} %tile.4), channel_id=1, replica_groups=mesh['x'=4,'c'=2,'h'=4,'l'=4,'y'=4] {'h'}, dimensions={0} | all-to-all | bytes 131072 | tf_op jit(solution)/shard_map/all_to_all | solution.py:304
  162.3 6.0 %all-to-all-start.4 = ((f32[16,32,128]{2,1,0:T(8,128)}), f32[16,32,128]{2,1,0:T(8,128)S(1)}, u32[]{:S(2)}, u32[]{:S(2)}) async-start(f32[16,32,128]{2,1,0:T(8,128)} %tile.5), calls=%async_computation.4 | async-start | bytes 524288 | tf_op jit(solution)/shard_map/all_to_all | solution.py:304
  168.4 2.0 %collective-permute-start.13 = (f32[128,128]{1,0:T(8,128)S(1)}, f32[128,128]{1,0:T(8,128)S(1)}, u32[]{:S(2)}, u32[]{:S(2)}) collective-permute-start(f32[128,128]{1,0:T(8,128)S(1)} %pad_maximum_fusion.4), channel_id=1, source_target_pairs={{0,1},{1,0},{2,3},{3,2},{4,5},{5,4},{6,7},{7,6},{8,9},{9,8},{10,11... | collective-permute-start | bytes 196616 | tf_op jit(solution)/shard_map/ppermute | solution.py:276
  170.4 4.3 %collective-permute-done.13.second_ref = f32[128,128]{1,0:T(8,128)S(1)} collective-permute-done((f32[128,128]{1,0:T(8,128)S(1)}, f32[128,128]{1,0:T(8,128)S(1)}, u32[]{:S(2)}, u32[]{:S(2)}) %collective-permute-start.13) | collective-permute-done | bytes 65568 | tf_op jit(solution)/shard_map/ppermute | solution.py:276
  175.4 1.6 all-to-all-done.4
  (62 shorter events, 5.1 us)
Async XLA Ops:
  2.7 25.6 %collective-permute-start.1 = (f32[32,1024]{1,0:T(8,128)S(1)}, f32[32,1024]{1,0:T(8,128)S(1)}, u32[]{:S(2)}, u32[]{:S(2)}) collective-permute-start(f32[32,1024]{1,0:T(8,128)S(1)} %pad.8), channel_id=1, source_target_pairs={{0,48},{4,52},{8,56},{12,60},{16,0},{20,4},{24,8},{28,12},{32,16},... | collective-permute-start | bytes 393224 | tf_op jit(solution)/shard_map/ppermute | solution.py:241
  15.4 14.4 %collective-permute-start = (f32[32,1024]{1,0:T(8,128)S(1)}, f32[32,1024]{1,0:T(8,128)S(1)}, u32[]{:S(2)}, u32[]{:S(2)}) collective-permute-start(f32[32,1024]{1,0:T(8,128)S(1)} %pad.8), channel_id=1, source_target_pairs={{0,16},{4,20},{8,24},{12,28},{16,32},{20,36},{24,40},{28,44},{32,4... | collective-permute-start | bytes 393224 | tf_op jit(solution)/shard_map/ppermute | solution.py:241
  17.3 1.5 copy-start.5
  22.1 1.3 copy-start.1
  23.4 48.0 %all-to-all-start = ((f32[8,128,512]{2,1,0:T(8,128)}), f32[8,128,512]{2,1,0:T(8,128)S(1)}, u32[]{:S(2)}, u32[]{:S(2)}) async-start(f32[8,128,512]{2,1,0:T(8,128)} %copy-done.1), calls=%async_computation | async-start | bytes 4194304 | tf_op jit(solution)/shard_map/all_to_all | solution.py:304
  28.3 37.4 %copy-start.2 = (f32[2,512,512]{2,1,0:T(8,128)S(1)}, f32[2,512,512]{2,1,0:T(8,128)}, u32[]{:S(2)}) copy-start(f32[2,512,512]{2,1,0:T(8,128)} %refs_6_.1) | copy-start | bytes 6291460
  29.8 14.1 %collective-permute-start.3 = (f32[96,1024]{1,0:T(8,128)S(1)}, f32[96,1024]{1,0:T(8,128)S(1)}, u32[]{:S(2)}, u32[]{:S(2)}) collective-permute-start(f32[96,1024]{1,0:T(8,128)S(1)} %pad_maximum_fusion.2.refs_0_), channel_id=1, source_target_pairs={{0,60},{4,0},{8,4},{12,8},{16,12},{20,16},{24,20},{28,24},{32,28},... | collective-permute-start | bytes 1179656 | tf_op jit(solution)/shard_map/ppermute | solution.py:241
  35.0 15.1 %collective-permute-start.2 = (f32[96,1024]{1,0:T(8,128)S(1)}, f32[96,1024]{1,0:T(8,128)S(1)}, u32[]{:S(2)}, u32[]{:S(2)}) collective-permute-start(f32[96,1024]{1,0:T(8,128)S(1)} %pad_maximum_fusion.2.refs_0_), channel_id=1, source_target_pairs={{0,4},{4,8},{8,12},{12,16},{16,20},{20,24},{24,28},{28,32},{32,36}... | collective-permute-start | bytes 1179656 | tf_op jit(solution)/shard_map/ppermute | solution.py:241
  36.9 13.2 %collective-permute-start.4 = (f32[32,1024]{1,0:T(8,128)S(1)}, f32[32,1024]{1,0:T(8,128)S(1)}, u32[]{:S(2)}, u32[]{:S(2)}) collective-permute-start(f32[32,1024]{1,0:T(8,128)S(1)} %collective-permute-done), channel_id=1, source_target_pairs={{0,16},{4,20},{8,24},{12,28},{16,32},{20,36},{24,40},{28,44},{32,4... | collective-permute-start | bytes 393224 | tf_op jit(solution)/shard_map/ppermute | solution.py:241
  50.2 15.5 %collective-permute-start.5 = (f32[96,1024]{1,0:T(8,128)S(1)}, f32[96,1024]{1,0:T(8,128)S(1)}, u32[]{:S(2)}, u32[]{:S(2)}) collective-permute-start(f32[96,1024]{1,0:T(8,128)S(1)} %get-tuple-element.43), channel_id=1, source_target_pairs={{0,4},{4,8},{8,12},{12,16},{16,20},{20,24},{24,28},{28,32},{32,36}... | collective-permute-start | bytes 1179656 | tf_op jit(solution)/shard_map/ppermute | solution.py:241
  53.0 12.8 %collective-permute-start.6 = (f32[96,1024]{1,0:T(8,128)S(1)}, f32[96,1024]{1,0:T(8,128)S(1)}, u32[]{:S(2)}, u32[]{:S(2)}) collective-permute-start(f32[96,1024]{1,0:T(8,128)S(1)} %get-tuple-element.42), channel_id=1, source_target_pairs={{0,60},{4,0},{8,4},{12,8},{16,12},{20,16},{24,20},{28,24},{32,28},... | collective-permute-start | bytes 1179656 | tf_op jit(solution)/shard_map/ppermute | solution.py:241
  68.4 1.4 copy-start.3
  69.7 0.8 copy-start.6
  70.5 0.8 copy-start.7
  71.4 10.6 %collective-permute-start.7 = (f32[512,1024]{1,0:T(8,128)}, f32[512,1024]{1,0:T(8,128)S(1)}, u32[]{:S(2)}, u32[]{:S(2)}) collective-permute-start(f32[512,1024]{1,0:T(8,128)} %copy-done.3), channel_id=1, source_target_pairs={{0,64},{64,0},{1,65},{65,1},{2,66},{66,2},{3,67},{67,3},{4,68},{68... | collective-permute-start | bytes 6291464 | tf_op jit(solution)/shard_map/ppermute | solution.py:245
  74.3 15.4 %collective-permute-start.8 = (f32[256,512]{1,0:T(8,128)}, f32[256,512]{1,0:T(8,128)S(1)}, u32[]{:S(2)}, u32[]{:S(2)}) collective-permute-start(f32[256,512]{1,0:T(8,128)} %copy-done.7), channel_id=1, source_target_pairs={{0,256},{1,257},{2,258},{3,259},{4,260},{5,261},{6,262},{7,263},{7... | collective-permute-start | bytes 1572872 | tf_op jit(solution)/shard_map/ppermute | solution.py:268
  79.3 12.6 %collective-permute-start.9 = (f32[256,512]{1,0:T(8,128)}, f32[256,512]{1,0:T(8,128)S(1)}, u32[]{:S(2)}, u32[]{:S(2)}) collective-permute-start(f32[256,512]{1,0:T(8,128)} %copy-done.6), channel_id=1, source_target_pairs={{0,128},{1,129},{2,130},{3,131},{4,132},{5,133},{6,134},{7,135},{7... | collective-permute-start | bytes 1572872 | tf_op jit(solution)/shard_map/ppermute | solution.py:268
  80.6 11.3 %collective-permute-start.10 = (f32[256,512]{1,0:T(8,128)S(1)}, f32[256,512]{1,0:T(8,128)S(1)}, u32[]{:S(2)}, u32[]{:S(2)}) collective-permute-start(f32[256,512]{1,0:T(8,128)S(1)} %get-tuple-element.22), channel_id=1, source_target_pairs={{0,384},{1,385},{2,386},{3,387},{4,388},{5,389},{6,390},{7,391},{7... | collective-permute-start | bytes 1572872 | tf_op jit(solution)/shard_map/ppermute | solution.py:268
  82.0 1.6 copy-start.4
  88.4 1.4 copy-start
  89.8 2.1 %copy-start.8 = (f32[256,512]{1,0:T(8,128)}, f32[256,512]{1,0:T(8,128)S(1)}, u32[]{:S(2)}) copy-start(f32[256,512]{1,0:T(8,128)S(1)} %collective-permute-done.8) | copy-start | bytes 1572868
  91.9 0.8 copy-start.10
  92.7 0.8 copy-start.11
  93.5 8.1 %copy-start.13 = (f32[2,512]{1,0:T(2,128)S(1)}, f32[2,512]{1,0:T(2,128)}, u32[]{:S(2)}) copy-start(f32[2,512]{1,0:T(2,128)} %param.12) | copy-start | bytes 12292
  93.5 8.7 %copy-start.12 = (f32[2,512]{1,0:T(2,128)S(1)}, f32[2,512]{1,0:T(2,128)}, u32[]{:S(2)}) copy-start(f32[2,512]{1,0:T(2,128)} %param.11) | copy-start | bytes 12292
  93.5 9.3 %copy-start.14 = (s32[2,512]{1,0:T(2,128)S(1)}, s32[2,512]{1,0:T(2,128)}, u32[]{:S(2)}) copy-start(s32[2,512]{1,0:T(2,128)} %param.10) | copy-start | bytes 12292
  93.5 11.0 %copy-start.9 = (f32[256,512]{1,0:T(8,128)S(1)}, f32[256,512]{1,0:T(8,128)}, u32[]{:S(2)}) copy-start(f32[256,512]{1,0:T(8,128)} %copy-done.8) | copy-start | bytes 1572868
  93.5 33.7 %all-to-all-start.1 = ((f32[32,128,128]{2,1,0:T(8,128)}), f32[32,128,128]{2,1,0:T(8,128)S(1)}, u32[]{:S(2)}, u32[]{:S(2)}) async-start(f32[32,128,128]{2,1,0:T(8,128)} %bitcast.31), calls=%async_computation.1 | async-start | bytes 4194304 | tf_op jit(solution)/shard_map/all_to_all | solution.py:304
  105.9 7.0 %collective-permute-start.11 = (f32[256,512]{1,0:T(8,128)S(1)}, f32[256,512]{1,0:T(8,128)S(1)}, u32[]{:S(2)}, u32[]{:S(2)}) collective-permute-start(f32[256,512]{1,0:T(8,128)S(1)} %add_select_fusion), channel_id=1, source_target_pairs={{0,64},{1,65},{2,66},{3,67},{4,68},{5,69},{6,70},{7,71},{72,8},{73... | collective-permute-start | bytes 1572872 | tf_op jit(solution)/shard_map/ppermute | solution.py:259
  128.4 14.1 %all-to-all-start.2 = ((f32[16,32,128]{2,1,0:T(8,128)}), f32[16,32,128]{2,1,0:T(8,128)S(1)}, u32[]{:S(2)}, u32[]{:S(2)}) async-start(f32[16,32,128]{2,1,0:T(8,128)} %bitcast.20), calls=%async_computation.2 | async-start | bytes 524288 | tf_op jit(solution)/shard_map/all_to_all | solution.py:304
  133.5 9.0 %collective-permute-start.12 = (f32[128,128]{1,0:T(8,128)S(1)}, f32[128,128]{1,0:T(8,128)S(1)}, u32[]{:S(2)}, u32[]{:S(2)}) collective-permute-start(f32[128,128]{1,0:T(8,128)S(1)} %pad_maximum_fusion.3), channel_id=1, source_target_pairs={{0,2},{1,3},{2,0},{3,1},{4,6},{5,7},{6,4},{7,5},{8,10},{9,11},{10,... | collective-permute-start | bytes 196616 | tf_op jit(solution)/shard_map/ppermute | solution.py:276
  162.3 14.7 %all-to-all-start.4 = ((f32[16,32,128]{2,1,0:T(8,128)}), f32[16,32,128]{2,1,0:T(8,128)S(1)}, u32[]{:S(2)}, u32[]{:S(2)}) async-start(f32[16,32,128]{2,1,0:T(8,128)} %tile.5), calls=%async_computation.4 | async-start | bytes 524288 | tf_op jit(solution)/shard_map/all_to_all | solution.py:304
  168.4 6.3 %collective-permute-start.13 = (f32[128,128]{1,0:T(8,128)S(1)}, f32[128,128]{1,0:T(8,128)S(1)}, u32[]{:S(2)}, u32[]{:S(2)}) collective-permute-start(f32[128,128]{1,0:T(8,128)S(1)} %pad_maximum_fusion.4), channel_id=1, source_target_pairs={{0,1},{1,0},{2,3},{3,2},{4,5},{5,4},{6,7},{7,6},{8,9},{9,8},{10,11... | collective-permute-start | bytes 196616 | tf_op jit(solution)/shard_map/ppermute | solution.py:276

commit v5 on v4

--- a/solution.py
+++ b/solution.py
@@ -105,7 +105,7 @@
 N_PIECES = len(PIECES)
 
 
-STEPS = (0, 2, 1, 3)
+STEPS = (2, 1, 3)
 
 
 def panel_kernel(where_ref, *refs):
@@ -132,9 +132,9 @@
     own = jax.ShapeDtypeStruct((PAD, C), f32)
     return pl.pallas_call(
         panel_kernel,
-        out_shape=(jax.ShapeDtypeStruct((DEPTH, WIDE), f32),) + (own,) * 4,
+        out_shape=(jax.ShapeDtypeStruct((DEPTH, WIDE), f32),) + (own,) * 3,
         in_specs=[pl.BlockSpec(memory_space=pltpu.SMEM)] + [vmem] * (N_PIECES + 1),
-        out_specs=(vmem,) * 5,
+        out_specs=(vmem,) * 4,
         scratch_shapes=[pltpu.VMEM((DEPTH, WIDE), f32)],
         compiler_params=pltpu.CompilerParams(vmem_limit_bytes=14 << 20),
         cost_estimate=pl.CostEstimate(
@@ -350,13 +350,14 @@
 
     x = lax.axis_index("x")
     where = jnp.stack([z, core, x]).astype(jnp.int32)
-    y_all, kept, *leaving = panel_rows(where, pieces, panel_inverse)
+    y_all, *leaving = panel_rows(where, pieces, panel_inverse)
     y_all, s_parts = lax.optimization_barrier((y_all, s_parts))
 
-    parts = [from_root(a, step) for a, step in zip(leaving, STEPS[1:])]
+    parts = [from_root(a, step) for a, step in zip(leaving, STEPS)]
     image = chip_image(where, y_all, swap_core(y_all), s_parts)
     image, *parts = lax.optimization_barrier((image, *parts))
     got = exchange(image.reshape(32 * HALF, OWN), PLANE)
+    kept = jnp.where(x % 2 == 0, leaving[1], leaving[2])
     mine = jnp.where(x == z // 4, kept, parts[0] + parts[1] + parts[2])
     y_rows = jnp.where(core == z // 2 % 2, mine, to_other_core(mine))
 

time: 179 us -> 178 us (level)
    unnamed x33 -> x29, local copies, waits for them, and re-layouts: 11.1 us -> 10.3 us
where the time goes in v5:
time: 178 us; the launch traced here: 177 us
  starting transfers between devices  75 us (42%)
  waiting for transfers between devices  45.2 us (25%)
  blocking collectives  19 us (11%)
  local copies, waits for them, and re-layouts  15.1 us (8%)
  Pallas kernels  12.5 us (7%)
  other arithmetic  6.53 us (4%)
  matrix products  2.27 us (1%)
    ppermute x7, starting transfers between devices, shift_z(): return lax.ppermute(a, ('c',) + Z, pairs)  33.4 us
    all_to_all x4, starting transfers between devices, exchange(): return lax.all_to_all(a, axes, 0, 0, tiled=True)  23 us
    all_to_all x4, waiting for transfers between devices, exchange(): return lax.all_to_all(a, axes, 0, 0, tiled=True)  20.4 us
    all_to_all x1, blocking collectives, exchange(): return lax.all_to_all(a, axes, 0, 0, tiled=True)  19 us
    ppermute x7, waiting for transfers between devices, shift_z(): return lax.ppermute(a, ('c',) + Z, pairs)  18.4 us
    unnamed x29, local copies, waits for them, and re-layouts  10.3 us
    ppermute x3, starting transfers between devices, from_root(): return lax.ppermute(a, AXES, pairs)  7.6 us
    ppermute x2, starting transfers between devices, swap_y(): return lax.ppermute(a, 'y', [(i, i ^ bit) for i in range(NY)])  6 us
  transfers between devices with their start and end apart: 18, of which 9 were waited for; matrix products, arithmetic and copies ran while one was open for 6% of the time, Pallas kernels for 6%

profile of v5, /device:TPU:8, one launch (start us, length us, event | category | flops | bytes accessed | tf_op | source)
XLA Modules:
  0.0 176.8 jit_solution(10578112315871582305)
XLA Ops:
  0.7 0.8 fusion.18
  1.7 0.9 mul.127
  2.7 12.7 %collective-permute-start.1 = (f32[32,1024]{1,0:T(8,128)S(1)}, f32[32,1024]{1,0:T(8,128)S(1)}, u32[]{:S(2)}, u32[]{:S(2)}) collective-permute-start(f32[32,1024]{1,0:T(8,128)S(1)} %pad.8), channel_id=1, source_target_pairs={{0,48},{4,52},{8,56},{12,60},{16,0},{20,4},{24,8},{28,12},{32,16},... | collective-permute-start | bytes 393224 | tf_op jit(solution)/shard_map/ppermute | solution.py:241
  15.4 1.9 %collective-permute-start = (f32[32,1024]{1,0:T(8,128)S(1)}, f32[32,1024]{1,0:T(8,128)S(1)}, u32[]{:S(2)}, u32[]{:S(2)}) collective-permute-start(f32[32,1024]{1,0:T(8,128)S(1)} %pad.8), channel_id=1, source_target_pairs={{0,16},{4,20},{8,24},{12,28},{16,32},{20,36},{24,40},{28,44},{32,4... | collective-permute-start | bytes 393224 | tf_op jit(solution)/shard_map/ppermute | solution.py:241
  17.3 1.5 copy-done.5
  18.8 3.2 %shard_map.87 = f32[8,128,512]{2,1,0:T(8,128)S(1)} custom-call(f32[240,1920]{1,0:T(8,128)S(1)} %copy-done.5), custom_call_target="tpu_custom_call" | custom-call | flops 1258291200 | bytes 3932160 | tf_op jit(solution)/shard_map/pallas_call | solution.py:86
  22.1 1.3 copy-done.1
  23.4 4.9 %all-to-all-start = ((f32[8,128,512]{2,1,0:T(8,128)}), f32[8,128,512]{2,1,0:T(8,128)S(1)}, u32[]{:S(2)}, u32[]{:S(2)}) async-start(f32[8,128,512]{2,1,0:T(8,128)} %copy-done.1), calls=%async_computation | async-start | bytes 4194304 | tf_op jit(solution)/shard_map/all_to_all | solution.py:304
  28.3 1.5 collective-permute-done
  29.8 5.2 %collective-permute-start.3 = (f32[96,1024]{1,0:T(8,128)S(1)}, f32[96,1024]{1,0:T(8,128)S(1)}, u32[]{:S(2)}, u32[]{:S(2)}) collective-permute-start(f32[96,1024]{1,0:T(8,128)S(1)} %pad_maximum_fusion.2.refs_0_), channel_id=1, source_target_pairs={{0,60},{4,0},{8,4},{12,8},{16,12},{20,16},{24,20},{28,24},{32,28},... | collective-permute-start | bytes 1179656 | tf_op jit(solution)/shard_map/ppermute | solution.py:241
  35.0 1.9 %collective-permute-start.2 = (f32[96,1024]{1,0:T(8,128)S(1)}, f32[96,1024]{1,0:T(8,128)S(1)}, u32[]{:S(2)}, u32[]{:S(2)}) collective-permute-start(f32[96,1024]{1,0:T(8,128)S(1)} %pad_maximum_fusion.2.refs_0_), channel_id=1, source_target_pairs={{0,4},{4,8},{8,12},{12,16},{16,20},{20,24},{24,28},{28,32},{32,36}... | collective-permute-start | bytes 1179656 | tf_op jit(solution)/shard_map/ppermute | solution.py:241
  36.9 2.9 %collective-permute-start.4 = (f32[32,1024]{1,0:T(8,128)S(1)}, f32[32,1024]{1,0:T(8,128)S(1)}, u32[]{:S(2)}, u32[]{:S(2)}) collective-permute-start(f32[32,1024]{1,0:T(8,128)S(1)} %collective-permute-done), channel_id=1, source_target_pairs={{0,16},{4,20},{8,24},{12,28},{16,32},{20,36},{24,40},{28,44},{32,4... | collective-permute-start | bytes 393224 | tf_op jit(solution)/shard_map/ppermute | solution.py:241
  39.8 4.1 %collective-permute-done.3.refs_2_ = f32[96,1024]{1,0:T(8,128)S(1)} collective-permute-done((f32[96,1024]{1,0:T(8,128)S(1)}, f32[96,1024]{1,0:T(8,128)S(1)}, u32[]{:S(2)}, u32[]{:S(2)}) %collective-permute-start.3) | collective-permute-done | bytes 393248 | tf_op jit(solution)/shard_map/ppermute | solution.py:241
  43.9 6.2 %collective-permute-done.2.refs_1_ = f32[96,1024]{1,0:T(8,128)S(1)} collective-permute-done((f32[96,1024]{1,0:T(8,128)S(1)}, f32[96,1024]{1,0:T(8,128)S(1)}, u32[]{:S(2)}, u32[]{:S(2)}) %collective-permute-start.2) | collective-permute-done | bytes 393248 | tf_op jit(solution)/shard_map/ppermute | solution.py:241
  50.2 2.8 %collective-permute-start.5 = (f32[96,1024]{1,0:T(8,128)S(1)}, f32[96,1024]{1,0:T(8,128)S(1)}, u32[]{:S(2)}, u32[]{:S(2)}) collective-permute-start(f32[96,1024]{1,0:T(8,128)S(1)} %get-tuple-element.41), channel_id=1, source_target_pairs={{0,4},{4,8},{8,12},{12,16},{16,20},{20,24},{24,28},{28,32},{32,36}... | collective-permute-start | bytes 1179656 | tf_op jit(solution)/shard_map/ppermute | solution.py:241
  53.0 6.0 %collective-permute-start.6 = (f32[96,1024]{1,0:T(8,128)S(1)}, f32[96,1024]{1,0:T(8,128)S(1)}, u32[]{:S(2)}, u32[]{:S(2)}) collective-permute-start(f32[96,1024]{1,0:T(8,128)S(1)} %get-tuple-element.40), channel_id=1, source_target_pairs={{0,60},{4,0},{8,4},{12,8},{16,12},{20,16},{24,20},{28,24},{32,28},... | collective-permute-start | bytes 1179656 | tf_op jit(solution)/shard_map/ppermute | solution.py:241
  59.1 6.7 %collective-permute-done.5.refs_4_ = f32[96,1024]{1,0:T(8,128)S(1)} collective-permute-done((f32[96,1024]{1,0:T(8,128)S(1)}, f32[96,1024]{1,0:T(8,128)S(1)}, u32[]{:S(2)}, u32[]{:S(2)}) %collective-permute-start.5) | collective-permute-done | bytes 393248 | tf_op jit(solution)/shard_map/ppermute | solution.py:241
  65.8 2.6 %shard_map.86 = (f32[512,1024]{1,0:T(8,128)S(1)}, f32[256,512]{1,0:T(8,128)S(1)}, f32[256,512]{1,0:T(8,128)S(1)}, f32[256,512]{1,0:T(8,128)S(1)}) custom-call(s32[3]{0:T(128)S(1)} %pad_add_fusion.where_ref, f32[96,1024]{1,0:T(8,128)S(1)} %pad_maximum_fusion.2.refs_0_, f32[96,1024]{1,0:T(8,128)S(1)} %collective-permute-done.2.refs_1_, ...), custom_call_target="tpu_custom_call" | custom-call | flops 8053063680 | bytes 9437184 | tf_op jit(solution)/shard_map/pallas_call | solution.py:133
  68.4 1.3 copy-done.3
  69.7 0.8 copy-done.6
  70.5 3.0 %collective-permute-start.7 = (f32[512,1024]{1,0:T(8,128)}, f32[512,1024]{1,0:T(8,128)S(1)}, u32[]{:S(2)}, u32[]{:S(2)}) collective-permute-start(f32[512,1024]{1,0:T(8,128)} %copy-done.3), channel_id=1, source_target_pairs={{0,64},{64,0},{1,65},{65,1},{2,66},{66,2},{3,67},{67,3},{4,68},{68... | collective-permute-start | bytes 6291464 | tf_op jit(solution)/shard_map/ppermute | solution.py:245
  73.5 5.0 %collective-permute-start.8 = (f32[256,512]{1,0:T(8,128)}, f32[256,512]{1,0:T(8,128)S(1)}, u32[]{:S(2)}, u32[]{:S(2)}) collective-permute-start(f32[256,512]{1,0:T(8,128)} %copy-done.6), channel_id=1, source_target_pairs={{0,256},{1,257},{2,258},{3,259},{4,260},{5,261},{6,262},{7,263},{7... | collective-permute-start | bytes 1572872 | tf_op jit(solution)/shard_map/ppermute | solution.py:268
  78.4 1.3 collective-permute-start.9
  79.8 1.3 collective-permute-start.10
  81.1 1.6 copy-done.4
  82.7 4.8 %shard_map.88 = f32[8,4,128,128]{3,2,1,0:T(8,128)S(1)} custom-call(s32[3]{0:T(128)S(1)} %pad_add_fusion.where_ref, f32[512,1024]{1,0:T(8,128)S(1)} %copy-done.4, f32[512,1024]{1,0:T(8,128)S(1)} %collective-permute-done.7.other_ref, f32[8,128,512]{2,1,0:T(8,128)S(1)} %all-to-all-done.s_ref), custom_call_target="tpu_custom_call" | custom-call | flops 3221225472 | bytes 8388608 | tf_op jit(solution)/shard_map/pallas_call | solution.py:170
  87.5 1.3 copy-done
  88.9 2.0 %collective-permute-done.9 = f32[256,512]{1,0:T(8,128)S(1)} collective-permute-done((f32[256,512]{1,0:T(8,128)S(1)}, f32[256,512]{1,0:T(8,128)S(1)}, u32[]{:S(2)}, u32[]{:S(2)}) %collective-permute-start.9) | collective-permute-done | bytes 524320 | tf_op jit(solution)/shard_map/ppermute | solution.py:268
  90.9 0.8 copy-done.8
  91.7 0.8 copy-done.9
  92.5 7.0 %all-to-all-start.1 = ((f32[32,128,128]{2,1,0:T(8,128)}), f32[32,128,128]{2,1,0:T(8,128)S(1)}, u32[]{:S(2)}, u32[]{:S(2)}) async-start(f32[32,128,128]{2,1,0:T(8,128)} %bitcast.31), calls=%async_computation.1 | async-start | bytes 4194304 | tf_op jit(solution)/shard_map/all_to_all | solution.py:304
  99.7 0.8 convert_reduce_fusion
  102.2 1.5 constant_dynamic-slice_fusion.1
  103.7 1.6 add_select_fusion
  105.3 2.0 %collective-permute-start.11 = (f32[256,512]{1,0:T(8,128)S(1)}, f32[256,512]{1,0:T(8,128)S(1)}, u32[]{:S(2)}, u32[]{:S(2)}) collective-permute-start(f32[256,512]{1,0:T(8,128)S(1)} %add_select_fusion), channel_id=1, source_target_pairs={{0,64},{1,65},{2,66},{3,67},{4,68},{5,69},{6,70},{7,71},{72,8},{73... | collective-permute-start | bytes 1572872 | tf_op jit(solution)/shard_map/ppermute | solution.py:259
  107.3 0.8 fusion.22
  108.1 2.1 %divide_select_fusion = (f32[512]{0:T(512)S(1)}, f32[512]{0:T(512)S(1)}, f32[512]{0:T(512)S(1)}) fusion(pred[512]{0:T(512)(128)(4,1)S(1)} %get-tuple-element.30, f32[512]{0:T(512)S(1)} %bitcast.41, pred[512]{0:T(512)(128)(4,1)S(1)} %get-tuple-element.31, f32[512]{0:T(512)S(1)} %bitcast.39, f32[511]{0:T(512)S(1)} %bitcast.36, f32[1]{0:T(128)} %bitcast.16, ...), kind=kLoop, calls=%fused_computation.42 | loop fusion | flops 9216 | bytes 19968 | tf_op jit(solution)/shard_map/jit(_where)/select_n | solution.py:223
  110.2 2.3 %convolution_select_fusion.pivot_ref = f32[32,128]{1,0:T(8,128)S(1)} fusion(f32[1,1,128]{2,1,0:T(1,128)S(1)} %get-tuple-element.34, f32[1,511,128]{2,1,0:T(8,128)S(1)} %get-tuple-element.36, f32[1,511,128]{2,1,0:T(8,128)S(1)} %get-tuple-element.35, f32[1,1,128]{2,1,0:T(1,128)S(1)} %get-tuple-element.33, f32[2,512,512]{2,1,0:T(8,128)} %refs_6_.1, ...), kind=kOutput, calls=%fused_computation | convolution fusion | flops 25628672 | bytes 1073664 | tf_op jit(solution)/shard_map/dot_general | solution.py:339
  112.6 13.8 %all-to-all-done.1 = f32[32,128,128]{2,1,0:T(8,128)S(1)} async-done(((f32[32,128,128]{2,1,0:T(8,128)}), f32[32,128,128]{2,1,0:T(8,128)S(1)}, u32[]{:S(2)}, u32[]{:S(2)}) %all-to-all-start.1) | async-done | bytes 2097184 | tf_op jit(solution)/shard_map/all_to_all | solution.py:304
  126.4 1.2 shard_map.89
  127.6 5.1 %all-to-all-start.2 = ((f32[16,32,128]{2,1,0:T(8,128)}), f32[16,32,128]{2,1,0:T(8,128)S(1)}, u32[]{:S(2)}, u32[]{:S(2)}) async-start(f32[16,32,128]{2,1,0:T(8,128)} %bitcast.20), calls=%async_computation.2 | async-start | bytes 524288 | tf_op jit(solution)/shard_map/all_to_all | solution.py:304
  132.7 4.0 %collective-permute-start.12 = (f32[128,128]{1,0:T(8,128)S(1)}, f32[128,128]{1,0:T(8,128)S(1)}, u32[]{:S(2)}, u32[]{:S(2)}) collective-permute-start(f32[128,128]{1,0:T(8,128)S(1)} %pad_maximum_fusion.3), channel_id=1, source_target_pairs={{0,2},{1,3},{2,0},{3,1},{4,6},{5,7},{6,4},{7,5},{8,10},{9,11},{10,... | collective-permute-start | bytes 196616 | tf_op jit(solution)/shard_map/ppermute | solution.py:276
  136.7 5.0 %all-to-all-done.2 = f32[16,32,128]{2,1,0:T(8,128)S(1)} async-done(((f32[16,32,128]{2,1,0:T(8,128)}), f32[16,32,128]{2,1,0:T(8,128)S(1)}, u32[]{:S(2)}, u32[]{:S(2)}) %all-to-all-start.2) | async-done | bytes 262176 | tf_op jit(solution)/shard_map/all_to_all | solution.py:304
  141.7 19.0 %all_to_all.38 = f32[4,32,128]{2,1,0:T(8,128)S(1)} all-to-all(f32[4,32,128]{2,1,0:T(8,128)S(1)} %tile.4), channel_id=1, replica_groups=mesh['x'=4,'c'=2,'h'=4,'l'=4,'y'=4] {'h'}, dimensions={0} | all-to-all | bytes 131072 | tf_op jit(solution)/shard_map/all_to_all | solution.py:304
  161.4 6.0 %all-to-all-start.4 = ((f32[16,32,128]{2,1,0:T(8,128)}), f32[16,32,128]{2,1,0:T(8,128)S(1)}, u32[]{:S(2)}, u32[]{:S(2)}) async-start(f32[16,32,128]{2,1,0:T(8,128)} %tile.5), calls=%async_computation.4 | async-start | bytes 524288 | tf_op jit(solution)/shard_map/all_to_all | solution.py:304
  167.5 2.0 %collective-permute-start.13 = (f32[128,128]{1,0:T(8,128)S(1)}, f32[128,128]{1,0:T(8,128)S(1)}, u32[]{:S(2)}, u32[]{:S(2)}) collective-permute-start(f32[128,128]{1,0:T(8,128)S(1)} %pad_maximum_fusion.4), channel_id=1, source_target_pairs={{0,1},{1,0},{2,3},{3,2},{4,5},{5,4},{6,7},{7,6},{8,9},{9,8},{10,11... | collective-permute-start | bytes 196616 | tf_op jit(solution)/shard_map/ppermute | solution.py:276
  169.5 4.3 %collective-permute-done.13.second_ref = f32[128,128]{1,0:T(8,128)S(1)} collective-permute-done((f32[128,128]{1,0:T(8,128)S(1)}, f32[128,128]{1,0:T(8,128)S(1)}, u32[]{:S(2)}, u32[]{:S(2)}) %collective-permute-start.13) | collective-permute-done | bytes 65568 | tf_op jit(solution)/shard_map/ppermute | solution.py:276
  174.5 1.6 all-to-all-done.4
  (58 shorter events, 4.4 us)
Async XLA Ops:
  2.7 25.7 %collective-permute-start.1 = (f32[32,1024]{1,0:T(8,128)S(1)}, f32[32,1024]{1,0:T(8,128)S(1)}, u32[]{:S(2)}, u32[]{:S(2)}) collective-permute-start(f32[32,1024]{1,0:T(8,128)S(1)} %pad.8), channel_id=1, source_target_pairs={{0,48},{4,52},{8,56},{12,60},{16,0},{20,4},{24,8},{28,12},{32,16},... | collective-permute-start | bytes 393224 | tf_op jit(solution)/shard_map/ppermute | solution.py:241
  15.4 14.4 %collective-permute-start = (f32[32,1024]{1,0:T(8,128)S(1)}, f32[32,1024]{1,0:T(8,128)S(1)}, u32[]{:S(2)}, u32[]{:S(2)}) collective-permute-start(f32[32,1024]{1,0:T(8,128)S(1)} %pad.8), channel_id=1, source_target_pairs={{0,16},{4,20},{8,24},{12,28},{16,32},{20,36},{24,40},{28,44},{32,4... | collective-permute-start | bytes 393224 | tf_op jit(solution)/shard_map/ppermute | solution.py:241
  17.3 1.5 copy-start.5
  22.1 1.3 copy-start.1
  23.4 47.1 %all-to-all-start = ((f32[8,128,512]{2,1,0:T(8,128)}), f32[8,128,512]{2,1,0:T(8,128)S(1)}, u32[]{:S(2)}, u32[]{:S(2)}) async-start(f32[8,128,512]{2,1,0:T(8,128)} %copy-done.1), calls=%async_computation | async-start | bytes 4194304 | tf_op jit(solution)/shard_map/all_to_all | solution.py:304
  28.3 37.4 %copy-start.2 = (f32[2,512,512]{2,1,0:T(8,128)S(1)}, f32[2,512,512]{2,1,0:T(8,128)}, u32[]{:S(2)}) copy-start(f32[2,512,512]{2,1,0:T(8,128)} %refs_6_.1) | copy-start | bytes 6291460
  29.8 14.0 %collective-permute-start.3 = (f32[96,1024]{1,0:T(8,128)S(1)}, f32[96,1024]{1,0:T(8,128)S(1)}, u32[]{:S(2)}, u32[]{:S(2)}) collective-permute-start(f32[96,1024]{1,0:T(8,128)S(1)} %pad_maximum_fusion.2.refs_0_), channel_id=1, source_target_pairs={{0,60},{4,0},{8,4},{12,8},{16,12},{20,16},{24,20},{28,24},{32,28},... | collective-permute-start | bytes 1179656 | tf_op jit(solution)/shard_map/ppermute | solution.py:241
  35.0 15.1 %collective-permute-start.2 = (f32[96,1024]{1,0:T(8,128)S(1)}, f32[96,1024]{1,0:T(8,128)S(1)}, u32[]{:S(2)}, u32[]{:S(2)}) collective-permute-start(f32[96,1024]{1,0:T(8,128)S(1)} %pad_maximum_fusion.2.refs_0_), channel_id=1, source_target_pairs={{0,4},{4,8},{8,12},{12,16},{16,20},{20,24},{24,28},{28,32},{32,36}... | collective-permute-start | bytes 1179656 | tf_op jit(solution)/shard_map/ppermute | solution.py:241
  36.9 13.2 %collective-permute-start.4 = (f32[32,1024]{1,0:T(8,128)S(1)}, f32[32,1024]{1,0:T(8,128)S(1)}, u32[]{:S(2)}, u32[]{:S(2)}) collective-permute-start(f32[32,1024]{1,0:T(8,128)S(1)} %collective-permute-done), channel_id=1, source_target_pairs={{0,16},{4,20},{8,24},{12,28},{16,32},{20,36},{24,40},{28,44},{32,4... | collective-permute-start | bytes 393224 | tf_op jit(solution)/shard_map/ppermute | solution.py:241
  50.2 15.5 %collective-permute-start.5 = (f32[96,1024]{1,0:T(8,128)S(1)}, f32[96,1024]{1,0:T(8,128)S(1)}, u32[]{:S(2)}, u32[]{:S(2)}) collective-permute-start(f32[96,1024]{1,0:T(8,128)S(1)} %get-tuple-element.41), channel_id=1, source_target_pairs={{0,4},{4,8},{8,12},{12,16},{16,20},{20,24},{24,28},{28,32},{32,36}... | collective-permute-start | bytes 1179656 | tf_op jit(solution)/shard_map/ppermute | solution.py:241
  53.0 12.8 %collective-permute-start.6 = (f32[96,1024]{1,0:T(8,128)S(1)}, f32[96,1024]{1,0:T(8,128)S(1)}, u32[]{:S(2)}, u32[]{:S(2)}) collective-permute-start(f32[96,1024]{1,0:T(8,128)S(1)} %get-tuple-element.40), channel_id=1, source_target_pairs={{0,60},{4,0},{8,4},{12,8},{16,12},{20,16},{24,20},{28,24},{32,28},... | collective-permute-start | bytes 1179656 | tf_op jit(solution)/shard_map/ppermute | solution.py:241
  68.3 1.3 copy-start.3
  69.7 0.8 copy-start.6
  70.5 10.6 %collective-permute-start.7 = (f32[512,1024]{1,0:T(8,128)}, f32[512,1024]{1,0:T(8,128)S(1)}, u32[]{:S(2)}, u32[]{:S(2)}) collective-permute-start(f32[512,1024]{1,0:T(8,128)} %copy-done.3), channel_id=1, source_target_pairs={{0,64},{64,0},{1,65},{65,1},{2,66},{66,2},{3,67},{67,3},{4,68},{68... | collective-permute-start | bytes 6291464 | tf_op jit(solution)/shard_map/ppermute | solution.py:245
  73.5 15.4 %collective-permute-start.8 = (f32[256,512]{1,0:T(8,128)}, f32[256,512]{1,0:T(8,128)S(1)}, u32[]{:S(2)}, u32[]{:S(2)}) collective-permute-start(f32[256,512]{1,0:T(8,128)} %copy-done.6), channel_id=1, source_target_pairs={{0,256},{1,257},{2,258},{3,259},{4,260},{5,261},{6,262},{7,263},{7... | collective-permute-start | bytes 1572872 | tf_op jit(solution)/shard_map/ppermute | solution.py:268
  78.4 12.5 %collective-permute-start.9 = (f32[256,512]{1,0:T(8,128)S(1)}, f32[256,512]{1,0:T(8,128)S(1)}, u32[]{:S(2)}, u32[]{:S(2)}) collective-permute-start(f32[256,512]{1,0:T(8,128)S(1)} %get-tuple-element.20), channel_id=1, source_target_pairs={{0,128},{1,129},{2,130},{3,131},{4,132},{5,133},{6,134},{7,135},{7... | collective-permute-start | bytes 1572872 | tf_op jit(solution)/shard_map/ppermute | solution.py:268
  79.8 11.2 %collective-permute-start.10 = (f32[256,512]{1,0:T(8,128)S(1)}, f32[256,512]{1,0:T(8,128)S(1)}, u32[]{:S(2)}, u32[]{:S(2)}) collective-permute-start(f32[256,512]{1,0:T(8,128)S(1)} %get-tuple-element.21), channel_id=1, source_target_pairs={{0,384},{1,385},{2,386},{3,387},{4,388},{5,389},{6,390},{7,391},{7... | collective-permute-start | bytes 1572872 | tf_op jit(solution)/shard_map/ppermute | solution.py:268
  81.1 1.6 copy-start.4
  87.5 1.3 copy-start
  88.9 2.1 %copy-start.7 = (f32[256,512]{1,0:T(8,128)}, f32[256,512]{1,0:T(8,128)S(1)}, u32[]{:S(2)}) copy-start(f32[256,512]{1,0:T(8,128)S(1)} %collective-permute-done.8) | copy-start | bytes 1572868
  90.9 0.8 copy-start.8
  91.7 0.8 copy-start.9
  92.5 8.3 %copy-start.11 = (f32[2,512]{1,0:T(2,128)S(1)}, f32[2,512]{1,0:T(2,128)}, u32[]{:S(2)}) copy-start(f32[2,512]{1,0:T(2,128)} %param.12) | copy-start | bytes 12292
  92.5 8.9 %copy-start.10 = (f32[2,512]{1,0:T(2,128)S(1)}, f32[2,512]{1,0:T(2,128)}, u32[]{:S(2)}) copy-start(f32[2,512]{1,0:T(2,128)} %param.11) | copy-start | bytes 12292
  92.5 9.5 %copy-start.12 = (s32[2,512]{1,0:T(2,128)S(1)}, s32[2,512]{1,0:T(2,128)}, u32[]{:S(2)}) copy-start(s32[2,512]{1,0:T(2,128)} %param.10) | copy-start | bytes 12292
  92.5 33.8 %all-to-all-start.1 = ((f32[32,128,128]{2,1,0:T(8,128)}), f32[32,128,128]{2,1,0:T(8,128)S(1)}, u32[]{:S(2)}, u32[]{:S(2)}) async-start(f32[32,128,128]{2,1,0:T(8,128)} %bitcast.31), calls=%async_computation.1 | async-start | bytes 4194304 | tf_op jit(solution)/shard_map/all_to_all | solution.py:304
  105.3 7.1 %collective-permute-start.11 = (f32[256,512]{1,0:T(8,128)S(1)}, f32[256,512]{1,0:T(8,128)S(1)}, u32[]{:S(2)}, u32[]{:S(2)}) collective-permute-start(f32[256,512]{1,0:T(8,128)S(1)} %add_select_fusion), channel_id=1, source_target_pairs={{0,64},{1,65},{2,66},{3,67},{4,68},{5,69},{6,70},{7,71},{72,8},{73... | collective-permute-start | bytes 1572872 | tf_op jit(solution)/shard_map/ppermute | solution.py:259
  127.6 14.1 %all-to-all-start.2 = ((f32[16,32,128]{2,1,0:T(8,128)}), f32[16,32,128]{2,1,0:T(8,128)S(1)}, u32[]{:S(2)}, u32[]{:S(2)}) async-start(f32[16,32,128]{2,1,0:T(8,128)} %bitcast.20), calls=%async_computation.2 | async-start | bytes 524288 | tf_op jit(solution)/shard_map/all_to_all | solution.py:304
  132.7 9.0 %collective-permute-start.12 = (f32[128,128]{1,0:T(8,128)S(1)}, f32[128,128]{1,0:T(8,128)S(1)}, u32[]{:S(2)}, u32[]{:S(2)}) collective-permute-start(f32[128,128]{1,0:T(8,128)S(1)} %pad_maximum_fusion.3), channel_id=1, source_target_pairs={{0,2},{1,3},{2,0},{3,1},{4,6},{5,7},{6,4},{7,5},{8,10},{9,11},{10,... | collective-permute-start | bytes 196616 | tf_op jit(solution)/shard_map/ppermute | solution.py:276
  161.4 14.7 %all-to-all-start.4 = ((f32[16,32,128]{2,1,0:T(8,128)}), f32[16,32,128]{2,1,0:T(8,128)S(1)}, u32[]{:S(2)}, u32[]{:S(2)}) async-start(f32[16,32,128]{2,1,0:T(8,128)} %tile.5), calls=%async_computation.4 | async-start | bytes 524288 | tf_op jit(solution)/shard_map/all_to_all | solution.py:304
  167.5 6.3 %collective-permute-start.13 = (f32[128,128]{1,0:T(8,128)S(1)}, f32[128,128]{1,0:T(8,128)S(1)}, u32[]{:S(2)}, u32[]{:S(2)}) collective-permute-start(f32[128,128]{1,0:T(8,128)S(1)} %pad_maximum_fusion.4), channel_id=1, source_target_pairs={{0,1},{1,0},{2,3},{3,2},{4,5},{5,4},{6,7},{7,6},{8,9},{9,8},{10,11... | collective-permute-start | bytes 196616 | tf_op jit(solution)/shard_map/ppermute | solution.py:276
